TPU v7x, 512 devices: a whole 4x8x8 slice. The times are simulated.
512 devices in a mesh: dates: 8 (over x, core), cols: 64 (over y, z).
Axes of the slice: x: 4, y: 8, z: 8, core: 2. Of those that a mesh axis runs over, the one named last changes fastest.
Arguments:
- slc: bfloat16 [2, 32, 128, 16384], P(None, 'dates', None, 'cols')
- pairs: int32 [64, 2], replicated, may hold values from 0 to 31, as said below
- owner: int32 [64], replicated, may hold values from 0 to 7, as said below
Outputs:
- interferogram: float32 [2, 96, 32, 1024], P(None, 'dates', None, 'cols')
- coherence: float32 [96, 32, 1024], P('dates', None, 'cols')
Inputs may be any that keep to these rules, and one draw needn't show every extreme that they name: `pairs`: reference < secondary <= reference + 5 for every pair. Each owner holds at most 12 pairs, and some owner holds exactly 12.
All inputs are finite; a program needn't handle non-finite values.
Results may differ from a plain program's by a relative error of at most 0.0003.
Values may be sent and summed in bfloat16 or wider, within the bound.
A program may use at most 64 MiB of HBM per device.

v0:
```python
import math

import jax
import jax.numpy as jnp
from jax import lax
from jax.sharding import PartitionSpec as P

TAPS = [math.exp(-k * k / 8.0) for k in range(-4, 5)]
WEIGHTS = [t / sum(TAPS) for t in TAPS]


def padded_2(cells, sides, width):
    for axis, dim in sides:
        count = lax.axis_size(axis)
        ends = count - 1
        head = lax.slice_in_dim(cells, 0, width, axis=dim)
        tail = lax.slice_in_dim(cells, cells.shape[dim] - width, cells.shape[dim], axis=dim)
        cells = jnp.concatenate(
            [
                lax.ppermute(tail, axis, [(i, (i + 1) % count) for i in range(ends)]),
                cells,
                lax.ppermute(head, axis, [((i + 1) % count, i) for i in range(ends)]),
            ],
            axis=dim,
        )
    return cells


def smooth(plane):
    count = plane.shape[0]
    inner = plane.shape[1] - 8
    padded = jnp.pad(plane, ((4, 4), (0, 0)))
    along = WEIGHTS[0] * padded[0:count]
    for k in range(1, 9):
        along = along + WEIGHTS[k] * padded[k : k + count]
    result = WEIGHTS[0] * along[:, 0:inner]
    for k in range(1, 9):
        result = result + WEIGHTS[k] * along[:, k : k + inner]
    return result


def looks(plane):
    count, inner = plane.shape
    return jnp.mean(plane.reshape(count // 4, 4, inner // 16, 16), axis=(1, 3))


def one_pair(tile, first_scale, second_scale):
    values = tile.astype(jnp.float32)
    real_a = values[0, 0]
    imag_a = values[0, 1]
    real_b = values[1, 0]
    imag_b = values[1, 1]
    real_part = real_a * real_b + imag_a * imag_b
    imag_part = imag_a * real_b - real_a * imag_b
    power_first = real_a * real_a + imag_a * imag_a
    power_second = real_b * real_b + imag_b * imag_b
    smooth_real = smooth(real_part)
    smooth_imag = smooth(imag_part)
    smooth_first = smooth(power_first)
    smooth_second = smooth(power_second)
    cell_coherence = jnp.sqrt(smooth_real * smooth_real + smooth_imag * smooth_imag) / (
        jnp.sqrt(smooth_first * smooth_second) + 1e-06
    )
    inner = real_part.shape[1] - 8
    product_scale = first_scale * second_scale
    look_real = looks(real_part[:, 4 : 4 + inner]) / product_scale
    look_imag = looks(imag_part[:, 4 : 4 + inner]) / product_scale
    return jnp.stack([look_real, look_imag, looks(cell_coherence)])


def local(slc, pairs, owner):
    groups = lax.axis_size("dates")
    here = lax.axis_index("dates")
    date_dev = slc.shape[1]
    rows = slc.shape[2]
    width = slc.shape[3]
    total_pairs = pairs.shape[0]
    block = total_pairs // groups
    capacity = block + max(1, block // 2)
    all_dates = date_dev * groups
    local_power = jnp.sum(jnp.square(slc.astype(jnp.float32)), axis=(0, 2, 3))
    spread = lax.dynamic_update_slice(
        jnp.zeros((all_dates,), jnp.float32), local_power, (here * date_dev,)
    )
    totals = lax.psum(spread, ("dates", "cols"))
    scales = jnp.sqrt(totals / (rows * width * lax.axis_size("cols")) + 1e-06)
    order = jnp.arange(total_pairs, dtype=jnp.int32)
    same = owner[:, None] == owner[None, :]
    rank = jnp.sum(same & (order[None, :] < order[:, None]), axis=1)
    mine = (owner[None, :] == here) & (
        rank[None, :] == jnp.arange(capacity, dtype=jnp.int32)[:, None]
    )
    chosen = jnp.stack(
        [
            jnp.sum(jnp.where(mine, pairs[None, :, 0], 0), axis=1),
            jnp.sum(jnp.where(mine, pairs[None, :, 1], 0), axis=1),
        ],
        axis=1,
    )
    first_date = chosen[:, 0]
    second_date = chosen[:, 1]
    piece = lax.all_gather(slc, "dates", axis=1, tiled=True)
    span = piece.shape[1]
    local_dates = jnp.arange(span, dtype=jnp.int32)
    picks = jnp.stack(
        [first_date[:, None] == local_dates[None, :], second_date[:, None] == local_dates[None, :]],
        axis=1,
    ).astype(jnp.bfloat16)
    taken = jnp.einsum("stj,cjrw->stcrw", picks, piece, preferred_element_type=jnp.float32)
    tiles = taken.astype(jnp.bfloat16)
    tiles = padded_2(tiles, (("cols", 4),), 4)
    calendar = jnp.arange(all_dates, dtype=jnp.int32)
    first_scale = jnp.sum(
        jnp.where(first_date[:, None] == calendar[None, :], scales[None, :], 0.0), axis=1
    )
    second_scale = jnp.sum(
        jnp.where(second_date[:, None] == calendar[None, :], scales[None, :], 0.0), axis=1
    )

    def run_slot(item):
        return one_pair(item[0], item[1], item[2])

    results = lax.map(run_slot, (tiles, first_scale, second_scale))
    filled = jnp.any(mine, axis=1)
    placed = jnp.where(filled[:, None, None, None], results, 0.0)
    return (jnp.moveaxis(placed[:, 0:2], 1, 0), placed[:, 2])


def solution(mesh):
    return jax.shard_map(
        local,
        mesh=mesh,
        in_specs=(P(None, "dates", None, "cols"), P(), P()),
        out_specs=(P(None, "dates", None, "cols"), P("dates", None, "cols")),
        check_vma=False,
    )
```

profile of v0, /device:TPU:1, one launch (start us, length us, event | category | flops | bytes accessed | tf_op | source)
XLA Modules:
  0.0 247.3 jit_solution(4043667768932498026)
XLA Ops:
  7.2 1.9 copy.22
  9.1 1.3 multiply_reduce_fusion
  10.6 106.9 %psum.7 = f32[32]{0:T(128)S(1)} all-reduce(f32[32]{0:T(128)S(1)} %dynamic_update_slice.10), channel_id=1, replica_groups=mesh['dates'=8,'cols'=64] {'dates','cols'}, use_global_device_ids=true, to_apply=%region_5.6 | all-reduce | flops 32 | bytes 256 | tf_op jit(solution)/shard_map/psum | solution.py:85
  117.5 0.9 convert_reduce_fusion
  118.4 0.7 broadcast_compare_fusion
  119.1 0.8 slice_bitcast_fusion.2
  120.2 4.8 %fusion.63 = bf16[12,2,2,128,256]{4,0,3,2,1:T(8,128)(2,1)S(1)} fusion(bf16[2,32,128,256]{3,2,0,1:T(8,128)(2,1)} %all-gather.2.cloned.1.call-done, pred[12,1,32]{2,0,1:T(8,128)(4,1)S(1)} %get-tuple-element.116, pred[12,1,32]{2,0,1:T(8,128)(4,1)S(1)} %get-tuple-element.117), kind=kOutput, calls=%fused_computation.126 | convolution fusion | flops 102236928 | bytes 7340800 | tf_op jit(solution)/shard_map/stj,cjrw->stcrw/dot_general | solution.py:109
  125.0 1.9 copy-done
  126.9 2.3 fusion.72
  129.2 2.9 %copy.24 = bf16[12,2,2,128,4]{3,4,2,1,0:T(4,128)(2,1)S(1)} copy(bf16[12,2,2,128,4]{4,0,3,2,1:T(8,128)(2,1)} %get-tuple-element.112) | data formatting | bytes 98304 | tf_op jit(solution)/shard_map/slice | solution.py:17
  132.1 1.8 collective-permute-start
  133.8 1.4 copy.25
  135.3 1.5 collective-permute-start.1
  136.9 1.7 copy.26
  138.6 1.5 collective-permute-done.1
  140.1 2.5 %copy.27 = bf16[12,2,2,128,4]{4,0,3,2,1:T(8,128)(2,1)} copy(bf16[12,2,2,128,4]{3,4,2,1,0:T(4,128)(2,1)S(1)} %collective-permute-done.1) | data formatting | bytes 98304 | tf_op jit(solution)/shard_map/ppermute | solution.py:22
  142.6 6.1 %pad_maximum_fusion = bf16[12,2,2,128,264]{4,0,3,2,1:T(8,128)(2,1)S(1)} fusion(bf16[12,2,2,128,4]{4,0,3,2,1:T(8,128)(2,1)} %copy.27, bf16[12,2,2,128,256]{4,0,3,2,1:T(8,128)(2,1)} %copy-done, bf16[12,2,2,128,4]{4,0,3,2,1:T(8,128)(2,1)S(1)} %copy.26), kind=kLoop, calls=%fused_computation.122 | loop fusion | flops 9732096 | bytes 6488064 | tf_op jit(solution)/shard_map/concatenate | solution.py:18
  148.8 3.3 %copy.29 = bf16[12,2,2,128,264]{4,3,2,1,0:T(8,128)(2,1)} copy(bf16[12,2,2,128,264]{4,0,3,2,1:T(8,128)(2,1)S(1)} %pad_maximum_fusion) | data formatting | bytes 6488064 | tf_op jit(solution)/shard_map/while | solution.py:123
  152.1 86.9 %while.13 = (s32[]{:T(128)}, f32[12,3,32,16]{2,3,0,1:T(8,128)S(1)}, bf16[12,2,2,128,264]{4,3,2,1,0:T(8,128)(2,1)}, f32[12]{0:T(128)S(1)}, f32[12]{0:T(128)S(1)}) while((s32[]{:T(128)}, f32[12,3,32,16]{2,3,0,1:T(8,128)S(1)}, bf16[12,2,2,128,264]{4,3,2,1,0:T(8,128)(2,1)}, f32[12]{0:T(128)S(1)}, f32[12]{0:T(128)S(1)}) %tuple.60), condition=%wide.region_12.13_spmd.clone, body=%wide.region_8.12_spmd.sunk.clone | while | flops 5365763 | bytes 9619577 | solution.py:123
  152.1 1.0 bitcast_convert_fusion.3
  154.0 1.2 fusion.75
  155.7 0.6 dynamic_slice.28
  159.3 1.1 bitcast_convert_fusion.3
  161.3 1.2 fusion.75
  166.6 1.1 bitcast_convert_fusion.3
  168.5 1.2 fusion.75
  173.8 1.1 bitcast_convert_fusion.3
  175.8 1.2 fusion.75
  181.0 1.1 bitcast_convert_fusion.3
  183.0 1.2 fusion.75
  184.7 0.6 dynamic_slice.28
  188.3 1.1 bitcast_convert_fusion.3
  190.2 1.2 fusion.75
  195.5 1.1 bitcast_convert_fusion.3
  197.5 1.2 fusion.75
  202.8 1.1 bitcast_convert_fusion.3
  204.7 1.2 fusion.75
  210.0 1.1 bitcast_convert_fusion.3
  212.0 1.2 fusion.75
  213.6 0.6 dynamic_slice.28
  217.3 1.1 bitcast_convert_fusion.3
  219.2 1.2 fusion.75
  224.5 1.1 bitcast_convert_fusion.3
  226.5 1.2 fusion.75
  231.8 1.1 bitcast_convert_fusion.3
  233.7 1.2 fusion.75
  239.1 0.7 slice_bitcast_fusion
  239.8 0.6 slice_bitcast_fusion.1
  (227 shorter events, 43.7 us)
Async XLA Ops:
  7.2 113.0 %all-gather.2.cloned.1.call-start = ((), (), s32[]{:S(2)}) async-start(), calls=%async_computation | async-start | bytes 4718592 | tf_op jit(solution)/shard_map/all_gather | solution.py:102
  125.0 1.9 copy-start
  132.1 4.8 %collective-permute-start = (bf16[12,2,2,128,4]{3,4,2,1,0:T(4,128)(2,1)S(1)}, bf16[12,2,2,128,4]{3,4,2,1,0:T(4,128)(2,1)S(1)}, u32[]{:S(2)}, u32[]{:S(2)}) collective-permute-start(bf16[12,2,2,128,4]{3,4,2,1,0:T(4,128)(2,1)S(1)} %copy.24), channel_id=1, source_target_pairs={{0,1},{1,2},{2,3},{3,4},{4,5},{5,6},{6,7},{7,8},{8,9},{9,10},{10,1... | collective-permute-start | bytes 147464 | tf_op jit(solution)/shard_map/ppermute | solution.py:20
  135.3 4.8 %collective-permute-start.1 = (bf16[12,2,2,128,4]{3,4,2,1,0:T(4,128)(2,1)S(1)}, bf16[12,2,2,128,4]{3,4,2,1,0:T(4,128)(2,1)S(1)}, u32[]{:S(2)}, u32[]{:S(2)}) collective-permute-start(bf16[12,2,2,128,4]{3,4,2,1,0:T(4,128)(2,1)S(1)} %copy.25), channel_id=1, source_target_pairs={{1,0},{2,1},{3,2},{4,3},{5,4},{6,5},{7,6},{8,7},{9,8},{10,9},{11,1... | collective-permute-start | bytes 147464 | tf_op jit(solution)/shard_map/ppermute | solution.py:22
Sparse Core Ops, SparseCore 0:
  10.1 43.3 all-gather.1
where the time goes:
time: 250 us; the launch traced here: 247 us
  blocking collectives  107 us (43%)
  other arithmetic  52.2 us (21%)
  local copies, waits for them, and re-layouts  48.7 us (19%)
  loops' own time  15.8 us (6%)
  between operations  14.1 us (6%)
  matrix products  4.78 us (2%)
  starting transfers between devices  3.29 us (1%)
    psum x1, blocking collectives, local(): totals = lax.psum(spread, ('dates', 'cols'))  107 us
    another operation x1, loops' own time, local(): results = lax.map(run_slot, (tiles, first_scale, second_scale))  15.8 us
    div x12, other arithmetic, one_pair(): jnp.sqrt(smooth_real * smooth_real + smooth_imag * smooth_imag)  13.9 us
    dynamic_slice x24, local copies, waits for them, and re-layouts, local(): results = lax.map(run_slot, (tiles, first_scale, second_scale))  13.7 us
    convert_element_type x12, other arithmetic, one_pair(): values = tile.astype(jnp.float32)  12.7 us
    reshape x36, local copies, waits for them, and re-layouts, looks(): return jnp.mean(plane.reshape(count // 4, 4, inner // 16, 16), axis=(1, 3))  11.7 us
    add x24, other arithmetic, smooth(): along = along + WEIGHTS[k] * padded[k:k + count]  9.44 us
    concatenate x1, other arithmetic, padded_2(): jnp.concatenate([lax.ppermute(tail, axis, [(i, (i + 1) % count) for i in...  6.14 us
  transfers between devices with their start and end apart: 3, of which 1 were waited for; matrix products, arithmetic and copies ran while one was open for 3% of the time, Pallas kernels for 0%

commit v1 on v0

v1 whole, which is shorter than its diff:
```python
import math

import jax
import jax.numpy as jnp
import ml_dtypes
import numpy as np
from jax import lax
from jax.experimental import pallas as pl
from jax.experimental.pallas import tpu as pltpu
from jax.sharding import PartitionSpec as P

MESH = pl.DeviceIdType.MESH
F32 = jnp.float32
BF16 = jnp.bfloat16

TAPS = [math.exp(-k * k / 8.0) for k in range(-4, 5)]
WEIGHTS = [float(np.float32(t / sum(TAPS))) for t in TAPS]
HIGH = [float(np.float32(w).astype(ml_dtypes.bfloat16)) for w in WEIGHTS]
LOW = [float(np.float32(w - h).astype(ml_dtypes.bfloat16)) for w, h in zip(WEIGHTS, HIGH)]

GROUP = 8
EACH = 4
DATES = GROUP * EACH
PAIRS = 64
CAP = 12
ROWS = 128
PART = 32
TILE = PART + 8
WIDTH = GROUP * PART
BLOCK = EACH * 2 * TILE
EDGE = EACH * 2 * 8
CHUNK = 8


def split(x):
    high = x.astype(BF16)
    return high, (x - high.astype(F32)).astype(BF16)


def split3(x):
    high = x.astype(BF16)
    rest = x - high.astype(F32)
    mid = rest.astype(BF16)
    return high, mid, (rest - mid.astype(F32)).astype(BF16)


def dot(a, b):
    return jnp.dot(a, b, preferred_element_type=F32)


def iota(shape, axis):
    return lax.broadcasted_iota(jnp.int32, shape, axis)


def cutter():
    lane = iota((TILE, WIDTH), 1)
    row = iota((TILE, WIDTH), 0)
    pieces = [jnp.where(lane == row + (PART * e - 4), 1.0, 0.0) for e in range(GROUP)]
    lane = iota((8, WIDTH), 1)
    row = iota((8, WIDTH), 0)
    pieces.append(jnp.where(lane == row + (WIDTH - 4), 1.0, 0.0))
    pieces.append(jnp.where(lane == row - 4, 1.0, 0.0))
    return jnp.concatenate(pieces, axis=0).astype(BF16)


def band(weights):
    gap = jnp.abs(iota((ROWS, ROWS), 0) - iota((ROWS, ROWS), 1))
    result = jnp.zeros((ROWS, ROWS), F32)
    for k in range(5):
        result = jnp.where(gap == k, weights[4 + k], result)
    return result.astype(BF16)


def along_columns(ref, index):
    result = WEIGHTS[4] * ref[index, 4 : 4 + PART, :]
    for k in range(4):
        both = ref[index, k : k + PART, :] + ref[index, 8 - k : 8 - k + PART, :]
        result = result + WEIGHTS[k] * both
    return result


def kernel(
    ny, nz, slc, pairs_s, pairs_v, owner_v, landed,
    smoother, sent, got, edge_out, edge_in, images, roots, fields, lhs, sums,
    power_y, power_z, power_d, power_y_in, power_z_in, totals, results,
    main_send, main_recv, edge_send, edge_recv, y_send, y_recv, z_send, z_recv,
    d_send, d_recv, out_send, out_recv,
):
    d = lax.axis_index("dates")
    c = lax.axis_index("cols")
    count = ny * nz
    y = c // nz
    z = c % nz

    def date_peer(k):
        return {"dates": (d + k) % GROUP, "cols": c}

    def y_peer(k):
        return {"dates": d, "cols": ((y + k) % ny) * nz + z}

    def z_peer(k):
        return {"dates": d, "cols": y * nz + (z + k) % nz}

    after = (c + 1) % count
    before = (c + count - 1) % count

    barrier = pltpu.get_barrier_semaphore()

    def greet(device):
        pl.semaphore_signal(barrier, inc=1, device_id=device, device_id_type=MESH)

    for k in range(1, GROUP):
        greet(date_peer(k))
    for k in range(1, ny):
        greet(y_peer(k))
    for k in range(1, nz):
        greet(z_peer(k))

    @pl.when(d == 0)
    def _():
        for e in range(GROUP):
            greet({"dates": e, "cols": before})

    @pl.when(d == GROUP - 1)
    def _():
        for e in range(GROUP):
            greet({"dates": e, "cols": after})

    cut = cutter()
    power_rows = []
    for t in range(EACH):
        both = jnp.concatenate([slc[0, t], slc[1, t]], axis=0)
        turned = lax.dot_general(cut, both, (((1,), (1,)), ((), ())), preferred_element_type=F32)
        real = turned[:, :ROWS]
        imag = turned[:, ROWS:]
        for e in range(GROUP):
            part = slice(TILE * e, TILE * e + TILE)
            sent[e, 2 * TILE * t : 2 * TILE * (t + 1), :] = jnp.concatenate(
                [real[part], imag[part]], axis=0
            ).astype(BF16)
        for side in range(2):
            part = slice(TILE * GROUP + 8 * side, TILE * GROUP + 8 * side + 8)
            edge_out[side, 16 * t : 16 * (t + 1), :] = jnp.concatenate(
                [real[part], imag[part]], axis=0
            ).astype(BF16)
        wide = both.astype(F32)
        square = jnp.sum(wide * wide, axis=0, keepdims=True)
        power_rows.append(square[:, :ROWS] + square[:, ROWS:])
    power_y[...] = jnp.concatenate(power_rows + [jnp.zeros((8 - EACH, ROWS), F32)], axis=0)

    pl.semaphore_wait(barrier, (GROUP - 1) + (ny - 1) + (nz - 1) + 2)

    def spread(src, dst, send, recv, peer, number):
        copies = []
        for k in range(1, number):
            copy = pltpu.make_async_remote_copy(
                src_ref=src(k), dst_ref=dst(k), send_sem=send.at[k - 1], recv_sem=recv.at[k - 1],
                device_id=peer(k), device_id_type=MESH,
            )
            copy.start()
            copies.append(copy)
        return copies

    y_copies = spread(lambda k: power_y, lambda k: power_y_in.at[k - 1], y_send, y_recv, y_peer, ny)
    main_copies = spread(
        lambda k: sent.at[(d + k) % GROUP], lambda k: got.at[d], main_send, main_recv, date_peer, GROUP
    )
    edge_copies = []
    for side, device in enumerate(
        ({"dates": 0, "cols": after}, {"dates": GROUP - 1, "cols": before})
    ):
        copy = pltpu.make_async_remote_copy(
            src_ref=edge_out.at[side], dst_ref=edge_in.at[d], send_sem=edge_send.at[side],
            recv_sem=edge_recv.at[d], device_id=device, device_id_type=MESH,
        )
        copy.start()
        edge_copies.append(copy)

    high = band(HIGH)
    low = band(LOW)
    smoother[:, :ROWS] = jnp.concatenate([high, high], axis=0)
    smoother[:, ROWS:] = jnp.concatenate([low, low], axis=0)

    owner_row = owner_v[...]
    owner_down = jnp.transpose(jnp.broadcast_to(owner_row.astype(F32), (ROWS, PAIRS)))[:, :PAIRS]
    earlier = iota((PAIRS, PAIRS), 0) < iota((PAIRS, PAIRS), 1)
    same = owner_down == owner_row.astype(F32)
    rank = jnp.sum(jnp.where(same & earlier, 1.0, 0.0), axis=0, keepdims=True).astype(jnp.int32)
    place = (rank & 3) * 32 + owner_row * 4 + (rank >> 2)
    select = jnp.where(iota((128, PAIRS), 0) == place, 1.0, 0.0).astype(BF16)

    def date_rows(which):
        date = pairs_v[which : which + 1, :]
        row = ((date >> 2) * 8 + (date & 3)).astype(F32)
        down = jnp.transpose(jnp.broadcast_to(row, (ROWS, PAIRS)))[:, : 8 * GROUP]
        lane = iota((PAIRS, 8 * GROUP), 1).astype(F32)
        return jnp.where(down == lane, 1.0, 0.0).astype(BF16)

    def take(source, block):
        for t in range(EACH):
            piece = block[2 * TILE * t : 2 * TILE * (t + 1), :].astype(F32)
            images[source * EACH + t, 0] = piece[:TILE]
            images[source * EACH + t, 1] = piece[TILE:]

        @pl.when((d == 0) & (c > 0))
        def _():
            for t in range(EACH):
                piece = edge_in[source, 16 * t : 16 * (t + 1), :].astype(F32)
                images[source * EACH + t, 0, 0:8] += piece[:8]
                images[source * EACH + t, 1, 0:8] += piece[8:]

        @pl.when((d == GROUP - 1) & (c < count - 1))
        def _():
            for t in range(EACH):
                piece = edge_in[source, 16 * t : 16 * (t + 1), :].astype(F32)
                images[source * EACH + t, 0, TILE - 8 : TILE] += piece[:8]
                images[source * EACH + t, 1, TILE - 8 : TILE] += piece[8:]

        for t in range(EACH):
            real = images[source * EACH + t, 0]
            imag = images[source * EACH + t, 1]
            fields[t] = real * real + imag * imag
        for t in range(EACH):
            big, small = split(along_columns(fields, t))
            lhs[PART * t : PART * (t + 1), :ROWS] = big
            lhs[PART * t : PART * (t + 1), ROWS:] = small
        smooth = dot(lhs[: EACH * PART, :], smoother[...])
        smooth = jnp.sqrt(smooth[:, :ROWS] + smooth[:, ROWS:])
        for t in range(EACH):
            roots[source * EACH + t] = smooth[PART * t : PART * (t + 1)]

    @pl.when((d == 0) | (d == GROUP - 1))
    def _():
        for e in range(GROUP):
            pltpu.make_async_remote_copy(
                src_ref=edge_out.at[0], dst_ref=edge_in.at[e], send_sem=edge_send.at[0],
                recv_sem=edge_recv.at[e], device_id=date_peer(1), device_id_type=MESH,
            ).wait_recv()

    take(d, sent.at[d])

    def arrive(k):
        main_copies[k - 1].wait_recv()
        source = (d + GROUP - k) % GROUP
        take(source, got.at[source])

    for copy in y_copies:
        copy.wait_recv()
    power = power_y[...]
    for k in range(1, ny):
        power = power + power_y_in[k - 1]
    power_z[...] = power
    z_copies = spread(lambda k: power_z, lambda k: power_z_in.at[k - 1], z_send, z_recv, z_peer, nz)
    arrive(1)
    arrive(7)
    for copy in z_copies:
        copy.wait_recv()
    power = power_z[...]
    for k in range(1, nz):
        power = power + power_z_in[k - 1]
    power_d[...] = power
    totals[d] = power
    d_copies = spread(lambda k: power_d, lambda k: totals.at[d], d_send, d_recv, date_peer, GROUP)
    arrive(2)
    arrive(6)
    arrive(3)
    arrive(5)
    arrive(4)
    for copy in d_copies:
        copy.wait_recv()

    def chunk(index, carry):
        dates = []
        for i in range(CHUNK):
            p = index * CHUNK + i
            first = pairs_s[0, p]
            second = pairs_s[1, p]
            dates.append((first, second))
            real_a = images[first, 0]
            imag_a = images[first, 1]
            real_b = images[second, 0]
            imag_b = images[second, 1]
            fields[2 * i] = real_a * real_b + imag_a * imag_b
            fields[2 * i + 1] = imag_a * real_b - real_a * imag_b
        for i in range(CHUNK):
            p = index * CHUNK + i
            for f in range(2):
                n = 2 * i + f
                big, small = split(along_columns(fields, n))
                lhs[PART * n : PART * (n + 1), :ROWS] = big
                lhs[PART * n : PART * (n + 1), ROWS:] = small
                sums[f, p] = fields[n, 4:12, :] + fields[n, 12:20, :]
                sums[3 + f, p] = fields[n, 20:28, :] + fields[n, 28:36, :]
        smooth = dot(lhs[...], smoother[...])
        smooth = smooth[:, :ROWS] + smooth[:, ROWS:]
        for i in range(CHUNK):
            p = index * CHUNK + i
            first, second = dates[i]
            real = smooth[2 * PART * i : 2 * PART * i + PART]
            imag = smooth[2 * PART * i + PART : 2 * PART * (i + 1)]
            value = jnp.sqrt(real * real + imag * imag) / (roots[first] * roots[second] + 1e-06)
            sums[2, p] = value[0:8] + value[8:16]
            sums[5, p] = value[16:24] + value[24:32]
        return carry

    lax.fori_loop(0, PAIRS // CHUNK, chunk, 0)

    flat = totals[...].reshape(8 * GROUP, ROWS)
    parts = split3(flat)

    def scale(which):
        hot = date_rows(which)
        taken = dot(hot, parts[0]) + dot(hot, parts[1]) + dot(hot, parts[2])
        total = jnp.sum(taken, axis=1, keepdims=True)
        return jnp.sqrt(total / (ROWS * WIDTH * count) + 1e-06)

    factor = (1.0 / 64.0) / (scale(0) * scale(1))

    look = jnp.where((iota((ROWS, 128), 0) >> 2) == (iota((ROWS, 128), 1) & 31), 1.0, 0.0).astype(BF16)
    lane = iota((32, 128), 1)
    for q in range(6):
        rows = sums[q, :, 0, :]
        for s in range(1, 8):
            rows = rows + sums[q, :, s, :]
        a, b, e = split3(rows)
        looked = dot(a, look) + dot(b, look) + dot(e, look)
        looked = looked * (factor if q % 3 < 2 else 1.0 / 64.0)
        a, b, e = split3(looked)
        placed = dot(select, a) + dot(select, b) + dot(select, e)
        value = jnp.where(
            lane < 64,
            jnp.where(lane < 32, placed[0:32], placed[32:64]),
            jnp.where(lane < 96, placed[64:96], placed[96:128]),
        )
        for e in range(GROUP):
            results[e, 4 * q : 4 * q + 4, :] = value[4 * e : 4 * e + 4]

    out_copies = spread(
        lambda k: results.at[(d + k) % GROUP], lambda k: landed.at[d], out_send, out_recv, date_peer, GROUP
    )
    landed[d] = results[d]
    for copy in out_copies:
        copy.wait()
    for copy in y_copies + z_copies + d_copies + main_copies + edge_copies:
        copy.wait_send()


def place_kernel(landed, interferogram, coherence):
    for f in range(3):
        for g in range(3):
            block = landed[pl.ds(f * 4 + g, 16, stride=12), :]
            for j in range(4):
                piece = block[:, 32 * j : 32 * j + 32]
                if f < 2:
                    interferogram[f, 4 * g + j] = piece
                else:
                    coherence[4 * g + j] = piece


def solution(mesh):
    columns = mesh.shape["cols"]
    nz = 8 if columns % 8 == 0 else columns
    ny = columns // nz
    sem = pltpu.SemaphoreType.DMA
    vmem = pl.BlockSpec(memory_space=pltpu.VMEM)

    def local(slc, pairs, owner):
        pairs = pairs.T
        owner = owner.reshape(1, PAIRS)
        landed = pl.pallas_call(
            lambda *refs: kernel(ny, nz, *refs),
            out_shape=jax.ShapeDtypeStruct((GROUP, 24, 128), F32),
            in_specs=[vmem, pl.BlockSpec(memory_space=pltpu.SMEM), vmem, vmem],
            out_specs=vmem,
            scratch_shapes=[
                pltpu.VMEM((2 * ROWS, 2 * ROWS), BF16),
                pltpu.VMEM((GROUP, BLOCK, ROWS), BF16),
                pltpu.VMEM((GROUP, BLOCK, ROWS), BF16),
                pltpu.VMEM((2, EDGE, ROWS), BF16),
                pltpu.VMEM((GROUP, EDGE, ROWS), BF16),
                pltpu.VMEM((DATES, 2, TILE, ROWS), F32),
                pltpu.VMEM((DATES, PART, ROWS), F32),
                pltpu.VMEM((2 * CHUNK, TILE, ROWS), F32),
                pltpu.VMEM((2 * CHUNK * PART, 2 * ROWS), BF16),
                pltpu.VMEM((6, PAIRS, 8, ROWS), F32),
                pltpu.VMEM((8, ROWS), F32),
                pltpu.VMEM((8, ROWS), F32),
                pltpu.VMEM((8, ROWS), F32),
                pltpu.VMEM((max(ny - 1, 1), 8, ROWS), F32),
                pltpu.VMEM((max(nz - 1, 1), 8, ROWS), F32),
                pltpu.VMEM((GROUP, 8, ROWS), F32),
                pltpu.VMEM((GROUP, 24, 128), F32),
                sem((GROUP - 1,)), sem((GROUP - 1,)),
                sem((2,)), sem((GROUP,)),
                sem((max(ny - 1, 1),)), sem((max(ny - 1, 1),)),
                sem((max(nz - 1, 1),)), sem((max(nz - 1, 1),)),
                sem((GROUP - 1,)), sem((GROUP - 1,)),
                sem((GROUP - 1,)), sem((GROUP - 1,)),
            ],
            compiler_params=pltpu.CompilerParams(
                collective_id=0, has_side_effects=True, vmem_limit_bytes=40 * 1024 * 1024
            ),
        )(slc, pairs, pairs, owner)
        interferogram, coherence = pl.pallas_call(
            place_kernel,
            out_shape=(
                jax.ShapeDtypeStruct((2, CAP, 16, 32), F32),
                jax.ShapeDtypeStruct((CAP, 16, 32), F32),
            ),
            in_specs=[vmem],
            out_specs=(vmem, vmem),
        )(landed.reshape(GROUP * 24, 128))
        return jnp.swapaxes(interferogram, 2, 3), jnp.swapaxes(coherence, 1, 2)

    return jax.shard_map(
        local,
        mesh=mesh,
        in_specs=(P(None, "dates", None, "cols"), P(), P()),
        out_specs=(P(None, "dates", None, "cols"), P("dates", None, "cols")),
        check_vma=False,
    )
```

time: 250 us -> 43.3 us (0.17); the launches traced: 247 us -> 43.1 us
  blocking collectives: 107 us -> 0 us
  other arithmetic: 52.2 us -> 0 us
  local copies, waits for them, and re-layouts: 48.7 us -> 2.34 us
  Pallas kernels: 0 us -> 40.1 us
  loops' own time: 15.8 us -> 0 us
  between operations: 14.1 us -> 0.66 us
  matrix products: 4.78 us -> 0 us
  starting transfers between devices: 3.29 us -> 0 us
    psum x1 -> x0, blocking collectives: 107 us -> none  [local(): totals = lax.psum(spread, ('dates', 'cols'))]
    pallas_call x0 -> x2, Pallas kernels: none -> 40.1 us  [the longest x1 38.4 us: local(): pl.pallas_call(lambda *refs: kernel(ny, nz, *refs), out_shape=jax.ShapeDt...]
    another operation x1 -> x0, loops' own time: 15.8 us -> none  [local(): results = lax.map(run_slot, (tiles, first_scale, second_scale))]
    div x36 -> x0, other arithmetic: 14.1 us -> none  [the longest x12 13.9 us: one_pair(): jnp.sqrt(smooth_real * smooth_real + smooth_imag * smooth_imag)]
    dynamic_slice x24 -> x0, local copies, waits for them, and re-layouts: 13.7 us -> none  [local(): results = lax.map(run_slot, (tiles, first_scale, second_scale))]
    convert_element_type x12 -> x0, other arithmetic: 12.7 us -> none  [one_pair(): values = tile.astype(jnp.float32)]
    reshape x36 -> x0, local copies, waits for them, and re-layouts: 11.7 us -> none  [looks(): return jnp.mean(plane.reshape(count // 4, 4, inner // 16, 16), axis=(1, 3))]
    add x36 -> x0, other arithmetic: 10.5 us -> none  [the longest x24 9.44 us: smooth(): along = along + WEIGHTS[k] * padded[k:k + count]]
  transfers between devices with their start and end apart: 3 -> 0, of which waited for: 1 -> 0; matrix products, arithmetic and copies ran while one was open for 3% -> 0% of each run, Pallas kernels for 0% -> 0%
where the time goes in v1:
time: 43.3 us; the launch traced here: 43.1 us
  Pallas kernels  40.1 us (93%)
  local copies, waits for them, and re-layouts  2.34 us (5%)
  between operations  0.66 us (2%)
    pallas_call x1, Pallas kernels, local(): pl.pallas_call(lambda *refs: kernel(ny, nz, *refs), out_shape=jax.ShapeDt...  38.4 us
    unnamed x8, local copies, waits for them, and re-layouts  2.34 us
    pallas_call x1, Pallas kernels, local(): pl.pallas_call(place_kernel, out_shape=(jax.ShapeDtypeStruct((2, CAP, 16,...  1.7 us

profile of v1, /device:TPU:1, one launch (start us, length us, event | category | flops | bytes accessed | tf_op | source)
XLA Modules:
  0.0 43.1 jit_solution(3828343912390381634)
XLA Ops:
  0.6 0.0 copy-start.2
  0.6 0.0 copy-start.3
  0.6 0.7 %copy-done.2 = s32[64,2]{0,1:T(2,128)S(1)} copy-done((s32[64,2]{0,1:T(2,128)S(1)}, s32[64,2]{0,1:T(2,128)}, u32[]{:S(2)}) %copy-start.2) | copy-done | bytes 536
  1.3 0.0 copy-done.3
  1.3 0.0 copy-start
  1.3 1.0 %copy-done = bf16[2,4,128,256]{3,2,1,0:T(8,128)(2,1)S(1)} copy-done((bf16[2,4,128,256]{3,2,1,0:T(8,128)(2,1)S(1)}, bf16[2,4,128,256]{3,2,1,0:T(8,128)(2,1)}, u32[]{:S(2)}) %copy-start) | copy-done | bytes 524312
  2.4 38.4 %shard_map.50 = f32[8,24,128]{2,1,0:T(8,128)S(1)} custom-call(bf16[2,4,128,256]{3,2,1,0:T(8,128)(2,1)S(1)} %copy-done, s32[2,64]{1,0:T(2,128)S(1)} %bitcast.6, s32[2,64]{1,0:T(2,128)S(1)} %bitcast.7, s32[1,64]{1,0:T(1,128)S(1)} %bitcast.8), custom_call_target="tpu_custom_call" | custom-call | tf_op jit(solution)/shard_map/pallas_call | solution.py:370
  40.8 0.0 copy-start.1
  40.8 0.6 %copy-done.1 = f32[8,24,128]{2,1,0:T(8,128)} copy-done((f32[8,24,128]{2,1,0:T(8,128)}, f32[8,24,128]{2,1,0:T(8,128)S(1)}, u32[]{:S(2)}) %copy-start.1) | copy-done | bytes 98328
  41.4 1.7 %shard_map.51 = (f32[2,12,16,32]{3,2,1,0:T(8,128)}, f32[12,16,32]{2,1,0:T(8,128)}) custom-call(f32[192,128]{1,0:T(8,128)} %bitcast.5), custom_call_target="tpu_custom_call" | custom-call | tf_op jit(solution)/shard_map/pallas_call | solution.py:404
Async XLA Ops:
  0.6 0.7 %copy-start.2 = (s32[64,2]{0,1:T(2,128)S(1)}, s32[64,2]{0,1:T(2,128)}, u32[]{:S(2)}) copy-start(s32[64,2]{0,1:T(2,128)} %param.4) | copy-start | bytes 1540
  0.6 0.7 %copy-start.3 = (s32[64]{0:T(128)S(1)}, s32[64]{0:T(128)}, u32[]{:S(2)}) copy-start(s32[64]{0:T(128)} %param.5) | copy-start | bytes 772
  1.3 1.0 %copy-start = (bf16[2,4,128,256]{3,2,1,0:T(8,128)(2,1)S(1)}, bf16[2,4,128,256]{3,2,1,0:T(8,128)(2,1)}, u32[]{:S(2)}) copy-start(bf16[2,4,128,256]{3,2,1,0:T(8,128)(2,1)} %refs_0_.1) | copy-start | bytes 1572868
  40.8 0.6 %copy-start.1 = (f32[8,24,128]{2,1,0:T(8,128)}, f32[8,24,128]{2,1,0:T(8,128)S(1)}, u32[]{:S(2)}) copy-start(f32[8,24,128]{2,1,0:T(8,128)S(1)} %shard_map.50) | copy-start | bytes 294916

commit v2 on v1

--- a/solution.py
+++ b/solution.py
@@ -80,11 +80,11 @@
 
 
 def kernel(
-    ny, nz, slc, pairs_s, pairs_v, owner_v, landed,
-    smoother, sent, got, edge_out, edge_in, images, roots, fields, lhs, sums,
+    ny, nz, slc_hbm, pairs_hbm, owner_hbm, landed,
+    slc, pairs_s, pairs_v, owner_v, select, look, hot, smoother, sent, got, edge_out, edge_in, images, roots, fields, lhs, sums,
     power_y, power_z, power_d, power_y_in, power_z_in, totals, results,
     main_send, main_recv, edge_send, edge_recv, y_send, y_recv, z_send, z_recv,
-    d_send, d_recv, out_send, out_recv,
+    d_send, d_recv, out_send, out_recv, in_sem, table_sem,
 ):
     d = lax.axis_index("dates")
     c = lax.axis_index("cols")
@@ -104,6 +104,12 @@
     after = (c + 1) % count
     before = (c + count - 1) % count
 
+    loads = [
+        pltpu.make_async_copy(slc_hbm.at[:, t], slc.at[:, t], in_sem.at[t]) for t in range(EACH)
+    ]
+    for load in loads:
+        load.start()
+
     barrier = pltpu.get_barrier_semaphore()
 
     def greet(device):
@@ -126,9 +132,18 @@
         for e in range(GROUP):
             greet({"dates": e, "cols": after})
 
+    tables = [
+        pltpu.make_async_copy(pairs_hbm, pairs_s, table_sem.at[0]),
+        pltpu.make_async_copy(pairs_hbm, pairs_v, table_sem.at[1]),
+        pltpu.make_async_copy(owner_hbm, owner_v, table_sem.at[2]),
+    ]
+    for table in tables:
+        table.start()
+
     cut = cutter()
     power_rows = []
     for t in range(EACH):
+        loads[t].wait()
         both = jnp.concatenate([slc[0, t], slc[1, t]], axis=0)
         turned = lax.dot_general(cut, both, (((1,), (1,)), ((), ())), preferred_element_type=F32)
         real = turned[:, :ROWS]
@@ -151,20 +166,17 @@
     pl.semaphore_wait(barrier, (GROUP - 1) + (ny - 1) + (nz - 1) + 2)
 
     def spread(src, dst, send, recv, peer, number):
-        copies = []
-        for k in range(1, number):
+        copies = {}
+        for k in sorted(range(1, number), key=lambda k: -min(k, number - k)):
             copy = pltpu.make_async_remote_copy(
                 src_ref=src(k), dst_ref=dst(k), send_sem=send.at[k - 1], recv_sem=recv.at[k - 1],
                 device_id=peer(k), device_id_type=MESH,
             )
             copy.start()
-            copies.append(copy)
+            copies[k] = copy
         return copies
 
     y_copies = spread(lambda k: power_y, lambda k: power_y_in.at[k - 1], y_send, y_recv, y_peer, ny)
-    main_copies = spread(
-        lambda k: sent.at[(d + k) % GROUP], lambda k: got.at[d], main_send, main_recv, date_peer, GROUP
-    )
     edge_copies = []
     for side, device in enumerate(
         ({"dates": 0, "cols": after}, {"dates": GROUP - 1, "cols": before})
@@ -175,26 +187,37 @@
         )
         copy.start()
         edge_copies.append(copy)
+    main_copies = spread(
+        lambda k: sent.at[(d + k) % GROUP], lambda k: got.at[d], main_send, main_recv, date_peer, GROUP
+    )
 
     high = band(HIGH)
     low = band(LOW)
     smoother[:, :ROWS] = jnp.concatenate([high, high], axis=0)
     smoother[:, ROWS:] = jnp.concatenate([low, low], axis=0)
 
+    for table in tables:
+        table.wait()
     owner_row = owner_v[...]
     owner_down = jnp.transpose(jnp.broadcast_to(owner_row.astype(F32), (ROWS, PAIRS)))[:, :PAIRS]
     earlier = iota((PAIRS, PAIRS), 0) < iota((PAIRS, PAIRS), 1)
     same = owner_down == owner_row.astype(F32)
     rank = jnp.sum(jnp.where(same & earlier, 1.0, 0.0), axis=0, keepdims=True).astype(jnp.int32)
     place = (rank & 3) * 32 + owner_row * 4 + (rank >> 2)
-    select = jnp.where(iota((128, PAIRS), 0) == place, 1.0, 0.0).astype(BF16)
+    one = jnp.where(iota((128, PAIRS), 0) == place, 1.0, 0.0)
+    select[...] = jnp.concatenate([one, one, one], axis=1).astype(BF16)
 
     def date_rows(which):
         date = pairs_v[which : which + 1, :]
         row = ((date >> 2) * 8 + (date & 3)).astype(F32)
         down = jnp.transpose(jnp.broadcast_to(row, (ROWS, PAIRS)))[:, : 8 * GROUP]
         lane = iota((PAIRS, 8 * GROUP), 1).astype(F32)
-        return jnp.where(down == lane, 1.0, 0.0).astype(BF16)
+        one = jnp.where(down == lane, 1.0, 0.0)
+        return jnp.concatenate([one, one, one], axis=1).astype(BF16)
+
+    hot[...] = jnp.concatenate([date_rows(0), date_rows(1)], axis=0)
+    one = jnp.where((iota((ROWS, 128), 0) >> 2) == (iota((ROWS, 128), 1) & 31), 1.0, 0.0)
+    look[...] = jnp.concatenate([one, one, one], axis=0).astype(BF16)
 
     def take(source, block):
         for t in range(EACH):
@@ -229,6 +252,19 @@
         for t in range(EACH):
             roots[source * EACH + t] = smooth[PART * t : PART * (t + 1)]
 
+    def arrive(k):
+        main_copies[k].wait_recv()
+        source = (d + GROUP - k) % GROUP
+        take(source, got.at[source])
+
+    for copy in y_copies.values():
+        copy.wait_recv()
+    power = power_y[...]
+    for k in range(1, ny):
+        power = power + power_y_in[k - 1]
+    power_z[...] = power
+    z_copies = spread(lambda k: power_z, lambda k: power_z_in.at[k - 1], z_send, z_recv, z_peer, nz)
+
     @pl.when((d == 0) | (d == GROUP - 1))
     def _():
         for e in range(GROUP):
@@ -238,22 +274,11 @@
             ).wait_recv()
 
     take(d, sent.at[d])
-
-    def arrive(k):
-        main_copies[k - 1].wait_recv()
-        source = (d + GROUP - k) % GROUP
-        take(source, got.at[source])
-
-    for copy in y_copies:
-        copy.wait_recv()
-    power = power_y[...]
-    for k in range(1, ny):
-        power = power + power_y_in[k - 1]
-    power_z[...] = power
-    z_copies = spread(lambda k: power_z, lambda k: power_z_in.at[k - 1], z_send, z_recv, z_peer, nz)
     arrive(1)
     arrive(7)
-    for copy in z_copies:
+    arrive(2)
+    arrive(6)
+    for copy in z_copies.values():
         copy.wait_recv()
     power = power_z[...]
     for k in range(1, nz):
@@ -261,13 +286,9 @@
     power_d[...] = power
     totals[d] = power
     d_copies = spread(lambda k: power_d, lambda k: totals.at[d], d_send, d_recv, date_peer, GROUP)
-    arrive(2)
-    arrive(6)
     arrive(3)
     arrive(5)
     arrive(4)
-    for copy in d_copies:
-        copy.wait_recv()
 
     def chunk(index, carry):
         dates = []
@@ -289,8 +310,8 @@
                 big, small = split(along_columns(fields, n))
                 lhs[PART * n : PART * (n + 1), :ROWS] = big
                 lhs[PART * n : PART * (n + 1), ROWS:] = small
-                sums[f, p] = fields[n, 4:12, :] + fields[n, 12:20, :]
-                sums[3 + f, p] = fields[n, 20:28, :] + fields[n, 28:36, :]
+                sums[pl.ds((f * PAIRS + p) * 8, 8), :] = fields[n, 4:12, :] + fields[n, 12:20, :]
+                sums[pl.ds(((3 + f) * PAIRS + p) * 8, 8), :] = fields[n, 20:28, :] + fields[n, 28:36, :]
         smooth = dot(lhs[...], smoother[...])
         smooth = smooth[:, :ROWS] + smooth[:, ROWS:]
         for i in range(CHUNK):
@@ -299,38 +320,36 @@
             real = smooth[2 * PART * i : 2 * PART * i + PART]
             imag = smooth[2 * PART * i + PART : 2 * PART * (i + 1)]
             value = jnp.sqrt(real * real + imag * imag) / (roots[first] * roots[second] + 1e-06)
-            sums[2, p] = value[0:8] + value[8:16]
-            sums[5, p] = value[16:24] + value[24:32]
+            sums[pl.ds((2 * PAIRS + p) * 8, 8), :] = value[0:8] + value[8:16]
+            sums[pl.ds((5 * PAIRS + p) * 8, 8), :] = value[16:24] + value[24:32]
         return carry
 
     lax.fori_loop(0, PAIRS // CHUNK, chunk, 0)
 
-    flat = totals[...].reshape(8 * GROUP, ROWS)
-    parts = split3(flat)
-
-    def scale(which):
-        hot = date_rows(which)
-        taken = dot(hot, parts[0]) + dot(hot, parts[1]) + dot(hot, parts[2])
-        total = jnp.sum(taken, axis=1, keepdims=True)
-        return jnp.sqrt(total / (ROWS * WIDTH * count) + 1e-06)
-
-    factor = (1.0 / 64.0) / (scale(0) * scale(1))
-
-    look = jnp.where((iota((ROWS, 128), 0) >> 2) == (iota((ROWS, 128), 1) & 31), 1.0, 0.0).astype(BF16)
+    for copy in d_copies.values():
+        copy.wait_recv()
+    parts = jnp.concatenate(split3(totals[...].reshape(8 * GROUP, ROWS)), axis=0)
+    total = jnp.sum(dot(hot[...], parts), axis=1, keepdims=True)
+    scale = jnp.sqrt(total / (ROWS * WIDTH * count) + 1e-06)
+    factor = (1.0 / 64.0) / (scale[:PAIRS] * scale[PAIRS:])
+
+    rows = sums[pl.ds(0, 6 * PAIRS, stride=8), :]
+    for i in range(1, 8):
+        rows = rows + sums[pl.ds(i, 6 * PAIRS, stride=8), :]
+    looked = dot(jnp.concatenate(split3(rows), axis=1), look[...])
+    wide = []
+    for q in range(6):
+        piece = looked[PAIRS * q : PAIRS * (q + 1)]
+        wide.append(piece * (factor if q % 3 < 2 else 1.0 / 64.0))
+    stacked = jnp.concatenate(split3(jnp.concatenate(wide, axis=1)), axis=0)
+    placed = dot(select[...], stacked)
     lane = iota((32, 128), 1)
     for q in range(6):
-        rows = sums[q, :, 0, :]
-        for s in range(1, 8):
-            rows = rows + sums[q, :, s, :]
-        a, b, e = split3(rows)
-        looked = dot(a, look) + dot(b, look) + dot(e, look)
-        looked = looked * (factor if q % 3 < 2 else 1.0 / 64.0)
-        a, b, e = split3(looked)
-        placed = dot(select, a) + dot(select, b) + dot(select, e)
+        part = placed[:, 128 * q : 128 * (q + 1)]
         value = jnp.where(
             lane < 64,
-            jnp.where(lane < 32, placed[0:32], placed[32:64]),
-            jnp.where(lane < 96, placed[64:96], placed[96:128]),
+            jnp.where(lane < 32, part[0:32], part[32:64]),
+            jnp.where(lane < 96, part[64:96], part[96:128]),
         )
         for e in range(GROUP):
             results[e, 4 * q : 4 * q + 4, :] = value[4 * e : 4 * e + 4]
@@ -339,10 +358,13 @@
         lambda k: results.at[(d + k) % GROUP], lambda k: landed.at[d], out_send, out_recv, date_peer, GROUP
     )
     landed[d] = results[d]
-    for copy in out_copies:
+    for copies in (y_copies, z_copies, d_copies, main_copies):
+        for copy in copies.values():
+            copy.wait_send()
+    for copy in edge_copies:
+        copy.wait_send()
+    for copy in out_copies.values():
         copy.wait()
-    for copy in y_copies + z_copies + d_copies + main_copies + edge_copies:
-        copy.wait_send()
 
 
 def place_kernel(landed, interferogram, coherence):
@@ -370,9 +392,16 @@
         landed = pl.pallas_call(
             lambda *refs: kernel(ny, nz, *refs),
             out_shape=jax.ShapeDtypeStruct((GROUP, 24, 128), F32),
-            in_specs=[vmem, pl.BlockSpec(memory_space=pltpu.SMEM), vmem, vmem],
+            in_specs=[pl.BlockSpec(memory_space=pl.ANY)] * 3,
             out_specs=vmem,
             scratch_shapes=[
+                pltpu.VMEM((2, EACH, ROWS, WIDTH), BF16),
+                pltpu.SMEM((2, PAIRS), jnp.int32),
+                pltpu.VMEM((2, PAIRS), jnp.int32),
+                pltpu.VMEM((1, PAIRS), jnp.int32),
+                pltpu.VMEM((128, 3 * PAIRS), BF16),
+                pltpu.VMEM((3 * ROWS, 128), BF16),
+                pltpu.VMEM((2 * PAIRS, 24 * GROUP), BF16),
                 pltpu.VMEM((2 * ROWS, 2 * ROWS), BF16),
                 pltpu.VMEM((GROUP, BLOCK, ROWS), BF16),
                 pltpu.VMEM((GROUP, BLOCK, ROWS), BF16),
@@ -382,7 +411,7 @@
                 pltpu.VMEM((DATES, PART, ROWS), F32),
                 pltpu.VMEM((2 * CHUNK, TILE, ROWS), F32),
                 pltpu.VMEM((2 * CHUNK * PART, 2 * ROWS), BF16),
-                pltpu.VMEM((6, PAIRS, 8, ROWS), F32),
+                pltpu.VMEM((6 * PAIRS * 8, ROWS), F32),
                 pltpu.VMEM((8, ROWS), F32),
                 pltpu.VMEM((8, ROWS), F32),
                 pltpu.VMEM((8, ROWS), F32),
@@ -396,11 +425,12 @@
                 sem((max(nz - 1, 1),)), sem((max(nz - 1, 1),)),
                 sem((GROUP - 1,)), sem((GROUP - 1,)),
                 sem((GROUP - 1,)), sem((GROUP - 1,)),
+                sem((EACH,)), sem((3,)),
             ],
             compiler_params=pltpu.CompilerParams(
-                collective_id=0, has_side_effects=True, vmem_limit_bytes=40 * 1024 * 1024
+                collective_id=0, has_side_effects=True, vmem_limit_bytes=62 * 1024 * 1024
             ),
-        )(slc, pairs, pairs, owner)
+        )(slc, pairs, owner)
         interferogram, coherence = pl.pallas_call(
             place_kernel,
             out_shape=(

time: 43.3 us -> 37.3 us (0.86)
  Pallas kernels: 40.1 us -> 36.5 us
  local copies, waits for them, and re-layouts: 2.34 us -> 0 us
    pallas_call x1, Pallas kernels: 38.4 us -> 34.8 us  [local(): pl.pallas_call(lambda *refs: kernel(ny, nz, *refs), out_shape=jax.ShapeDt...]
    unnamed x8 -> x0, local copies, waits for them, and re-layouts: 2.34 us -> none
where the time goes in v2:
time: 37.3 us; the launch traced here: 37.1 us
  Pallas kernels  36.5 us (98%)
  between operations  0.64 us (2%)
    pallas_call x1, Pallas kernels, local(): pl.pallas_call(lambda *refs: kernel(ny, nz, *refs), out_shape=jax.ShapeDt...  34.8 us
    pallas_call x1, Pallas kernels, local(): pl.pallas_call(place_kernel, out_shape=(jax.ShapeDtypeStruct((2, CAP, 16,...  1.7 us

profile of v2, /device:TPU:1, one launch (start us, length us, event | category | flops | bytes accessed | tf_op | source)
XLA Modules:
  0.0 37.1 jit_solution(18146899685006283931)
XLA Ops:
  0.6 34.8 %shard_map.50 = f32[8,24,128]{2,1,0:T(8,128)} custom-call(bf16[2,4,128,256]{3,2,1,0:T(8,128)(2,1)} %refs_0_.1, s32[2,64]{1,0:T(2,128)} %bitcast.6, s32[1,64]{1,0:T(1,128)} %bitcast.7), custom_call_target="tpu_custom_call" | custom-call | tf_op jit(solution)/shard_map/pallas_call | solution.py:392
  35.4 1.7 %shard_map.51 = (f32[2,12,16,32]{3,2,1,0:T(8,128)}, f32[12,16,32]{2,1,0:T(8,128)}) custom-call(f32[192,128]{1,0:T(8,128)} %bitcast.5), custom_call_target="tpu_custom_call" | custom-call | tf_op jit(solution)/shard_map/pallas_call | solution.py:434

commit v3 on v2

v3 whole, which is shorter than its diff:
```python
import math

import jax
import jax.numpy as jnp
import ml_dtypes
import numpy as np
from jax import lax
from jax.experimental import pallas as pl
from jax.experimental.pallas import tpu as pltpu
from jax.sharding import PartitionSpec as P

MESH = pl.DeviceIdType.MESH
F32 = jnp.float32
BF16 = jnp.bfloat16

TAPS = [math.exp(-k * k / 8.0) for k in range(-4, 5)]
WEIGHTS = [float(np.float32(t / sum(TAPS))) for t in TAPS]
HIGH = [float(np.float32(w).astype(ml_dtypes.bfloat16)) for w in WEIGHTS]
LOW = [float(np.float32(w - h).astype(ml_dtypes.bfloat16)) for w, h in zip(WEIGHTS, HIGH)]

GROUP = 8
EACH = 4
DATES = GROUP * EACH
PAIRS = 64
CAP = 12
ROWS = 128
PART = 32
TILE = PART + 8
WIDTH = GROUP * PART
PIECES = (24, 16)
HALF = PART // 2
WINDOW = HALF + 8
EDGE = EACH * 2 * 8
CHUNK = 16


def split(x):
    high = x.astype(BF16)
    return high, (x - high.astype(F32)).astype(BF16)


def split3(x):
    high = x.astype(BF16)
    rest = x - high.astype(F32)
    mid = rest.astype(BF16)
    return high, mid, (rest - mid.astype(F32)).astype(BF16)


def dot(a, b):
    return jnp.dot(a, b, preferred_element_type=F32)


def iota(shape, axis):
    return lax.broadcasted_iota(jnp.int32, shape, axis)


def cutter(half):
    start, size = (-4, PIECES[0]) if half == 0 else (PIECES[0] - 4, PIECES[1])
    lane = iota((size, WIDTH), 1)
    row = iota((size, WIDTH), 0)
    pieces = [jnp.where(lane == row + (PART * e + start), 1.0, 0.0) for e in range(GROUP)]
    lane = iota((8, WIDTH), 1)
    row = iota((8, WIDTH), 0)
    pieces.append(jnp.where(lane == row + (WIDTH - 4 if half == 0 else -4), 1.0, 0.0))
    return jnp.concatenate(pieces, axis=0).astype(BF16)


def band(weights):
    gap = jnp.abs(iota((ROWS, ROWS), 0) - iota((ROWS, ROWS), 1))
    result = jnp.zeros((ROWS, ROWS), F32)
    for k in range(5):
        result = jnp.where(gap == k, weights[4 + k], result)
    return result.astype(BF16)


def along_columns(ref, index):
    result = WEIGHTS[4] * ref[index, 4 : 4 + HALF, :]
    for k in range(4):
        both = ref[index, k : k + HALF, :] + ref[index, 8 - k : 8 - k + HALF, :]
        result = result + WEIGHTS[k] * both
    return result


def kernel(
    ny, nz, slc_hbm, pairs_hbm, owner_hbm, interferogram, coherence,
    landed,    slc, pairs_s, pairs_v, owner_v, select, look, hot, smoother, sent_0, sent_1, got_0, got_1, edge_out, edge_left, edge_right, images, roots, fields, lhs, sums,
    looked, power_y, power_z, power_d, power_y_in, power_z_in, totals, results,
    main_send_0, main_recv_0, main_send_1, main_recv_1, edge_send, edge_recv, y_send, y_recv, z_send, z_recv,
    d_send, d_recv, out_send, out_recv, in_sem, table_sem,
):
    d = lax.axis_index("dates")
    c = lax.axis_index("cols")
    count = ny * nz
    y = c // nz
    z = c % nz

    def date_peer(k):
        return {"dates": (d + k) % GROUP, "cols": c}

    def y_peer(k):
        return {"dates": d, "cols": ((y + k) % ny) * nz + z}

    def z_peer(k):
        return {"dates": d, "cols": y * nz + (z + k) % nz}

    after = (c + 1) % count
    before = (c + count - 1) % count

    loads = [
        pltpu.make_async_copy(slc_hbm.at[:, t], slc.at[:, t], in_sem.at[t]) for t in range(EACH)
    ]
    for load in loads:
        load.start()

    barrier = pltpu.get_barrier_semaphore()

    def greet(device):
        pl.semaphore_signal(barrier, inc=1, device_id=device, device_id_type=MESH)

    for k in range(1, GROUP):
        greet(date_peer(k))
    for k in range(1, ny):
        greet(y_peer(k))
    for k in range(1, nz):
        greet(z_peer(k))

    @pl.when(d == 0)
    def _():
        for e in range(GROUP):
            greet({"dates": e, "cols": before})

    @pl.when(d == GROUP - 1)
    def _():
        for e in range(GROUP):
            greet({"dates": e, "cols": after})

    tables = [
        pltpu.make_async_copy(pairs_hbm, pairs_s, table_sem.at[0]),
        pltpu.make_async_copy(pairs_hbm, pairs_v, table_sem.at[1]),
        pltpu.make_async_copy(owner_hbm, owner_v, table_sem.at[2]),
    ]
    for table in tables:
        table.start()

    sent = (sent_0, sent_1)
    edge_in = (edge_left, edge_right)
    got = (got_0, got_1)

    def cut(half):
        size = PIECES[half]
        matrix = cutter(half)
        for t in range(EACH):
            if half == 0:
                loads[t].wait()
            both = jnp.concatenate([slc[0, t], slc[1, t]], axis=0)
            turned = lax.dot_general(
                matrix, both, (((1,), (1,)), ((), ())), preferred_element_type=F32
            )
            for e in range(GROUP + 1):
                rows = turned[size * e : size * (e + 1)] if e < GROUP else turned[size * GROUP :]
                value = jnp.concatenate([rows[:, :ROWS], rows[:, ROWS:]], axis=0).astype(BF16)
                if e < GROUP:
                    sent[half][e, 2 * size * t : 2 * size * (t + 1), :] = value
                else:
                    edge_out[half, 16 * t : 16 * (t + 1), :] = value

    cut(0)

    pl.semaphore_wait(barrier, (GROUP - 1) + (ny - 1) + (nz - 1) + 2)

    def spread(src, dst, send, recv, peer, number):
        copies = {}
        for k in sorted(range(1, number), key=lambda k: -min(k, number - k)):
            copy = pltpu.make_async_remote_copy(
                src_ref=src(k), dst_ref=dst(k), send_sem=send.at[k - 1], recv_sem=recv.at[k - 1],
                device_id=peer(k), device_id_type=MESH,
            )
            copy.start()
            copies[k] = copy
        return copies

    edge_copies = []

    def send_edge(side, device):
        copy = pltpu.make_async_remote_copy(
            src_ref=edge_out.at[side], dst_ref=edge_in[side].at[d], send_sem=edge_send.at[side],
            recv_sem=edge_recv.at[d], device_id=device, device_id_type=MESH,
        )
        copy.start()
        edge_copies.append(copy)

    def send_half(half, send, recv):
        return spread(
            lambda k: sent[half].at[(d + k) % GROUP], lambda k: got[half].at[d], send, recv,
            date_peer, GROUP,
        )

    send_edge(0, {"dates": 0, "cols": after})
    main_0 = send_half(0, main_send_0, main_recv_0)
    power_rows = []
    for t in range(EACH):
        wide = jnp.concatenate([slc[0, t], slc[1, t]], axis=0).astype(F32)
        square = jnp.sum(wide * wide, axis=0, keepdims=True)
        power_rows.append(square[:, :ROWS] + square[:, ROWS:])
    power_y[...] = jnp.concatenate(power_rows + [jnp.zeros((8 - EACH, ROWS), F32)], axis=0)
    y_copies = spread(lambda k: power_y, lambda k: power_y_in.at[k - 1], y_send, y_recv, y_peer, ny)
    cut(1)
    send_edge(1, {"dates": GROUP - 1, "cols": before})
    main_1 = send_half(1, main_send_1, main_recv_1)
    got_1[d] = sent_1[d]

    @pl.when(d != 0)
    def _():
        edge_left[...] = jnp.zeros_like(edge_left)

    @pl.when(d != GROUP - 1)
    def _():
        edge_right[...] = jnp.zeros_like(edge_right)


    high = band(HIGH)
    low = band(LOW)
    smoother[:, :ROWS] = jnp.concatenate([high, high], axis=0)
    smoother[:, ROWS:] = jnp.concatenate([low, low], axis=0)

    for table in tables:
        table.wait()
    owner_row = owner_v[...]
    owner_down = jnp.transpose(jnp.broadcast_to(owner_row.astype(F32), (ROWS, PAIRS)))[:, :PAIRS]
    earlier = iota((PAIRS, PAIRS), 0) < iota((PAIRS, PAIRS), 1)
    same = owner_down == owner_row.astype(F32)
    rank = jnp.sum(jnp.where(same & earlier, 1.0, 0.0), axis=0, keepdims=True).astype(jnp.int32)
    place = (rank & 3) * 32 + owner_row * 4 + (rank >> 2)
    one = jnp.where(iota((128, PAIRS), 0) == place, 1.0, 0.0)
    select[...] = jnp.concatenate([one, one, one], axis=1).astype(BF16)

    def date_rows(which):
        date = pairs_v[which : which + 1, :]
        row = ((date >> 2) * 8 + (date & 3)).astype(F32)
        down = jnp.transpose(jnp.broadcast_to(row, (ROWS, PAIRS)))[:, : 8 * GROUP]
        lane = iota((PAIRS, 8 * GROUP), 1).astype(F32)
        one = jnp.where(down == lane, 1.0, 0.0)
        return jnp.concatenate([one, one, one], axis=1).astype(BF16)

    hot[...] = jnp.concatenate([date_rows(0), date_rows(1)], axis=0)
    one = jnp.where((iota((ROWS, 128), 0) >> 2) == (iota((ROWS, 128), 1) & 31), 1.0, 0.0)
    look[...] = jnp.concatenate([one, one, one], axis=0).astype(BF16)

    def edges(side):
        for e in range(GROUP):
            pltpu.make_async_remote_copy(
                src_ref=edge_out.at[side], dst_ref=edge_in[side].at[e], send_sem=edge_send.at[side],
                recv_sem=edge_recv.at[e], device_id=date_peer(1), device_id_type=MESH,
            ).wait_recv()

    left_gate = jnp.where(c > 0, 1.0, 0.0).astype(F32)
    right_gate = jnp.where(c < count - 1, 1.0, 0.0).astype(F32)

    def smooth_powers(number):
        for t in range(number):
            big, small = split(along_columns(fields, t))
            lhs[HALF * t : HALF * (t + 1), :ROWS] = big
            lhs[HALF * t : HALF * (t + 1), ROWS:] = small
        smooth = dot(lhs[: number * HALF, :], smoother[...])
        return jnp.sqrt(smooth[:, :ROWS] + smooth[:, ROWS:])

    def take_first(source, block):
        size = PIECES[0]
        for t in range(EACH):
            piece = block[2 * size * t : 2 * size * (t + 1), :].astype(F32)
            edge = edge_left[source, 16 * t : 16 * (t + 1), :].astype(F32) * left_gate
            real = jnp.concatenate([piece[:8] + edge[:8], piece[8:size]], axis=0)
            imag = jnp.concatenate([piece[size : size + 8] + edge[8:], piece[size + 8 :]], axis=0)
            images[source * EACH + t, 0, :size] = real
            images[source * EACH + t, 1, :size] = imag
            fields[t] = real * real + imag * imag
        smooth = smooth_powers(EACH)
        for t in range(EACH):
            roots[source * EACH + t, :HALF] = smooth[HALF * t : HALF * (t + 1)]

    def arrive(k):
        main_0[k].wait_recv()
        source = (d + GROUP - k) % GROUP
        take_first(source, got_0.at[source])

    def take_second():
        size = PIECES[1]
        for date in range(DATES):
            source, t = date // EACH, date % EACH
            piece = got_1[source, 2 * size * t : 2 * size * (t + 1), :].astype(F32)
            edge = edge_right[source, 16 * t : 16 * (t + 1), :].astype(F32) * right_gate
            real = jnp.concatenate([piece[:8], piece[8:size] + edge[:8]], axis=0)
            imag = jnp.concatenate([piece[size : size + 8], piece[size + 8 :] + edge[8:]], axis=0)
            images[date, 0, PIECES[0] :] = real
            images[date, 1, PIECES[0] :] = imag
            real = jnp.concatenate([images[date, 0, HALF : PIECES[0]], real], axis=0)
            imag = jnp.concatenate([images[date, 1, HALF : PIECES[0]], imag], axis=0)
            fields[date] = real * real + imag * imag
        smooth = smooth_powers(DATES)
        for date in range(DATES):
            roots[date, HALF:] = smooth[HALF * date : HALF * (date + 1)]

    def pairs_of(half):
        window = slice(HALF * half, HALF * half + WINDOW)

        def place(field, p):
            return pl.ds(((3 * half + field) * PAIRS + p) * 8, 8)

        def chunk(index, carry):
            dates = []
            for i in range(CHUNK):
                p = index * CHUNK + i
                first = pairs_s[0, p]
                second = pairs_s[1, p]
                dates.append((first, second))
                real_a = images[first, 0, window]
                imag_a = images[first, 1, window]
                real_b = images[second, 0, window]
                imag_b = images[second, 1, window]
                fields[2 * i] = real_a * real_b + imag_a * imag_b
                fields[2 * i + 1] = imag_a * real_b - real_a * imag_b
            for i in range(CHUNK):
                p = index * CHUNK + i
                for f in range(2):
                    n = 2 * i + f
                    big, small = split(along_columns(fields, n))
                    lhs[HALF * n : HALF * (n + 1), :ROWS] = big
                    lhs[HALF * n : HALF * (n + 1), ROWS:] = small
                    sums[place(f, p), :] = fields[n, 4:12, :] + fields[n, 12:20, :]
            smooth = dot(lhs[...], smoother[...])
            smooth = smooth[:, :ROWS] + smooth[:, ROWS:]
            for i in range(CHUNK):
                p = index * CHUNK + i
                first, second = dates[i]
                real = smooth[2 * HALF * i : 2 * HALF * i + HALF]
                imag = smooth[2 * HALF * i + HALF : 2 * HALF * (i + 1)]
                below = (
                    roots[first, HALF * half : HALF * (half + 1)]
                    * roots[second, HALF * half : HALF * (half + 1)]
                )
                value = jnp.sqrt(real * real + imag * imag) / (below + 1e-06)
                sums[place(2, p), :] = value[0:8] + value[8:16]
            return carry

        lax.fori_loop(0, PAIRS // CHUNK, chunk, 0)
        rows = sums[pl.ds(3 * half * PAIRS * 8, 3 * PAIRS, stride=8), :]
        for i in range(1, 8):
            rows = rows + sums[pl.ds(3 * half * PAIRS * 8 + i, 3 * PAIRS, stride=8), :]
        looked[half] = dot(jnp.concatenate(split3(rows), axis=1), look[...])

    for copy in y_copies.values():
        copy.wait_recv()
    power = power_y[...]
    for k in range(1, ny):
        power = power + power_y_in[k - 1]
    power_z[...] = power
    z_copies = spread(lambda k: power_z, lambda k: power_z_in.at[k - 1], z_send, z_recv, z_peer, nz)

    @pl.when(d == 0)
    def _():
        edges(0)

    take_first(d, sent_0.at[d])
    for k in (4, 3, 5, 2, 6, 1, 7):
        arrive(k)
    for copy in z_copies.values():
        copy.wait_recv()
    power = power_z[...]
    for k in range(1, nz):
        power = power + power_z_in[k - 1]
    power_d[...] = power
    totals[d] = power
    d_copies = spread(lambda k: power_d, lambda k: totals.at[d], d_send, d_recv, date_peer, GROUP)
    pairs_of(0)

    @pl.when(d == GROUP - 1)
    def _():
        edges(1)

    for k in (4, 3, 5, 2, 6, 1, 7):
        main_1[k].wait_recv()
    take_second()
    pairs_of(1)

    for copy in d_copies.values():
        copy.wait_recv()
    parts = jnp.concatenate(split3(totals[...].reshape(8 * GROUP, ROWS)), axis=0)
    total = jnp.sum(dot(hot[...], parts), axis=1, keepdims=True)
    scale = jnp.sqrt(total / (ROWS * WIDTH * count) + 1e-06)
    factor = (1.0 / 64.0) / (scale[:PAIRS] * scale[PAIRS:])

    wide = []
    for q in range(6):
        piece = looked[q // 3, PAIRS * (q % 3) : PAIRS * (q % 3 + 1)]
        wide.append(piece * (factor if q % 3 < 2 else 1.0 / 64.0))
    stacked = jnp.concatenate(split3(jnp.concatenate(wide, axis=1)), axis=0)
    placed = dot(select[...], stacked)
    lane = iota((32, 128), 1)
    for q in range(6):
        part = placed[:, 128 * q : 128 * (q + 1)]
        value = jnp.where(
            lane < 64,
            jnp.where(lane < 32, part[0:32], part[32:64]),
            jnp.where(lane < 96, part[64:96], part[96:128]),
        )
        for e in range(GROUP):
            results[e, 4 * q : 4 * q + 4, :] = value[4 * e : 4 * e + 4]

    out_copies = spread(
        lambda k: results.at[(d + k) % GROUP], lambda k: landed.at[d], out_send, out_recv, date_peer, GROUP
    )
    landed[d] = results[d]
    for copy in out_copies.values():
        copy.wait_recv()
    flat = landed.reshape(GROUP * 24, 128)
    for f in range(3):
        for g in range(3):
            block = flat[pl.ds(f * 4 + g, 16, stride=12), :]
            for j in range(4):
                piece = block[:, 32 * j : 32 * j + 32]
                if f < 2:
                    interferogram[f, 4 * g + j] = piece
                else:
                    coherence[4 * g + j] = piece
    for copies in (y_copies, z_copies, d_copies, main_0, main_1, out_copies):
        for copy in copies.values():
            copy.wait_send()
    for copy in edge_copies:
        copy.wait_send()


def solution(mesh):
    columns = mesh.shape["cols"]
    nz = 8 if columns % 8 == 0 else columns
    ny = columns // nz
    sem = pltpu.SemaphoreType.DMA
    vmem = pl.BlockSpec(memory_space=pltpu.VMEM)

    def local(slc, pairs, owner):
        pairs = pairs.T
        owner = owner.reshape(1, PAIRS)
        interferogram, coherence = pl.pallas_call(
            lambda *refs: kernel(ny, nz, *refs),
            out_shape=(jax.ShapeDtypeStruct((2, CAP, 16, 32), F32), jax.ShapeDtypeStruct((CAP, 16, 32), F32)),
            in_specs=[pl.BlockSpec(memory_space=pl.ANY)] * 3,
            out_specs=(vmem, vmem),
            scratch_shapes=[
                pltpu.VMEM((GROUP, 24, 128), F32),
                pltpu.VMEM((2, EACH, ROWS, WIDTH), BF16),
                pltpu.SMEM((2, PAIRS), jnp.int32),
                pltpu.VMEM((2, PAIRS), jnp.int32),
                pltpu.VMEM((1, PAIRS), jnp.int32),
                pltpu.VMEM((128, 3 * PAIRS), BF16),
                pltpu.VMEM((3 * ROWS, 128), BF16),
                pltpu.VMEM((2 * PAIRS, 24 * GROUP), BF16),
                pltpu.VMEM((2 * ROWS, 2 * ROWS), BF16),
                pltpu.VMEM((GROUP, EACH * 2 * PIECES[0], ROWS), BF16),
                pltpu.VMEM((GROUP, EACH * 2 * PIECES[1], ROWS), BF16),
                pltpu.VMEM((GROUP, EACH * 2 * PIECES[0], ROWS), BF16),
                pltpu.VMEM((GROUP, EACH * 2 * PIECES[1], ROWS), BF16),
                pltpu.VMEM((2, EDGE, ROWS), BF16),
                pltpu.VMEM((GROUP, EDGE, ROWS), BF16),
                pltpu.VMEM((GROUP, EDGE, ROWS), BF16),
                pltpu.VMEM((DATES, 2, TILE, ROWS), F32),
                pltpu.VMEM((DATES, PART, ROWS), F32),
                pltpu.VMEM((2 * CHUNK, WINDOW, ROWS), F32),
                pltpu.VMEM((2 * CHUNK * HALF, 2 * ROWS), BF16),
                pltpu.VMEM((6 * PAIRS * 8, ROWS), F32),
                pltpu.VMEM((2, 3 * PAIRS, ROWS), F32),
                pltpu.VMEM((8, ROWS), F32),
                pltpu.VMEM((8, ROWS), F32),
                pltpu.VMEM((8, ROWS), F32),
                pltpu.VMEM((max(ny - 1, 1), 8, ROWS), F32),
                pltpu.VMEM((max(nz - 1, 1), 8, ROWS), F32),
                pltpu.VMEM((GROUP, 8, ROWS), F32),
                pltpu.VMEM((GROUP, 24, 128), F32),
                sem((GROUP - 1,)), sem((GROUP - 1,)),
                sem((GROUP - 1,)), sem((GROUP - 1,)),
                sem((2,)), sem((GROUP,)),
                sem((max(ny - 1, 1),)), sem((max(ny - 1, 1),)),
                sem((max(nz - 1, 1),)), sem((max(nz - 1, 1),)),
                sem((GROUP - 1,)), sem((GROUP - 1,)),
                sem((GROUP - 1,)), sem((GROUP - 1,)),
                sem((EACH,)), sem((3,)),
            ],
            compiler_params=pltpu.CompilerParams(
                collective_id=0, has_side_effects=True, vmem_limit_bytes=54682 * 1024
            ),
        )(slc, pairs, owner)
        return jnp.swapaxes(interferogram, 2, 3), jnp.swapaxes(coherence, 1, 2)

    return jax.shard_map(
        local,
        mesh=mesh,
        in_specs=(P(None, "dates", None, "cols"), P(), P()),
        out_specs=(P(None, "dates", None, "cols"), P("dates", None, "cols")),
        check_vma=False,
    )
```

time: 37.3 us -> 36.8 us (0.987)
  Pallas kernels: 36.5 us -> 34 us
  local copies, waits for them, and re-layouts: 0 us -> 1.99 us
    pallas_call x2 -> x1, Pallas kernels: 36.5 us -> 34 us  [local(): pl.pallas_call(lambda *refs: kernel(ny, nz, *refs), out_shape=(jax.ShapeD...]
    unnamed x0 -> x6, local copies, waits for them, and re-layouts: none -> 1.99 us
where the time goes in v3:
time: 36.8 us; the launch traced here: 36.6 us
  Pallas kernels  34 us (92%)
  local copies, waits for them, and re-layouts  1.99 us (5%)
  between operations  0.66 us (2%)
    pallas_call x1, Pallas kernels, local(): pl.pallas_call(lambda *refs: kernel(ny, nz, *refs), out_shape=(jax.ShapeD...  34 us
    unnamed x6, local copies, waits for them, and re-layouts  1.99 us

profile of v3, /device:TPU:1, one launch (start us, length us, event | category | flops | bytes accessed | tf_op | source)
XLA Modules:
  0.0 36.6 jit_solution(9865835817448607655)
XLA Ops:
  0.6 0.0 copy-start
  0.6 0.0 copy-start.1
  0.6 0.7 %copy-done = s32[64,2]{0,1:T(2,128)S(1)} copy-done((s32[64,2]{0,1:T(2,128)S(1)}, s32[64,2]{0,1:T(2,128)}, u32[]{:S(2)}) %copy-start) | copy-done | bytes 536
  1.3 0.0 copy-done.1
  1.3 34.0 %shard_map.50 = (f32[2,12,16,32]{3,2,1,0:T(8,128)S(1)}, f32[12,16,32]{2,1,0:T(8,128)S(1)}) custom-call(bf16[2,4,128,256]{3,2,1,0:T(8,128)(2,1)} %refs_0_.1, s32[2,64]{1,0:T(2,128)S(1)} %bitcast.6, s32[1,64]{1,0:T(1,128)S(1)} %bitcast.7), custom_call_target="tpu_custom_call" | custom-call | tf_op jit(solution)/shard_map/pallas_call | solution.py:442
  35.3 0.7 %copy.7 = f32[2,12,32,16]{2,3,1,0:T(8,128)} copy(f32[2,12,32,16]{2,3,1,0:T(8,128)S(1)} %bitcast.4) | data formatting | bytes 98304
  36.0 0.6 %copy.8 = f32[12,32,16]{1,2,0:T(8,128)} copy(f32[12,32,16]{1,2,0:T(8,128)S(1)} %bitcast.5) | data formatting | bytes 49152
Async XLA Ops:
  0.6 0.7 %copy-start = (s32[64,2]{0,1:T(2,128)S(1)}, s32[64,2]{0,1:T(2,128)}, u32[]{:S(2)}) copy-start(s32[64,2]{0,1:T(2,128)} %param.4) | copy-start | bytes 1540
  0.6 0.7 %copy-start.1 = (s32[64]{0:T(128)S(1)}, s32[64]{0:T(128)}, u32[]{:S(2)}) copy-start(s32[64]{0:T(128)} %param.5) | copy-start | bytes 772

commit v4 on v3

--- a/solution.py
+++ b/solution.py
@@ -82,8 +82,8 @@
 
 
 def kernel(
-    ny, nz, slc_hbm, pairs_hbm, owner_hbm, interferogram, coherence,
-    landed,    slc, pairs_s, pairs_v, owner_v, select, look, hot, smoother, sent_0, sent_1, got_0, got_1, edge_out, edge_left, edge_right, images, roots, fields, lhs, sums,
+    ny, nz, slc_hbm, pairs_hbm, owner_hbm, landed, scaling,
+       slc, pairs_s, pairs_v, owner_v, select, own, look, hot, smoother, sent_0, sent_1, got_0, got_1, edge_out, edge_left, edge_right, images, roots, fields, lhs, sums,
     looked, power_y, power_z, power_d, power_y_in, power_z_in, totals, results,
     main_send_0, main_recv_0, main_send_1, main_recv_1, edge_send, edge_recv, y_send, y_recv, z_send, z_recv,
     d_send, d_recv, out_send, out_recv, in_sem, table_sem,
@@ -117,12 +117,12 @@
     def greet(device):
         pl.semaphore_signal(barrier, inc=1, device_id=device, device_id_type=MESH)
 
-    for k in range(1, GROUP):
-        greet(date_peer(k))
     for k in range(1, ny):
         greet(y_peer(k))
     for k in range(1, nz):
         greet(z_peer(k))
+    for k in range(1, GROUP):
+        greet(date_peer(k))
 
     @pl.when(d == 0)
     def _():
@@ -233,6 +233,12 @@
     place = (rank & 3) * 32 + owner_row * 4 + (rank >> 2)
     one = jnp.where(iota((128, PAIRS), 0) == place, 1.0, 0.0)
     select[...] = jnp.concatenate([one, one, one], axis=1).astype(BF16)
+    later = iota((PAIRS, PAIRS), 0) > iota((PAIRS, PAIRS), 1)
+    rank_down = jnp.sum(jnp.where(same & later, 1.0, 0.0), axis=1, keepdims=True)
+    quarter = (iota((PAIRS, 128), 1) >> 5).astype(F32)
+    here = jnp.where(owner_down[:, :1] == d.astype(F32), rank_down, -1.0)
+    for g in range(3):
+        own[g] = jnp.where(here == quarter + 4.0 * g, 1.0, 0.0)
 
     def date_rows(which):
         date = pairs_v[which : which + 1, :]
@@ -363,6 +369,7 @@
     take_first(d, sent_0.at[d])
     for k in (4, 3, 5, 2, 6, 1, 7):
         arrive(k)
+    pairs_of(0)
     for copy in z_copies.values():
         copy.wait_recv()
     power = power_z[...]
@@ -371,7 +378,6 @@
     power_d[...] = power
     totals[d] = power
     d_copies = spread(lambda k: power_d, lambda k: totals.at[d], d_send, d_recv, date_peer, GROUP)
-    pairs_of(0)
 
     @pl.when(d == GROUP - 1)
     def _():
@@ -382,17 +388,10 @@
     take_second()
     pairs_of(1)
 
-    for copy in d_copies.values():
-        copy.wait_recv()
-    parts = jnp.concatenate(split3(totals[...].reshape(8 * GROUP, ROWS)), axis=0)
-    total = jnp.sum(dot(hot[...], parts), axis=1, keepdims=True)
-    scale = jnp.sqrt(total / (ROWS * WIDTH * count) + 1e-06)
-    factor = (1.0 / 64.0) / (scale[:PAIRS] * scale[PAIRS:])
-
     wide = []
     for q in range(6):
         piece = looked[q // 3, PAIRS * (q % 3) : PAIRS * (q % 3 + 1)]
-        wide.append(piece * (factor if q % 3 < 2 else 1.0 / 64.0))
+        wide.append(piece if q % 3 < 2 else piece * (1.0 / 64.0))
     stacked = jnp.concatenate(split3(jnp.concatenate(wide, axis=1)), axis=0)
     placed = dot(select[...], stacked)
     lane = iota((32, 128), 1)
@@ -410,23 +409,37 @@
         lambda k: results.at[(d + k) % GROUP], lambda k: landed.at[d], out_send, out_recv, date_peer, GROUP
     )
     landed[d] = results[d]
+
+    for copy in d_copies.values():
+        copy.wait_recv()
+    parts = jnp.concatenate(split3(totals[...].reshape(8 * GROUP, ROWS)), axis=0)
+    total = jnp.sum(dot(hot[...], parts), axis=1, keepdims=True)
+    scale = jnp.sqrt(total / (ROWS * WIDTH * count) + 1e-06)
+    factor = (1.0 / 64.0) / (scale[:PAIRS] * scale[PAIRS:])
+    factors = [jnp.sum(own[g] * factor, axis=0, keepdims=True) for g in range(3)]
+
     for copy in out_copies.values():
         copy.wait_recv()
-    flat = landed.reshape(GROUP * 24, 128)
+    scaling[...] = jnp.concatenate(factors + [jnp.zeros((5, 128), F32)], axis=0)
+    for copies in (y_copies, z_copies, d_copies, main_0, main_1, out_copies):
+        for copy in copies.values():
+            copy.wait_send()
+    for copy in edge_copies:
+        copy.wait_send()
+
+
+def place_kernel(landed, scaling, interferogram, coherence):
     for f in range(3):
         for g in range(3):
-            block = flat[pl.ds(f * 4 + g, 16, stride=12), :]
+            block = landed[pl.ds(f * 4 + g, 16, stride=12), :]
+            if f < 2:
+                block = block * scaling[g : g + 1, :]
             for j in range(4):
                 piece = block[:, 32 * j : 32 * j + 32]
                 if f < 2:
                     interferogram[f, 4 * g + j] = piece
                 else:
                     coherence[4 * g + j] = piece
-    for copies in (y_copies, z_copies, d_copies, main_0, main_1, out_copies):
-        for copy in copies.values():
-            copy.wait_send()
-    for copy in edge_copies:
-        copy.wait_send()
 
 
 def solution(mesh):
@@ -439,18 +452,18 @@
     def local(slc, pairs, owner):
         pairs = pairs.T
         owner = owner.reshape(1, PAIRS)
-        interferogram, coherence = pl.pallas_call(
+        landed, scaling = pl.pallas_call(
             lambda *refs: kernel(ny, nz, *refs),
-            out_shape=(jax.ShapeDtypeStruct((2, CAP, 16, 32), F32), jax.ShapeDtypeStruct((CAP, 16, 32), F32)),
+            out_shape=(jax.ShapeDtypeStruct((GROUP, 24, 128), F32), jax.ShapeDtypeStruct((8, 128), F32)),
             in_specs=[pl.BlockSpec(memory_space=pl.ANY)] * 3,
             out_specs=(vmem, vmem),
             scratch_shapes=[
-                pltpu.VMEM((GROUP, 24, 128), F32),
                 pltpu.VMEM((2, EACH, ROWS, WIDTH), BF16),
                 pltpu.SMEM((2, PAIRS), jnp.int32),
                 pltpu.VMEM((2, PAIRS), jnp.int32),
                 pltpu.VMEM((1, PAIRS), jnp.int32),
                 pltpu.VMEM((128, 3 * PAIRS), BF16),
+                pltpu.VMEM((3, PAIRS, 128), F32),
                 pltpu.VMEM((3 * ROWS, 128), BF16),
                 pltpu.VMEM((2 * PAIRS, 24 * GROUP), BF16),
                 pltpu.VMEM((2 * ROWS, 2 * ROWS), BF16),
@@ -487,6 +500,16 @@
                 collective_id=0, has_side_effects=True, vmem_limit_bytes=54682 * 1024
             ),
         )(slc, pairs, owner)
+        interferogram, coherence = pl.pallas_call(
+            place_kernel,
+            out_shape=(
+                jax.ShapeDtypeStruct((2, CAP, 16, 32), F32),
+                jax.ShapeDtypeStruct((CAP, 16, 32), F32),
+            ),
+            in_specs=[vmem, vmem],
+            out_specs=(vmem, vmem),
+            compiler_params=pltpu.CompilerParams(vmem_limit_bytes=2 * 1024 * 1024),
+        )(landed.reshape(GROUP * 24, 128), scaling)
         return jnp.swapaxes(interferogram, 2, 3), jnp.swapaxes(coherence, 1, 2)
 
     return jax.shard_map(

time: 36.8 us -> 34.7 us (0.943)
  local copies, waits for them, and re-layouts: 1.99 us -> 0.67 us
  Pallas kernels: 34 us -> 33.2 us
    pallas_call x1, Pallas kernels: 34 us -> 32.4 us  [local(): pl.pallas_call(lambda *refs: kernel(ny, nz, *refs), out_shape=(jax.ShapeD...]
    unnamed x6 -> x4, local copies, waits for them, and re-layouts: 1.99 us -> 0.67 us
    pallas_call x0 -> x1, Pallas kernels: none -> 0.81 us  [local(): pl.pallas_call(place_kernel, out_shape=(jax.ShapeDtypeStruct((2, CAP, 16,...]
where the time goes in v4:
time: 34.7 us; the launch traced here: 34.5 us
  Pallas kernels  33.2 us (96%)
  local copies, waits for them, and re-layouts  0.67 us (2%)
  between operations  0.65 us (2%)
    pallas_call x1, Pallas kernels, local(): pl.pallas_call(lambda *refs: kernel(ny, nz, *refs), out_shape=(jax.ShapeD...  32.4 us
    pallas_call x1, Pallas kernels, local(): pl.pallas_call(place_kernel, out_shape=(jax.ShapeDtypeStruct((2, CAP, 16,...  0.81 us

profile of v4, /device:TPU:1, one launch (start us, length us, event | category | flops | bytes accessed | tf_op | source)
XLA Modules:
  0.0 34.5 jit_solution(15187002866604693768)
XLA Ops:
  0.6 0.0 copy-start
  0.6 0.0 copy-start.1
  0.6 0.7 %copy-done = s32[64,2]{0,1:T(2,128)S(1)} copy-done((s32[64,2]{0,1:T(2,128)S(1)}, s32[64,2]{0,1:T(2,128)}, u32[]{:S(2)}) %copy-start) | copy-done | bytes 536
  1.3 0.0 copy-done.1
  1.3 32.4 %shard_map.50 = (f32[8,24,128]{2,1,0:T(8,128)S(1)}, f32[8,128]{1,0:T(8,128)S(1)}) custom-call(bf16[2,4,128,256]{3,2,1,0:T(8,128)(2,1)} %refs_0_.1, s32[2,64]{1,0:T(2,128)S(1)} %bitcast.6, s32[1,64]{1,0:T(1,128)S(1)} %bitcast.7), custom_call_target="tpu_custom_call" | custom-call | tf_op jit(solution)/shard_map/pallas_call | solution.py:455
  33.7 0.8 %shard_map.51 = (f32[2,12,16,32]{3,2,1,0:T(8,128)}, f32[12,16,32]{2,1,0:T(8,128)}) custom-call(f32[192,128]{1,0:T(8,128)S(1)} %bitcast.5, f32[8,128]{1,0:T(8,128)S(1)} %get-tuple-element.7.scaling), custom_call_target="tpu_custom_call" | custom-call | tf_op jit(solution)/shard_map/pallas_call | solution.py:503
Async XLA Ops:
  0.6 0.7 %copy-start = (s32[64,2]{0,1:T(2,128)S(1)}, s32[64,2]{0,1:T(2,128)}, u32[]{:S(2)}) copy-start(s32[64,2]{0,1:T(2,128)} %param.4) | copy-start | bytes 1540
  0.6 0.7 %copy-start.1 = (s32[64]{0:T(128)S(1)}, s32[64]{0:T(128)}, u32[]{:S(2)}) copy-start(s32[64]{0:T(128)} %param.5) | copy-start | bytes 772

commit v5 on v4

--- a/solution.py
+++ b/solution.py
@@ -82,29 +82,26 @@
 
 
 def kernel(
-    ny, nz, slc_hbm, pairs_hbm, owner_hbm, landed, scaling,
-       slc, pairs_s, pairs_v, owner_v, select, own, look, hot, smoother, sent_0, sent_1, got_0, got_1, edge_out, edge_left, edge_right, images, roots, fields, lhs, sums,
-    looked, power_y, power_z, power_d, power_y_in, power_z_in, totals, results,
-    main_send_0, main_recv_0, main_send_1, main_recv_1, edge_send, edge_recv, y_send, y_recv, z_send, z_recv,
-    d_send, d_recv, out_send, out_recv, in_sem, table_sem,
+    nz, count, slc_hbm, pairs_hbm, owner_hbm, landed, scaling,
+    slc, pairs_s, pairs_v, owner_v, select, own, look, hot, smoother, sent_0, sent_1, got_0, got_1,
+    edge_out, edge_left, edge_right, images, roots, fields, lhs, sums, looked,
+    power_up, power_in, power_d, totals, factor_out, factor_in, results,
+    main_send_0, main_recv_0, main_send_1, main_recv_1, edge_send, edge_recv, ready,
+    up_send, up_recv, down_send, down_recv, d_send, d_recv, out_send, out_recv, in_sem, table_sem,
 ):
     d = lax.axis_index("dates")
     c = lax.axis_index("cols")
-    count = ny * nz
-    y = c // nz
     z = c % nz
 
     def date_peer(k):
         return {"dates": (d + k) % GROUP, "cols": c}
 
-    def y_peer(k):
-        return {"dates": d, "cols": ((y + k) % ny) * nz + z}
-
-    def z_peer(k):
-        return {"dates": d, "cols": y * nz + (z + k) % nz}
-
-    after = (c + 1) % count
-    before = (c + count - 1) % count
+    right = (c + 1) % count
+    left = (c + count - 1) % count
+    right_later = (z < nz - 1) & (c < count - 1)
+    right_earlier = (z == nz - 1) & (c < count - 1)
+    left_later = (z == 0) & (c > 0)
+    left_earlier = (z > 0) & (c > 0)
 
     loads = [
         pltpu.make_async_copy(slc_hbm.at[:, t], slc.at[:, t], in_sem.at[t]) for t in range(EACH)
@@ -117,22 +114,29 @@
     def greet(device):
         pl.semaphore_signal(barrier, inc=1, device_id=device, device_id_type=MESH)
 
-    for k in range(1, ny):
-        greet(y_peer(k))
-    for k in range(1, nz):
-        greet(z_peer(k))
     for k in range(1, GROUP):
         greet(date_peer(k))
 
-    @pl.when(d == 0)
-    def _():
-        for e in range(GROUP):
-            greet({"dates": e, "cols": before})
-
-    @pl.when(d == GROUP - 1)
-    def _():
-        for e in range(GROUP):
-            greet({"dates": e, "cols": after})
+    def greet_neighbour(later, receiver, other):
+        @pl.when(later)
+        def _():
+            greet({"dates": receiver, "cols": other})
+
+        @pl.when(later & (d == GROUP - 1 - receiver))
+        def _():
+            for e in range(GROUP):
+                greet({"dates": e, "cols": other})
+
+    greet_neighbour(right_later, 0, right)
+    greet_neighbour(left_later, GROUP - 1, left)
+
+    @pl.when(c == 0)
+    def _():
+        def one(i, carry):
+            greet({"dates": d, "cols": i})
+            return carry
+
+        lax.fori_loop(1, count, one, 0)
 
     tables = [
         pltpu.make_async_copy(pairs_hbm, pairs_s, table_sem.at[0]),
@@ -150,8 +154,6 @@
         size = PIECES[half]
         matrix = cutter(half)
         for t in range(EACH):
-            if half == 0:
-                loads[t].wait()
             both = jnp.concatenate([slc[0, t], slc[1, t]], axis=0)
             turned = lax.dot_general(
                 matrix, both, (((1,), (1,)), ((), ())), preferred_element_type=F32
@@ -164,9 +166,30 @@
                 else:
                     edge_out[half, 16 * t : 16 * (t + 1), :] = value
 
+    for load in loads:
+        load.wait()
     cut(0)
 
-    pl.semaphore_wait(barrier, (GROUP - 1) + (ny - 1) + (nz - 1) + 2)
+    first = (d == 0).astype(jnp.int32)
+    last = (d == GROUP - 1).astype(jnp.int32)
+    pl.semaphore_wait(
+        barrier,
+        (GROUP - 1)
+        + (c > 0).astype(jnp.int32)
+        + right_earlier.astype(jnp.int32) * (1 + GROUP * last)
+        + left_earlier.astype(jnp.int32) * (1 + GROUP * first),
+    )
+
+    def tell_ready(side, condition, other):
+        @pl.when(condition)
+        def _():
+            for e in range(GROUP):
+                pl.semaphore_signal(
+                    ready.at[side], inc=1, device_id={"dates": e, "cols": other}, device_id_type=MESH
+                )
+
+    tell_ready(0, left_earlier & (d == 0), left)
+    tell_ready(1, right_earlier & (d == GROUP - 1), right)
 
     def spread(src, dst, send, recv, peer, number):
         copies = {}
@@ -179,15 +202,13 @@
             copies[k] = copy
         return copies
 
-    edge_copies = []
-
-    def send_edge(side, device):
-        copy = pltpu.make_async_remote_copy(
+    targets = ({"dates": 0, "cols": right}, {"dates": GROUP - 1, "cols": left})
+
+    def edge_copy(side):
+        return pltpu.make_async_remote_copy(
             src_ref=edge_out.at[side], dst_ref=edge_in[side].at[d], send_sem=edge_send.at[side],
-            recv_sem=edge_recv.at[d], device_id=device, device_id_type=MESH,
+            recv_sem=edge_recv.at[GROUP * side + d], device_id=targets[side], device_id_type=MESH,
         )
-        copy.start()
-        edge_copies.append(copy)
 
     def send_half(half, send, recv):
         return spread(
@@ -195,25 +216,49 @@
             date_peer, GROUP,
         )
 
-    send_edge(0, {"dates": 0, "cols": after})
     main_0 = send_half(0, main_send_0, main_recv_0)
+
+    @pl.when(right_earlier)
+    def _():
+        edge_copy(0).start()
+
     power_rows = []
     for t in range(EACH):
         wide = jnp.concatenate([slc[0, t], slc[1, t]], axis=0).astype(F32)
         square = jnp.sum(wide * wide, axis=0, keepdims=True)
         power_rows.append(square[:, :ROWS] + square[:, ROWS:])
-    power_y[...] = jnp.concatenate(power_rows + [jnp.zeros((8 - EACH, ROWS), F32)], axis=0)
-    y_copies = spread(lambda k: power_y, lambda k: power_y_in.at[k - 1], y_send, y_recv, y_peer, ny)
+    power_up[...] = jnp.concatenate(power_rows + [jnp.zeros((8 - EACH, ROWS), F32)], axis=0)
+
+    def up_copy(i):
+        return pltpu.make_async_remote_copy(
+            src_ref=power_up, dst_ref=power_in.at[i], send_sem=up_send.at[0], recv_sem=up_recv.at[i],
+            device_id={"dates": d, "cols": 0}, device_id_type=MESH,
+        )
+
+    def down_copy(i):
+        return pltpu.make_async_remote_copy(
+            src_ref=factor_out, dst_ref=factor_in, send_sem=down_send.at[i], recv_sem=down_recv.at[0],
+            device_id={"dates": d, "cols": i}, device_id_type=MESH,
+        )
+
+    @pl.when(c > 0)
+    def _():
+        up_copy(c).start()
+
     cut(1)
-    send_edge(1, {"dates": GROUP - 1, "cols": before})
     main_1 = send_half(1, main_send_1, main_recv_1)
+
+    @pl.when(left_earlier)
+    def _():
+        edge_copy(1).start()
+
     got_1[d] = sent_1[d]
 
-    @pl.when(d != 0)
+    @pl.when((d != 0) | (c == 0))
     def _():
         edge_left[...] = jnp.zeros_like(edge_left)
 
-    @pl.when(d != GROUP - 1)
+    @pl.when((d != GROUP - 1) | (c == count - 1))
     def _():
         edge_right[...] = jnp.zeros_like(edge_right)
 
@@ -256,11 +301,8 @@
         for e in range(GROUP):
             pltpu.make_async_remote_copy(
                 src_ref=edge_out.at[side], dst_ref=edge_in[side].at[e], send_sem=edge_send.at[side],
-                recv_sem=edge_recv.at[e], device_id=date_peer(1), device_id_type=MESH,
+                recv_sem=edge_recv.at[GROUP * side + e], device_id=targets[side], device_id_type=MESH,
             ).wait_recv()
-
-    left_gate = jnp.where(c > 0, 1.0, 0.0).astype(F32)
-    right_gate = jnp.where(c < count - 1, 1.0, 0.0).astype(F32)
 
     def smooth_powers(number):
         for t in range(number):
@@ -274,7 +316,7 @@
         size = PIECES[0]
         for t in range(EACH):
             piece = block[2 * size * t : 2 * size * (t + 1), :].astype(F32)
-            edge = edge_left[source, 16 * t : 16 * (t + 1), :].astype(F32) * left_gate
+            edge = edge_left[source, 16 * t : 16 * (t + 1), :].astype(F32)
             real = jnp.concatenate([piece[:8] + edge[:8], piece[8:size]], axis=0)
             imag = jnp.concatenate([piece[size : size + 8] + edge[8:], piece[size + 8 :]], axis=0)
             images[source * EACH + t, 0, :size] = real
@@ -294,7 +336,7 @@
         for date in range(DATES):
             source, t = date // EACH, date % EACH
             piece = got_1[source, 2 * size * t : 2 * size * (t + 1), :].astype(F32)
-            edge = edge_right[source, 16 * t : 16 * (t + 1), :].astype(F32) * right_gate
+            edge = edge_right[source, 16 * t : 16 * (t + 1), :].astype(F32)
             real = jnp.concatenate([piece[:8], piece[8:size] + edge[:8]], axis=0)
             imag = jnp.concatenate([piece[size : size + 8], piece[size + 8 :] + edge[8:]], axis=0)
             images[date, 0, PIECES[0] :] = real
@@ -354,15 +396,17 @@
             rows = rows + sums[pl.ds(3 * half * PAIRS * 8 + i, 3 * PAIRS, stride=8), :]
         looked[half] = dot(jnp.concatenate(split3(rows), axis=1), look[...])
 
-    for copy in y_copies.values():
-        copy.wait_recv()
-    power = power_y[...]
-    for k in range(1, ny):
-        power = power + power_y_in[k - 1]
-    power_z[...] = power
-    z_copies = spread(lambda k: power_z, lambda k: power_z_in.at[k - 1], z_send, z_recv, z_peer, nz)
-
-    @pl.when(d == 0)
+    @pl.when(right_later)
+    def _():
+        pl.semaphore_wait(ready.at[0], 1)
+        edge_copy(0).start()
+
+    @pl.when(left_later)
+    def _():
+        pl.semaphore_wait(ready.at[1], 1)
+        edge_copy(1).start()
+
+    @pl.when((d == 0) & (c > 0))
     def _():
         edges(0)
 
@@ -370,16 +414,27 @@
     for k in (4, 3, 5, 2, 6, 1, 7):
         arrive(k)
     pairs_of(0)
-    for copy in z_copies.values():
-        copy.wait_recv()
-    power = power_z[...]
-    for k in range(1, nz):
-        power = power + power_z_in[k - 1]
-    power_d[...] = power
-    totals[d] = power
-    d_copies = spread(lambda k: power_d, lambda k: totals.at[d], d_send, d_recv, date_peer, GROUP)
-
-    @pl.when(d == GROUP - 1)
+
+    def d_copy(k):
+        return pltpu.make_async_remote_copy(
+            src_ref=power_d, dst_ref=totals.at[d], send_sem=d_send.at[k - 1], recv_sem=d_recv.at[k - 1],
+            device_id=date_peer(k), device_id_type=MESH,
+        )
+
+    @pl.when(c == 0)
+    def _():
+        def one(i, carry):
+            up_copy(i).wait_recv()
+            return carry
+
+        lax.fori_loop(1, count, one, 0)
+        power = power_up[...] + jnp.sum(power_in[1:count], axis=0)
+        power_d[...] = power
+        totals[d] = power
+        for k in range(1, GROUP):
+            d_copy(k).start()
+
+    @pl.when((d == GROUP - 1) & (c < count - 1))
     def _():
         edges(1)
 
@@ -410,22 +465,60 @@
     )
     landed[d] = results[d]
 
-    for copy in d_copies.values():
-        copy.wait_recv()
-    parts = jnp.concatenate(split3(totals[...].reshape(8 * GROUP, ROWS)), axis=0)
-    total = jnp.sum(dot(hot[...], parts), axis=1, keepdims=True)
-    scale = jnp.sqrt(total / (ROWS * WIDTH * count) + 1e-06)
-    factor = (1.0 / 64.0) / (scale[:PAIRS] * scale[PAIRS:])
+    @pl.when(c == 0)
+    def _():
+        for k in range(1, GROUP):
+            d_copy(k).wait_recv()
+        parts = jnp.concatenate(split3(totals[...].reshape(8 * GROUP, ROWS)), axis=0)
+        total = jnp.sum(dot(hot[...], parts), axis=1, keepdims=True)
+        scale = jnp.sqrt(total / (ROWS * WIDTH * count) + 1e-06)
+        factor = (1.0 / 64.0) / (scale[:PAIRS] * scale[PAIRS:])
+        factor = jnp.broadcast_to(jnp.concatenate([factor, factor], axis=0), (ROWS, ROWS))
+        factor = jnp.transpose(factor)[:8]
+        factor_out[...] = factor
+        factor_in[...] = factor
+
+        def one(i, carry):
+            down_copy((i % (count // nz)) * nz + i // (count // nz)).start()
+            return carry
+
+        lax.fori_loop(1, count, one, 0)
+
+    @pl.when(c > 0)
+    def _():
+        down_copy(0).wait_recv()
+
+    factor = jnp.transpose(jnp.broadcast_to(factor_in[0:1, :PAIRS], (ROWS, PAIRS)))
     factors = [jnp.sum(own[g] * factor, axis=0, keepdims=True) for g in range(3)]
-
     for copy in out_copies.values():
         copy.wait_recv()
     scaling[...] = jnp.concatenate(factors + [jnp.zeros((5, 128), F32)], axis=0)
-    for copies in (y_copies, z_copies, d_copies, main_0, main_1, out_copies):
+    for copies in (main_0, main_1, out_copies):
         for copy in copies.values():
             copy.wait_send()
-    for copy in edge_copies:
-        copy.wait_send()
+
+    @pl.when(right_later | right_earlier)
+    def _():
+        edge_copy(0).wait_send()
+
+    @pl.when(left_later | left_earlier)
+    def _():
+        edge_copy(1).wait_send()
+
+    @pl.when(c > 0)
+    def _():
+        up_copy(c).wait_send()
+
+    @pl.when(c == 0)
+    def _():
+        for k in range(1, GROUP):
+            d_copy(k).wait_send()
+
+        def one(i, carry):
+            down_copy(i).wait_send()
+            return carry
+
+        lax.fori_loop(1, count, one, 0)
 
 
 def place_kernel(landed, scaling, interferogram, coherence):
@@ -444,8 +537,7 @@
 
 def solution(mesh):
     columns = mesh.shape["cols"]
-    nz = 8 if columns % 8 == 0 else columns
-    ny = columns // nz
+    nz = 8 if columns % 8 == 0 else 2
     sem = pltpu.SemaphoreType.DMA
     vmem = pl.BlockSpec(memory_space=pltpu.VMEM)
 
@@ -453,7 +545,7 @@
         pairs = pairs.T
         owner = owner.reshape(1, PAIRS)
         landed, scaling = pl.pallas_call(
-            lambda *refs: kernel(ny, nz, *refs),
+            lambda *refs: kernel(nz, columns, *refs),
             out_shape=(jax.ShapeDtypeStruct((GROUP, 24, 128), F32), jax.ShapeDtypeStruct((8, 128), F32)),
             in_specs=[pl.BlockSpec(memory_space=pl.ANY)] * 3,
             out_specs=(vmem, vmem),
@@ -481,17 +573,16 @@
                 pltpu.VMEM((6 * PAIRS * 8, ROWS), F32),
                 pltpu.VMEM((2, 3 * PAIRS, ROWS), F32),
                 pltpu.VMEM((8, ROWS), F32),
+                pltpu.VMEM((columns, 8, ROWS), F32),
+                pltpu.VMEM((8, ROWS), F32),
+                pltpu.VMEM((GROUP, 8, ROWS), F32),
                 pltpu.VMEM((8, ROWS), F32),
                 pltpu.VMEM((8, ROWS), F32),
-                pltpu.VMEM((max(ny - 1, 1), 8, ROWS), F32),
-                pltpu.VMEM((max(nz - 1, 1), 8, ROWS), F32),
-                pltpu.VMEM((GROUP, 8, ROWS), F32),
                 pltpu.VMEM((GROUP, 24, 128), F32),
                 sem((GROUP - 1,)), sem((GROUP - 1,)),
                 sem((GROUP - 1,)), sem((GROUP - 1,)),
-                sem((2,)), sem((GROUP,)),
-                sem((max(ny - 1, 1),)), sem((max(ny - 1, 1),)),
-                sem((max(nz - 1, 1),)), sem((max(nz - 1, 1),)),
+                sem((2,)), sem((2 * GROUP,)), pltpu.SemaphoreType.REGULAR((2,)),
+                sem((1,)), sem((columns,)), sem((columns,)), sem((1,)),
                 sem((GROUP - 1,)), sem((GROUP - 1,)),
                 sem((GROUP - 1,)), sem((GROUP - 1,)),
                 sem((EACH,)), sem((3,)),

time: 34.7 us -> 31.7 us (0.914)
  Pallas kernels: 33.2 us -> 30.2 us
    pallas_call x1, Pallas kernels: 32.4 us -> 29.4 us  [local(): pl.pallas_call(lambda *refs: kernel(nz, columns, *refs), out_shape=(jax.S...]
where the time goes in v5:
time: 31.7 us; the launch traced here: 31.6 us
  Pallas kernels  30.2 us (95%)
  local copies, waits for them, and re-layouts  0.67 us (2%)
  between operations  0.65 us (2%)
    pallas_call x1, Pallas kernels, local(): pl.pallas_call(lambda *refs: kernel(nz, columns, *refs), out_shape=(jax.S...  29.4 us
    pallas_call x1, Pallas kernels, local(): pl.pallas_call(place_kernel, out_shape=(jax.ShapeDtypeStruct((2, CAP, 16,...  0.81 us
    unnamed x4, local copies, waits for them, and re-layouts  0.67 us

profile of v5, /device:TPU:1, one launch (start us, length us, event | category | flops | bytes accessed | tf_op | source)
XLA Modules:
  0.0 31.6 jit_solution(1730777688750394498)
XLA Ops:
  0.6 0.0 copy-start
  0.6 0.0 copy-start.1
  0.6 0.7 %copy-done = s32[64,2]{0,1:T(2,128)S(1)} copy-done((s32[64,2]{0,1:T(2,128)S(1)}, s32[64,2]{0,1:T(2,128)}, u32[]{:S(2)}) %copy-start) | copy-done | bytes 536
  1.3 0.0 copy-done.1
  1.3 29.4 %shard_map.50 = (f32[8,24,128]{2,1,0:T(8,128)S(1)}, f32[8,128]{1,0:T(8,128)S(1)}) custom-call(bf16[2,4,128,256]{3,2,1,0:T(8,128)(2,1)} %refs_0_.1, s32[2,64]{1,0:T(2,128)S(1)} %bitcast.6, s32[1,64]{1,0:T(1,128)S(1)} %bitcast.7), custom_call_target="tpu_custom_call" | custom-call | tf_op jit(solution)/shard_map/pallas_call | solution.py:547
  30.8 0.8 %shard_map.51 = (f32[2,12,16,32]{3,2,1,0:T(8,128)}, f32[12,16,32]{2,1,0:T(8,128)}) custom-call(f32[192,128]{1,0:T(8,128)S(1)} %bitcast.5, f32[8,128]{1,0:T(8,128)S(1)} %get-tuple-element.7.scaling), custom_call_target="tpu_custom_call" | custom-call | tf_op jit(solution)/shard_map/pallas_call | solution.py:594
Async XLA Ops:
  0.6 0.7 %copy-start = (s32[64,2]{0,1:T(2,128)S(1)}, s32[64,2]{0,1:T(2,128)}, u32[]{:S(2)}) copy-start(s32[64,2]{0,1:T(2,128)} %param.4) | copy-start | bytes 1540
  0.6 0.7 %copy-start.1 = (s32[64]{0:T(128)S(1)}, s32[64]{0:T(128)}, u32[]{:S(2)}) copy-start(s32[64]{0:T(128)} %param.5) | copy-start | bytes 772

commit v6 on v5

--- a/solution.py
+++ b/solution.py
@@ -85,9 +85,9 @@
     nz, count, slc_hbm, pairs_hbm, owner_hbm, landed, scaling,
     slc, pairs_s, pairs_v, owner_v, select, own, look, hot, smoother, sent_0, sent_1, got_0, got_1,
     edge_out, edge_left, edge_right, images, roots, fields, lhs, sums, looked,
-    power_up, power_in, power_d, totals, factor_out, factor_in, results,
+    power_in, totals, factor_in, results,
     main_send_0, main_recv_0, main_send_1, main_recv_1, edge_send, edge_recv, ready,
-    up_send, up_recv, down_send, down_recv, d_send, d_recv, out_send, out_recv, in_sem, table_sem,
+    here, up_send, up_recv, down_send, down_recv, d_send, d_recv, out_send, out_recv, in_sem, table_sem,
 ):
     d = lax.axis_index("dates")
     c = lax.axis_index("cols")
@@ -98,16 +98,14 @@
 
     right = (c + 1) % count
     left = (c + count - 1) % count
+    near = min(2, nz)
     right_later = (z < nz - 1) & (c < count - 1)
     right_earlier = (z == nz - 1) & (c < count - 1)
     left_later = (z == 0) & (c > 0)
     left_earlier = (z > 0) & (c > 0)
 
-    loads = [
-        pltpu.make_async_copy(slc_hbm.at[:, t], slc.at[:, t], in_sem.at[t]) for t in range(EACH)
-    ]
-    for load in loads:
-        load.start()
+    load = pltpu.make_async_copy(slc_hbm, slc, in_sem.at[0])
+    load.start()
 
     barrier = pltpu.get_barrier_semaphore()
 
@@ -137,6 +135,14 @@
             return carry
 
         lax.fori_loop(1, count, one, 0)
+
+    hands_on = (z == 0) & (c > 0)
+    handed = (z >= near) & (c >= nz)
+
+    @pl.when(hands_on)
+    def _():
+        for i in range(near, nz):
+            greet({"dates": d, "cols": c - z + i})
 
     tables = [
         pltpu.make_async_copy(pairs_hbm, pairs_s, table_sem.at[0]),
@@ -150,9 +156,8 @@
     edge_in = (edge_left, edge_right)
     got = (got_0, got_1)
 
-    def cut(half):
+    def cut(half, matrix):
         size = PIECES[half]
-        matrix = cutter(half)
         for t in range(EACH):
             both = jnp.concatenate([slc[0, t], slc[1, t]], axis=0)
             turned = lax.dot_general(
@@ -166,9 +171,19 @@
                 else:
                     edge_out[half, 16 * t : 16 * (t + 1), :] = value
 
-    for load in loads:
-        load.wait()
-    cut(0)
+    matrix = cutter(0)
+    high = band(HIGH)
+    low = band(LOW)
+    smoother[:, :ROWS] = jnp.concatenate([high, high], axis=0)
+    smoother[:, ROWS:] = jnp.concatenate([low, low], axis=0)
+    load.wait()
+    power_rows = []
+    for t in range(EACH):
+        wide = jnp.concatenate([slc[0, t], slc[1, t]], axis=0).astype(F32)
+        square = jnp.sum(wide * wide, axis=0, keepdims=True)
+        power_rows.append(square[:, :ROWS] + square[:, ROWS:])
+    power_in[0] = jnp.concatenate(power_rows + [jnp.zeros((8 - EACH, ROWS), F32)], axis=0)
+    cut(0, matrix)
 
     first = (d == 0).astype(jnp.int32)
     last = (d == GROUP - 1).astype(jnp.int32)
@@ -176,6 +191,7 @@
         barrier,
         (GROUP - 1)
         + (c > 0).astype(jnp.int32)
+        + handed.astype(jnp.int32)
         + right_earlier.astype(jnp.int32) * (1 + GROUP * last)
         + left_earlier.astype(jnp.int32) * (1 + GROUP * first),
     )
@@ -188,65 +204,68 @@
                     ready.at[side], inc=1, device_id={"dates": e, "cols": other}, device_id_type=MESH
                 )
 
+    @pl.when(handed)
+    def _():
+        pl.semaphore_signal(
+            here, inc=1, device_id={"dates": d, "cols": c - z}, device_id_type=MESH
+        )
+
     tell_ready(0, left_earlier & (d == 0), left)
     tell_ready(1, right_earlier & (d == GROUP - 1), right)
 
-    def spread(src, dst, send, recv, peer, number):
-        copies = {}
-        for k in sorted(range(1, number), key=lambda k: -min(k, number - k)):
-            copy = pltpu.make_async_remote_copy(
-                src_ref=src(k), dst_ref=dst(k), send_sem=send.at[k - 1], recv_sem=recv.at[k - 1],
-                device_id=peer(k), device_id_type=MESH,
-            )
-            copy.start()
-            copies[k] = copy
-        return copies
+    def stage(src, dst, send, recv, peer):
+        return pltpu.make_async_remote_copy(
+            src_ref=src, dst_ref=dst, send_sem=send, recv_sem=recv, device_id=peer, device_id_type=MESH
+        )
+
+    def up_copy(i, size=1):
+        return stage(
+            power_in.at[pl.ds(0, size)], power_in.at[pl.ds(i, size)], up_send.at[0], up_recv.at[0],
+            {"dates": d, "cols": 0},
+        )
+
+    def down_copy(i):
+        return stage(factor_in, factor_in, down_send.at[0], down_recv.at[0], {"dates": d, "cols": i})
+
+    @pl.when(c > 0)
+    def _():
+        up_copy(c).start()
 
     targets = ({"dates": 0, "cols": right}, {"dates": GROUP - 1, "cols": left})
 
     def edge_copy(side):
         return pltpu.make_async_remote_copy(
             src_ref=edge_out.at[side], dst_ref=edge_in[side].at[d], send_sem=edge_send.at[side],
-            recv_sem=edge_recv.at[GROUP * side + d], device_id=targets[side], device_id_type=MESH,
-        )
-
-    def send_half(half, send, recv):
-        return spread(
-            lambda k: sent[half].at[(d + k) % GROUP], lambda k: got[half].at[d], send, recv,
-            date_peer, GROUP,
-        )
-
-    main_0 = send_half(0, main_send_0, main_recv_0)
+            recv_sem=edge_recv.at[0], device_id=targets[side], device_id_type=MESH,
+        )
+
+    order = (4, 3, 5, 2, 6, 1, 7)
+    slots = {4: 0, 3: 1, 5: 2}
+
+    def first_copy(k, size=1):
+        return stage(
+            sent_0.at[pl.ds((d + k) % GROUP if size == 1 else 0, size)],
+            got_0.at[pl.ds(d if size == 1 else 0, size)],
+            main_send_0.at[0], main_recv_0.at[slots.get(k, 3)], date_peer(k),
+        )
+
+    def second_copy(k, size=1):
+        return stage(
+            sent_1.at[pl.ds((d + k) % GROUP if size == 1 else 0, size)],
+            got_1.at[pl.ds(d if size == 1 else 0, size)],
+            main_send_1.at[0], main_recv_1.at[0], date_peer(k),
+        )
+
+    for k in order:
+        first_copy(k).start()
 
     @pl.when(right_earlier)
     def _():
         edge_copy(0).start()
 
-    power_rows = []
-    for t in range(EACH):
-        wide = jnp.concatenate([slc[0, t], slc[1, t]], axis=0).astype(F32)
-        square = jnp.sum(wide * wide, axis=0, keepdims=True)
-        power_rows.append(square[:, :ROWS] + square[:, ROWS:])
-    power_up[...] = jnp.concatenate(power_rows + [jnp.zeros((8 - EACH, ROWS), F32)], axis=0)
-
-    def up_copy(i):
-        return pltpu.make_async_remote_copy(
-            src_ref=power_up, dst_ref=power_in.at[i], send_sem=up_send.at[0], recv_sem=up_recv.at[i],
-            device_id={"dates": d, "cols": 0}, device_id_type=MESH,
-        )
-
-    def down_copy(i):
-        return pltpu.make_async_remote_copy(
-            src_ref=factor_out, dst_ref=factor_in, send_sem=down_send.at[i], recv_sem=down_recv.at[0],
-            device_id={"dates": d, "cols": i}, device_id_type=MESH,
-        )
-
-    @pl.when(c > 0)
-    def _():
-        up_copy(c).start()
-
-    cut(1)
-    main_1 = send_half(1, main_send_1, main_recv_1)
+    cut(1, cutter(1))
+    for k in order:
+        second_copy(k).start()
 
     @pl.when(left_earlier)
     def _():
@@ -262,11 +281,6 @@
     def _():
         edge_right[...] = jnp.zeros_like(edge_right)
 
-
-    high = band(HIGH)
-    low = band(LOW)
-    smoother[:, :ROWS] = jnp.concatenate([high, high], axis=0)
-    smoother[:, ROWS:] = jnp.concatenate([low, low], axis=0)
 
     for table in tables:
         table.wait()
@@ -281,9 +295,9 @@
     later = iota((PAIRS, PAIRS), 0) > iota((PAIRS, PAIRS), 1)
     rank_down = jnp.sum(jnp.where(same & later, 1.0, 0.0), axis=1, keepdims=True)
     quarter = (iota((PAIRS, 128), 1) >> 5).astype(F32)
-    here = jnp.where(owner_down[:, :1] == d.astype(F32), rank_down, -1.0)
+    mine = jnp.where(owner_down[:, :1] == d.astype(F32), rank_down, -1.0)
     for g in range(3):
-        own[g] = jnp.where(here == quarter + 4.0 * g, 1.0, 0.0)
+        own[g] = jnp.where(mine == quarter + 4.0 * g, 1.0, 0.0)
 
     def date_rows(which):
         date = pairs_v[which : which + 1, :]
@@ -298,11 +312,9 @@
     look[...] = jnp.concatenate([one, one, one], axis=0).astype(BF16)
 
     def edges(side):
-        for e in range(GROUP):
-            pltpu.make_async_remote_copy(
-                src_ref=edge_out.at[side], dst_ref=edge_in[side].at[e], send_sem=edge_send.at[side],
-                recv_sem=edge_recv.at[GROUP * side + e], device_id=targets[side], device_id_type=MESH,
-            ).wait_recv()
+        stage(
+            edge_in[side], edge_in[side], edge_send.at[side], edge_recv.at[0], targets[side]
+        ).wait_recv()
 
     def smooth_powers(number):
         for t in range(number):
@@ -312,24 +324,26 @@
         smooth = dot(lhs[: number * HALF, :], smoother[...])
         return jnp.sqrt(smooth[:, :ROWS] + smooth[:, ROWS:])
 
-    def take_first(source, block):
+    def take_first(sources, ref):
         size = PIECES[0]
-        for t in range(EACH):
-            piece = block[2 * size * t : 2 * size * (t + 1), :].astype(F32)
-            edge = edge_left[source, 16 * t : 16 * (t + 1), :].astype(F32)
-            real = jnp.concatenate([piece[:8] + edge[:8], piece[8:size]], axis=0)
-            imag = jnp.concatenate([piece[size : size + 8] + edge[8:], piece[size + 8 :]], axis=0)
-            images[source * EACH + t, 0, :size] = real
-            images[source * EACH + t, 1, :size] = imag
-            fields[t] = real * real + imag * imag
-        smooth = smooth_powers(EACH)
-        for t in range(EACH):
-            roots[source * EACH + t, :HALF] = smooth[HALF * t : HALF * (t + 1)]
-
-    def arrive(k):
-        main_0[k].wait_recv()
-        source = (d + GROUP - k) % GROUP
-        take_first(source, got_0.at[source])
+        for i, source in enumerate(sources):
+            for t in range(EACH):
+                piece = ref[source, 2 * size * t : 2 * size * (t + 1), :].astype(F32)
+                edge = edge_left[source, 16 * t : 16 * (t + 1), :].astype(F32)
+                real = jnp.concatenate([piece[:8] + edge[:8], piece[8:size]], axis=0)
+                imag = jnp.concatenate([piece[size : size + 8] + edge[8:], piece[size + 8 :]], axis=0)
+                images[source * EACH + t, 0, :size] = real
+                images[source * EACH + t, 1, :size] = imag
+                fields[EACH * i + t] = real * real + imag * imag
+        smooth = smooth_powers(EACH * len(sources))
+        for i, source in enumerate(sources):
+            for t in range(EACH):
+                at = HALF * (EACH * i + t)
+                roots[source * EACH + t, :HALF] = smooth[at : at + HALF]
+
+    def arrive(*ks):
+        first_copy(ks[0], len(ks)).wait_recv()
+        take_first([(d + GROUP - k) % GROUP for k in ks], got_0)
 
     def take_second():
         size = PIECES[1]
@@ -410,36 +424,31 @@
     def _():
         edges(0)
 
-    take_first(d, sent_0.at[d])
-    for k in (4, 3, 5, 2, 6, 1, 7):
-        arrive(k)
+    take_first([d], sent_0)
+    arrive(4)
+    arrive(3)
+    arrive(5)
+    arrive(2, 6, 1, 7)
     pairs_of(0)
 
-    def d_copy(k):
-        return pltpu.make_async_remote_copy(
-            src_ref=power_d, dst_ref=totals.at[d], send_sem=d_send.at[k - 1], recv_sem=d_recv.at[k - 1],
-            device_id=date_peer(k), device_id_type=MESH,
+    def d_copy(k, size=1):
+        return stage(
+            totals.at[pl.ds(d if size == 1 else 0, size)], totals.at[pl.ds(d if size == 1 else 0, size)],
+            d_send.at[0], d_recv.at[0], date_peer(k),
         )
 
     @pl.when(c == 0)
     def _():
-        def one(i, carry):
-            up_copy(i).wait_recv()
-            return carry
-
-        lax.fori_loop(1, count, one, 0)
-        power = power_up[...] + jnp.sum(power_in[1:count], axis=0)
-        power_d[...] = power
-        totals[d] = power
-        for k in range(1, GROUP):
+        up_copy(1, count - 1).wait_recv()
+        totals[d] = jnp.sum(power_in[...], axis=0)
+        for k in order:
             d_copy(k).start()
 
     @pl.when((d == GROUP - 1) & (c < count - 1))
     def _():
         edges(1)
 
-    for k in (4, 3, 5, 2, 6, 1, 7):
-        main_1[k].wait_recv()
+    second_copy(1, GROUP - 1).wait_recv()
     take_second()
     pairs_of(1)
 
@@ -460,42 +469,52 @@
         for e in range(GROUP):
             results[e, 4 * q : 4 * q + 4, :] = value[4 * e : 4 * e + 4]
 
-    out_copies = spread(
-        lambda k: results.at[(d + k) % GROUP], lambda k: landed.at[d], out_send, out_recv, date_peer, GROUP
-    )
+    def out_copy(k, size=1):
+        return stage(
+            results.at[pl.ds((d + k) % GROUP if size == 1 else 0, size)],
+            landed.at[pl.ds(d if size == 1 else 0, size)],
+            out_send.at[0], out_recv.at[0], date_peer(k),
+        )
+
+    for k in order:
+        out_copy(k).start()
     landed[d] = results[d]
 
     @pl.when(c == 0)
     def _():
-        for k in range(1, GROUP):
-            d_copy(k).wait_recv()
+        d_copy(1, GROUP - 1).wait_recv()
         parts = jnp.concatenate(split3(totals[...].reshape(8 * GROUP, ROWS)), axis=0)
         total = jnp.sum(dot(hot[...], parts), axis=1, keepdims=True)
         scale = jnp.sqrt(total / (ROWS * WIDTH * count) + 1e-06)
         factor = (1.0 / 64.0) / (scale[:PAIRS] * scale[PAIRS:])
         factor = jnp.broadcast_to(jnp.concatenate([factor, factor], axis=0), (ROWS, ROWS))
         factor = jnp.transpose(factor)[:8]
-        factor_out[...] = factor
         factor_in[...] = factor
-
-        def one(i, carry):
-            down_copy((i % (count // nz)) * nz + i // (count // nz)).start()
-            return carry
-
-        lax.fori_loop(1, count, one, 0)
+        for i in range(near):
+            for j in range(count // nz):
+                if i + j > 0:
+                    down_copy(j * nz + i).start()
+        for i in range(near, nz):
+            down_copy(i).start()
 
     @pl.when(c > 0)
     def _():
         down_copy(0).wait_recv()
+
+    @pl.when(hands_on)
+    def _():
+        if nz > near:
+            pl.semaphore_wait(here, nz - near)
+        for i in range(near, nz):
+            down_copy(c - z + i).start()
 
     factor = jnp.transpose(jnp.broadcast_to(factor_in[0:1, :PAIRS], (ROWS, PAIRS)))
     factors = [jnp.sum(own[g] * factor, axis=0, keepdims=True) for g in range(3)]
-    for copy in out_copies.values():
-        copy.wait_recv()
+    out_copy(1, GROUP - 1).wait_recv()
     scaling[...] = jnp.concatenate(factors + [jnp.zeros((5, 128), F32)], axis=0)
-    for copies in (main_0, main_1, out_copies):
-        for copy in copies.values():
-            copy.wait_send()
+    first_copy(1, GROUP - 1).wait_send()
+    second_copy(1, GROUP - 1).wait_send()
+    out_copy(1, GROUP - 1).wait_send()
 
     @pl.when(right_later | right_earlier)
     def _():
@@ -505,20 +524,26 @@
     def _():
         edge_copy(1).wait_send()
 
+    def sent_down(number):
+        stage(
+            power_in.at[pl.ds(0, number)], power_in.at[pl.ds(0, number)], down_send.at[0],
+            down_recv.at[0], {"dates": d, "cols": c},
+        ).wait_send()
+
     @pl.when(c > 0)
     def _():
         up_copy(c).wait_send()
 
     @pl.when(c == 0)
     def _():
-        for k in range(1, GROUP):
-            d_copy(k).wait_send()
-
-        def one(i, carry):
-            down_copy(i).wait_send()
-            return carry
-
-        lax.fori_loop(1, count, one, 0)
+        d_copy(1, GROUP - 1).wait_send()
+        sent_down(near * (count // nz) - 1 + nz - near)
+
+    if nz > near:
+
+        @pl.when(hands_on)
+        def _():
+            sent_down(nz - near)
 
 
 def place_kernel(landed, scaling, interferogram, coherence):
@@ -572,20 +597,15 @@
                 pltpu.VMEM((2 * CHUNK * HALF, 2 * ROWS), BF16),
                 pltpu.VMEM((6 * PAIRS * 8, ROWS), F32),
                 pltpu.VMEM((2, 3 * PAIRS, ROWS), F32),
-                pltpu.VMEM((8, ROWS), F32),
                 pltpu.VMEM((columns, 8, ROWS), F32),
-                pltpu.VMEM((8, ROWS), F32),
                 pltpu.VMEM((GROUP, 8, ROWS), F32),
                 pltpu.VMEM((8, ROWS), F32),
-                pltpu.VMEM((8, ROWS), F32),
                 pltpu.VMEM((GROUP, 24, 128), F32),
-                sem((GROUP - 1,)), sem((GROUP - 1,)),
-                sem((GROUP - 1,)), sem((GROUP - 1,)),
-                sem((2,)), sem((2 * GROUP,)), pltpu.SemaphoreType.REGULAR((2,)),
-                sem((1,)), sem((columns,)), sem((columns,)), sem((1,)),
-                sem((GROUP - 1,)), sem((GROUP - 1,)),
-                sem((GROUP - 1,)), sem((GROUP - 1,)),
-                sem((EACH,)), sem((3,)),
+                sem((1,)), sem((4,)), sem((1,)), sem((1,)),
+                sem((2,)), sem((1,)), pltpu.SemaphoreType.REGULAR((2,)), pltpu.SemaphoreType.REGULAR,
+                sem((1,)), sem((1,)), sem((1,)), sem((1,)),
+                sem((1,)), sem((1,)), sem((1,)), sem((1,)),
+                sem((1,)), sem((3,)),
             ],
             compiler_params=pltpu.CompilerParams(
                 collective_id=0, has_side_effects=True, vmem_limit_bytes=54682 * 1024

time: 31.7 us -> 29.1 us (0.918)
  Pallas kernels: 30.2 us -> 27.5 us
    pallas_call x1, Pallas kernels: 29.4 us -> 26.7 us  [local(): pl.pallas_call(lambda *refs: kernel(nz, columns, *refs), out_shape=(jax.S...]
where the time goes in v6:
time: 29.1 us; the launch traced here: 28.8 us
  Pallas kernels  27.5 us (95%)
  local copies, waits for them, and re-layouts  0.67 us (2%)
  between operations  0.65 us (2%)
    pallas_call x1, Pallas kernels, local(): pl.pallas_call(lambda *refs: kernel(nz, columns, *refs), out_shape=(jax.S...  26.7 us
    pallas_call x1, Pallas kernels, local(): pl.pallas_call(place_kernel, out_shape=(jax.ShapeDtypeStruct((2, CAP, 16,...  0.81 us
    unnamed x4, local copies, waits for them, and re-layouts  0.67 us

profile of v6, /device:TPU:1, one launch (start us, length us, event | category | flops | bytes accessed | tf_op | source)
XLA Modules:
  0.0 28.8 jit_solution(14383619717950050232)
XLA Ops:
  0.6 0.0 copy-start
  0.6 0.0 copy-start.1
  0.6 0.7 %copy-done = s32[64,2]{0,1:T(2,128)S(1)} copy-done((s32[64,2]{0,1:T(2,128)S(1)}, s32[64,2]{0,1:T(2,128)}, u32[]{:S(2)}) %copy-start) | copy-done | bytes 536
  1.3 0.0 copy-done.1
  1.3 26.7 %shard_map.50 = (f32[8,24,128]{2,1,0:T(8,128)S(1)}, f32[8,128]{1,0:T(8,128)S(1)}) custom-call(bf16[2,4,128,256]{3,2,1,0:T(8,128)(2,1)} %refs_0_.1, s32[2,64]{1,0:T(2,128)S(1)} %bitcast.6, s32[1,64]{1,0:T(1,128)S(1)} %bitcast.7), custom_call_target="tpu_custom_call" | custom-call | tf_op jit(solution)/shard_map/pallas_call | solution.py:572
  28.0 0.8 %shard_map.51 = (f32[2,12,16,32]{3,2,1,0:T(8,128)}, f32[12,16,32]{2,1,0:T(8,128)}) custom-call(f32[192,128]{1,0:T(8,128)S(1)} %bitcast.5, f32[8,128]{1,0:T(8,128)S(1)} %get-tuple-element.7.scaling), custom_call_target="tpu_custom_call" | custom-call | tf_op jit(solution)/shard_map/pallas_call | solution.py:614
Async XLA Ops:
  0.6 0.7 %copy-start = (s32[64,2]{0,1:T(2,128)S(1)}, s32[64,2]{0,1:T(2,128)}, u32[]{:S(2)}) copy-start(s32[64,2]{0,1:T(2,128)} %param.4) | copy-start | bytes 1540
  0.6 0.7 %copy-start.1 = (s32[64]{0:T(128)S(1)}, s32[64]{0:T(128)}, u32[]{:S(2)}) copy-start(s32[64]{0:T(128)} %param.5) | copy-start | bytes 772

commit v7 on v6

--- a/solution.py
+++ b/solution.py
@@ -83,11 +83,11 @@
 
 def kernel(
     nz, count, slc_hbm, pairs_hbm, owner_hbm, landed, scaling,
-    slc, pairs_s, pairs_v, owner_v, select, own, look, hot, smoother, sent_0, sent_1, got_0, got_1,
+    slc, pairs_s, pairs_v, owner_v, select, own, look, hot, quarters, smoother, sent_0, sent_1, got_0, got_1,
     edge_out, edge_left, edge_right, images, roots, fields, lhs, sums, looked,
-    power_in, totals, factor_in, results,
+    power_row, power_in, factor_in, results,
     main_send_0, main_recv_0, main_send_1, main_recv_1, edge_send, edge_recv, ready,
-    here, up_send, up_recv, down_send, down_recv, d_send, d_recv, out_send, out_recv, in_sem, table_sem,
+    here, up_send, up_recv, down_send, down_recv, out_send, out_recv, in_sem, table_sem,
 ):
     d = lax.axis_index("dates")
     c = lax.axis_index("cols")
@@ -127,14 +127,6 @@
 
     greet_neighbour(right_later, 0, right)
     greet_neighbour(left_later, GROUP - 1, left)
-
-    @pl.when(c == 0)
-    def _():
-        def one(i, carry):
-            greet({"dates": d, "cols": i})
-            return carry
-
-        lax.fori_loop(1, count, one, 0)
 
     hands_on = (z == 0) & (c > 0)
     handed = (z >= near) & (c >= nz)
@@ -182,7 +174,11 @@
         wide = jnp.concatenate([slc[0, t], slc[1, t]], axis=0).astype(F32)
         square = jnp.sum(wide * wide, axis=0, keepdims=True)
         power_rows.append(square[:, :ROWS] + square[:, ROWS:])
-    power_in[0] = jnp.concatenate(power_rows + [jnp.zeros((8 - EACH, ROWS), F32)], axis=0)
+    folded = jnp.concatenate(power_rows + [jnp.zeros((8 - EACH, ROWS), F32)], axis=0)
+    folded = folded + pltpu.roll(folded, 64, 1)
+    folded = folded + pltpu.roll(folded, 32, 1)
+    own_lane = (iota((8, ROWS), 1) >> 5) == iota((8, ROWS), 0)
+    power_row[...] = jnp.sum(jnp.where(own_lane, folded, 0.0), axis=0, keepdims=True)
     cut(0, matrix)
 
     first = (d == 0).astype(jnp.int32)
@@ -204,6 +200,14 @@
                     ready.at[side], inc=1, device_id={"dates": e, "cols": other}, device_id_type=MESH
                 )
 
+    @pl.when(c == 0)
+    def _():
+        def one(i, carry):
+            greet({"dates": d, "cols": i})
+            return carry
+
+        lax.fori_loop(1, count, one, 0)
+
     @pl.when(handed)
     def _():
         pl.semaphore_signal(
@@ -218,18 +222,26 @@
             src_ref=src, dst_ref=dst, send_sem=send, recv_sem=recv, device_id=peer, device_id_type=MESH
         )
 
-    def up_copy(i, size=1):
+    def up_copy(e, size=1):
         return stage(
-            power_in.at[pl.ds(0, size)], power_in.at[pl.ds(i, size)], up_send.at[0], up_recv.at[0],
-            {"dates": d, "cols": 0},
+            power_in.at[pl.ds(0, size)] if size > 1 else power_row,
+            power_in.at[pl.ds(0 if size > 1 else d * count + c, size)],
+            up_send.at[0], up_recv.at[0], {"dates": e, "cols": 0},
         )
 
     def down_copy(i):
         return stage(factor_in, factor_in, down_send.at[0], down_recv.at[0], {"dates": d, "cols": i})
 
+    for k in range(1, GROUP):
+        up_copy((d + k) % GROUP).start()
+
     @pl.when(c > 0)
     def _():
-        up_copy(c).start()
+        up_copy(d).start()
+
+    @pl.when(c == 0)
+    def _():
+        power_in[pl.ds(d * count, 1), :] = power_row[...]
 
     targets = ({"dates": 0, "cols": right}, {"dates": GROUP - 1, "cols": left})
 
@@ -300,14 +312,16 @@
         own[g] = jnp.where(mine == quarter + 4.0 * g, 1.0, 0.0)
 
     def date_rows(which):
-        date = pairs_v[which : which + 1, :]
-        row = ((date >> 2) * 8 + (date & 3)).astype(F32)
-        down = jnp.transpose(jnp.broadcast_to(row, (ROWS, PAIRS)))[:, : 8 * GROUP]
-        lane = iota((PAIRS, 8 * GROUP), 1).astype(F32)
-        one = jnp.where(down == lane, 1.0, 0.0)
-        return jnp.concatenate([one, one, one], axis=1).astype(BF16)
-
-    hot[...] = jnp.concatenate([date_rows(0), date_rows(1)], axis=0)
+        date = pairs_v[which : which + 1, :].astype(F32)
+        return jnp.transpose(jnp.broadcast_to(date, (ROWS, PAIRS)))
+
+    date = jnp.concatenate([date_rows(0), date_rows(1)], axis=0)
+    lane = iota((2 * PAIRS, ROWS), 1)
+    first_date = (EACH * (lane & 7)).astype(F32)
+    one = jnp.where((date >= first_date) & (date < first_date + EACH) & (lane < 24), 1.0, 0.0)
+    hot[...] = one[:, : 3 * GROUP].astype(BF16)
+    phase = date - EACH * jnp.floor(date * (1.0 / EACH))
+    quarters[...] = jnp.where(phase == (lane >> 5).astype(F32), 1.0, 0.0)
     one = jnp.where((iota((ROWS, 128), 0) >> 2) == (iota((ROWS, 128), 1) & 31), 1.0, 0.0)
     look[...] = jnp.concatenate([one, one, one], axis=0).astype(BF16)
 
@@ -431,19 +445,6 @@
     arrive(2, 6, 1, 7)
     pairs_of(0)
 
-    def d_copy(k, size=1):
-        return stage(
-            totals.at[pl.ds(d if size == 1 else 0, size)], totals.at[pl.ds(d if size == 1 else 0, size)],
-            d_send.at[0], d_recv.at[0], date_peer(k),
-        )
-
-    @pl.when(c == 0)
-    def _():
-        up_copy(1, count - 1).wait_recv()
-        totals[d] = jnp.sum(power_in[...], axis=0)
-        for k in order:
-            d_copy(k).start()
-
     @pl.when((d == GROUP - 1) & (c < count - 1))
     def _():
         edges(1)
@@ -482,9 +483,13 @@
 
     @pl.when(c == 0)
     def _():
-        d_copy(1, GROUP - 1).wait_recv()
-        parts = jnp.concatenate(split3(totals[...].reshape(8 * GROUP, ROWS)), axis=0)
-        total = jnp.sum(dot(hot[...], parts), axis=1, keepdims=True)
+        up_copy(0, GROUP * count - 1).wait_recv()
+        rows = [
+            jnp.sum(power_in[count * e : count * (e + 1), :], axis=0, keepdims=True)
+            for e in range(GROUP)
+        ]
+        parts = jnp.concatenate(split3(jnp.concatenate(rows, axis=0)), axis=0)
+        total = jnp.sum(dot(hot[...], parts) * quarters[...], axis=1, keepdims=True)
         scale = jnp.sqrt(total / (ROWS * WIDTH * count) + 1e-06)
         factor = (1.0 / 64.0) / (scale[:PAIRS] * scale[PAIRS:])
         factor = jnp.broadcast_to(jnp.concatenate([factor, factor], axis=0), (ROWS, ROWS))
@@ -526,17 +531,17 @@
 
     def sent_down(number):
         stage(
-            power_in.at[pl.ds(0, number)], power_in.at[pl.ds(0, number)], down_send.at[0],
+            power_in.at[pl.ds(0, 8 * number)], power_in.at[pl.ds(0, 8 * number)], down_send.at[0],
             down_recv.at[0], {"dates": d, "cols": c},
         ).wait_send()
 
     @pl.when(c > 0)
     def _():
-        up_copy(c).wait_send()
+        up_copy(0, GROUP).wait_send()
 
     @pl.when(c == 0)
     def _():
-        d_copy(1, GROUP - 1).wait_send()
+        up_copy(0, GROUP - 1).wait_send()
         sent_down(near * (count // nz) - 1 + nz - near)
 
     if nz > near:
@@ -582,7 +587,8 @@
                 pltpu.VMEM((128, 3 * PAIRS), BF16),
                 pltpu.VMEM((3, PAIRS, 128), F32),
                 pltpu.VMEM((3 * ROWS, 128), BF16),
-                pltpu.VMEM((2 * PAIRS, 24 * GROUP), BF16),
+                pltpu.VMEM((2 * PAIRS, 3 * GROUP), BF16),
+                pltpu.VMEM((2 * PAIRS, ROWS), F32),
                 pltpu.VMEM((2 * ROWS, 2 * ROWS), BF16),
                 pltpu.VMEM((GROUP, EACH * 2 * PIECES[0], ROWS), BF16),
                 pltpu.VMEM((GROUP, EACH * 2 * PIECES[1], ROWS), BF16),
@@ -597,14 +603,13 @@
                 pltpu.VMEM((2 * CHUNK * HALF, 2 * ROWS), BF16),
                 pltpu.VMEM((6 * PAIRS * 8, ROWS), F32),
                 pltpu.VMEM((2, 3 * PAIRS, ROWS), F32),
-                pltpu.VMEM((columns, 8, ROWS), F32),
-                pltpu.VMEM((GROUP, 8, ROWS), F32),
+                pltpu.VMEM((1, ROWS), F32),
+                pltpu.VMEM((GROUP * columns, ROWS), F32),
                 pltpu.VMEM((8, ROWS), F32),
                 pltpu.VMEM((GROUP, 24, 128), F32),
                 sem((1,)), sem((4,)), sem((1,)), sem((1,)),
                 sem((2,)), sem((1,)), pltpu.SemaphoreType.REGULAR((2,)), pltpu.SemaphoreType.REGULAR,
-                sem((1,)), sem((1,)), sem((1,)), sem((1,)),
-                sem((1,)), sem((1,)), sem((1,)), sem((1,)),
+                sem((1,)), sem((1,)), sem((1,)), sem((1,)), sem((1,)), sem((1,)),
                 sem((1,)), sem((3,)),
             ],
             compiler_params=pltpu.CompilerParams(

time: 29.1 us -> 30 us (1.031)
  Pallas kernels: 27.5 us -> 28.5 us
    pallas_call x1, Pallas kernels: 26.7 us -> 27.6 us  [local(): pl.pallas_call(lambda *refs: kernel(nz, columns, *refs), out_shape=(jax.S...]
where the time goes in v7:
time: 30 us; the launch traced here: 29.8 us
  Pallas kernels  28.5 us (95%)
  local copies, waits for them, and re-layouts  0.67 us (2%)
  between operations  0.65 us (2%)
    pallas_call x1, Pallas kernels, local(): pl.pallas_call(lambda *refs: kernel(nz, columns, *refs), out_shape=(jax.S...  27.6 us
    pallas_call x1, Pallas kernels, local(): pl.pallas_call(place_kernel, out_shape=(jax.ShapeDtypeStruct((2, CAP, 16,...  0.81 us
    unnamed x4, local copies, waits for them, and re-layouts  0.67 us

profile of v7, /device:TPU:1, one launch (start us, length us, event | category | flops | bytes accessed | tf_op | source)
XLA Modules:
  0.0 29.8 jit_solution(10115964046240402170)
XLA Ops:
  0.6 0.0 copy-start
  0.6 0.0 copy-start.1
  0.6 0.7 %copy-done = s32[64,2]{0,1:T(2,128)S(1)} copy-done((s32[64,2]{0,1:T(2,128)S(1)}, s32[64,2]{0,1:T(2,128)}, u32[]{:S(2)}) %copy-start) | copy-done | bytes 536
  1.3 0.0 copy-done.1
  1.3 27.6 %shard_map.50 = (f32[8,24,128]{2,1,0:T(8,128)S(1)}, f32[8,128]{1,0:T(8,128)S(1)}) custom-call(bf16[2,4,128,256]{3,2,1,0:T(8,128)(2,1)} %refs_0_.1, s32[2,64]{1,0:T(2,128)S(1)} %bitcast.6, s32[1,64]{1,0:T(1,128)S(1)} %bitcast.7), custom_call_target="tpu_custom_call" | custom-call | tf_op jit(solution)/shard_map/pallas_call | solution.py:577
  29.0 0.8 %shard_map.51 = (f32[2,12,16,32]{3,2,1,0:T(8,128)}, f32[12,16,32]{2,1,0:T(8,128)}) custom-call(f32[192,128]{1,0:T(8,128)S(1)} %bitcast.5, f32[8,128]{1,0:T(8,128)S(1)} %get-tuple-element.7.scaling), custom_call_target="tpu_custom_call" | custom-call | tf_op jit(solution)/shard_map/pallas_call | solution.py:619
Async XLA Ops:
  0.6 0.7 %copy-start = (s32[64,2]{0,1:T(2,128)S(1)}, s32[64,2]{0,1:T(2,128)}, u32[]{:S(2)}) copy-start(s32[64,2]{0,1:T(2,128)} %param.4) | copy-start | bytes 1540
  0.6 0.7 %copy-start.1 = (s32[64]{0:T(128)S(1)}, s32[64]{0:T(128)}, u32[]{:S(2)}) copy-start(s32[64]{0:T(128)} %param.5) | copy-start | bytes 772

commit v8 on v6

--- a/solution.py
+++ b/solution.py
@@ -83,9 +83,9 @@
 
 def kernel(
     nz, count, slc_hbm, pairs_hbm, owner_hbm, landed, scaling,
-    slc, pairs_s, pairs_v, owner_v, select, own, look, hot, smoother, sent_0, sent_1, got_0, got_1,
+    slc, pairs_s, pairs_v, owner_v, select, own, look, hot, quarters, smoother, sent_0, sent_1, got_0, got_1,
     edge_out, edge_left, edge_right, images, roots, fields, lhs, sums, looked,
-    power_in, totals, factor_in, results,
+    power_row, power_in, totals, factor_in, results,
     main_send_0, main_recv_0, main_send_1, main_recv_1, edge_send, edge_recv, ready,
     here, up_send, up_recv, down_send, down_recv, d_send, d_recv, out_send, out_recv, in_sem, table_sem,
 ):
@@ -182,7 +182,11 @@
         wide = jnp.concatenate([slc[0, t], slc[1, t]], axis=0).astype(F32)
         square = jnp.sum(wide * wide, axis=0, keepdims=True)
         power_rows.append(square[:, :ROWS] + square[:, ROWS:])
-    power_in[0] = jnp.concatenate(power_rows + [jnp.zeros((8 - EACH, ROWS), F32)], axis=0)
+    folded = jnp.concatenate(power_rows + [jnp.zeros((8 - EACH, ROWS), F32)], axis=0)
+    folded = folded + pltpu.roll(folded, 64, 1)
+    folded = folded + pltpu.roll(folded, 32, 1)
+    own_lane = (iota((8, ROWS), 1) >> 5) == iota((8, ROWS), 0)
+    power_row[...] = jnp.sum(jnp.where(own_lane, folded, 0.0), axis=0, keepdims=True)
     cut(0, matrix)
 
     first = (d == 0).astype(jnp.int32)
@@ -220,8 +224,8 @@
 
     def up_copy(i, size=1):
         return stage(
-            power_in.at[pl.ds(0, size)], power_in.at[pl.ds(i, size)], up_send.at[0], up_recv.at[0],
-            {"dates": d, "cols": 0},
+            power_in.at[pl.ds(0, size)] if size > 1 else power_row, power_in.at[pl.ds(i, size)],
+            up_send.at[0], up_recv.at[0], {"dates": d, "cols": 0},
         )
 
     def down_copy(i):
@@ -300,14 +304,16 @@
         own[g] = jnp.where(mine == quarter + 4.0 * g, 1.0, 0.0)
 
     def date_rows(which):
-        date = pairs_v[which : which + 1, :]
-        row = ((date >> 2) * 8 + (date & 3)).astype(F32)
-        down = jnp.transpose(jnp.broadcast_to(row, (ROWS, PAIRS)))[:, : 8 * GROUP]
-        lane = iota((PAIRS, 8 * GROUP), 1).astype(F32)
-        one = jnp.where(down == lane, 1.0, 0.0)
-        return jnp.concatenate([one, one, one], axis=1).astype(BF16)
-
-    hot[...] = jnp.concatenate([date_rows(0), date_rows(1)], axis=0)
+        date = pairs_v[which : which + 1, :].astype(F32)
+        return jnp.transpose(jnp.broadcast_to(date, (ROWS, PAIRS)))
+
+    date = jnp.concatenate([date_rows(0), date_rows(1)], axis=0)
+    lane = iota((2 * PAIRS, ROWS), 1)
+    first_date = (EACH * (lane & 7)).astype(F32)
+    one = jnp.where((date >= first_date) & (date < first_date + EACH) & (lane < 24), 1.0, 0.0)
+    hot[...] = one[:, : 3 * GROUP].astype(BF16)
+    phase = date - EACH * jnp.floor(date * (1.0 / EACH))
+    quarters[...] = jnp.where(phase == (lane >> 5).astype(F32), 1.0, 0.0)
     one = jnp.where((iota((ROWS, 128), 0) >> 2) == (iota((ROWS, 128), 1) & 31), 1.0, 0.0)
     look[...] = jnp.concatenate([one, one, one], axis=0).astype(BF16)
 
@@ -362,7 +368,7 @@
         for date in range(DATES):
             roots[date, HALF:] = smooth[HALF * date : HALF * (date + 1)]
 
-    def pairs_of(half):
+    def pairs_of(half, between=None):
         window = slice(HALF * half, HALF * half + WINDOW)
 
         def place(field, p):
@@ -404,7 +410,12 @@
                 sums[place(2, p), :] = value[0:8] + value[8:16]
             return carry
 
-        lax.fori_loop(0, PAIRS // CHUNK, chunk, 0)
+        if between is None:
+            lax.fori_loop(0, PAIRS // CHUNK, chunk, 0)
+        else:
+            lax.fori_loop(0, PAIRS // CHUNK // 2, chunk, 0)
+            between()
+            lax.fori_loop(PAIRS // CHUNK // 2, PAIRS // CHUNK, chunk, 0)
         rows = sums[pl.ds(3 * half * PAIRS * 8, 3 * PAIRS, stride=8), :]
         for i in range(1, 8):
             rows = rows + sums[pl.ds(3 * half * PAIRS * 8 + i, 3 * PAIRS, stride=8), :]
@@ -437,12 +448,14 @@
             d_send.at[0], d_recv.at[0], date_peer(k),
         )
 
-    @pl.when(c == 0)
-    def _():
-        up_copy(1, count - 1).wait_recv()
-        totals[d] = jnp.sum(power_in[...], axis=0)
-        for k in order:
-            d_copy(k).start()
+    def add_up():
+        @pl.when(c == 0)
+        def _():
+            up_copy(1, count - 1).wait_recv()
+            total = power_row[...] + jnp.sum(power_in[1:count, :], axis=0, keepdims=True)
+            totals[pl.ds(d, 1), :] = total
+            for k in order:
+                d_copy(k).start()
 
     @pl.when((d == GROUP - 1) & (c < count - 1))
     def _():
@@ -450,7 +463,7 @@
 
     second_copy(1, GROUP - 1).wait_recv()
     take_second()
-    pairs_of(1)
+    pairs_of(1, add_up)
 
     wide = []
     for q in range(6):
@@ -483,8 +496,8 @@
     @pl.when(c == 0)
     def _():
         d_copy(1, GROUP - 1).wait_recv()
-        parts = jnp.concatenate(split3(totals[...].reshape(8 * GROUP, ROWS)), axis=0)
-        total = jnp.sum(dot(hot[...], parts), axis=1, keepdims=True)
+        parts = jnp.concatenate(split3(totals[...]), axis=0)
+        total = jnp.sum(dot(hot[...], parts) * quarters[...], axis=1, keepdims=True)
         scale = jnp.sqrt(total / (ROWS * WIDTH * count) + 1e-06)
         factor = (1.0 / 64.0) / (scale[:PAIRS] * scale[PAIRS:])
         factor = jnp.broadcast_to(jnp.concatenate([factor, factor], axis=0), (ROWS, ROWS))
@@ -526,7 +539,7 @@
 
     def sent_down(number):
         stage(
-            power_in.at[pl.ds(0, number)], power_in.at[pl.ds(0, number)], down_send.at[0],
+            power_in.at[pl.ds(0, 8 * number)], power_in.at[pl.ds(0, 8 * number)], down_send.at[0],
             down_recv.at[0], {"dates": d, "cols": c},
         ).wait_send()
 
@@ -582,7 +595,8 @@
                 pltpu.VMEM((128, 3 * PAIRS), BF16),
                 pltpu.VMEM((3, PAIRS, 128), F32),
                 pltpu.VMEM((3 * ROWS, 128), BF16),
-                pltpu.VMEM((2 * PAIRS, 24 * GROUP), BF16),
+                pltpu.VMEM((2 * PAIRS, 3 * GROUP), BF16),
+                pltpu.VMEM((2 * PAIRS, ROWS), F32),
                 pltpu.VMEM((2 * ROWS, 2 * ROWS), BF16),
                 pltpu.VMEM((GROUP, EACH * 2 * PIECES[0], ROWS), BF16),
                 pltpu.VMEM((GROUP, EACH * 2 * PIECES[1], ROWS), BF16),
@@ -597,8 +611,9 @@
                 pltpu.VMEM((2 * CHUNK * HALF, 2 * ROWS), BF16),
                 pltpu.VMEM((6 * PAIRS * 8, ROWS), F32),
                 pltpu.VMEM((2, 3 * PAIRS, ROWS), F32),
-                pltpu.VMEM((columns, 8, ROWS), F32),
-                pltpu.VMEM((GROUP, 8, ROWS), F32),
+                pltpu.VMEM((1, ROWS), F32),
+                pltpu.VMEM((8 * columns, ROWS), F32),
+                pltpu.VMEM((GROUP, ROWS), F32),
                 pltpu.VMEM((8, ROWS), F32),
                 pltpu.VMEM((GROUP, 24, 128), F32),
                 sem((1,)), sem((4,)), sem((1,)), sem((1,)),

time: 29.1 us -> 28.8 us (0.990)
  the two profiles are of different devices: /device:TPU:1 before, /device:TPU:8 now
where the time goes in v8:
time: 28.8 us; the launch traced here: 28.6 us
  Pallas kernels  27.3 us (95%)
  local copies, waits for them, and re-layouts  0.67 us (2%)
  between operations  0.65 us (2%)
    pallas_call x1, Pallas kernels, local(): pl.pallas_call(lambda *refs: kernel(nz, columns, *refs), out_shape=(jax.S...  26.5 us
    pallas_call x1, Pallas kernels, local(): pl.pallas_call(place_kernel, out_shape=(jax.ShapeDtypeStruct((2, CAP, 16,...  0.81 us
    unnamed x4, local copies, waits for them, and re-layouts  0.67 us

profile of v8, /device:TPU:8, one launch (start us, length us, event | category | flops | bytes accessed | tf_op | source)
XLA Modules:
  0.0 28.6 jit_solution(10185950317413755052)
XLA Ops:
  0.6 0.0 copy-start
  0.6 0.0 copy-start.1
  0.6 0.7 %copy-done = s32[64,2]{0,1:T(2,128)S(1)} copy-done((s32[64,2]{0,1:T(2,128)S(1)}, s32[64,2]{0,1:T(2,128)}, u32[]{:S(2)}) %copy-start) | copy-done | bytes 536
  1.3 0.0 copy-done.1
  1.3 26.5 %shard_map.50 = (f32[8,24,128]{2,1,0:T(8,128)S(1)}, f32[8,128]{1,0:T(8,128)S(1)}) custom-call(bf16[2,4,128,256]{3,2,1,0:T(8,128)(2,1)} %refs_0_.1, s32[2,64]{1,0:T(2,128)S(1)} %bitcast.6, s32[1,64]{1,0:T(1,128)S(1)} %bitcast.7), custom_call_target="tpu_custom_call" | custom-call | tf_op jit(solution)/shard_map/pallas_call | solution.py:585
  27.8 0.8 %shard_map.51 = (f32[2,12,16,32]{3,2,1,0:T(8,128)}, f32[12,16,32]{2,1,0:T(8,128)}) custom-call(f32[192,128]{1,0:T(8,128)S(1)} %bitcast.5, f32[8,128]{1,0:T(8,128)S(1)} %get-tuple-element.7.scaling), custom_call_target="tpu_custom_call" | custom-call | tf_op jit(solution)/shard_map/pallas_call | solution.py:629
Async XLA Ops:
  0.6 0.7 %copy-start = (s32[64,2]{0,1:T(2,128)S(1)}, s32[64,2]{0,1:T(2,128)}, u32[]{:S(2)}) copy-start(s32[64,2]{0,1:T(2,128)} %param.4) | copy-start | bytes 1540
  0.6 0.7 %copy-start.1 = (s32[64]{0:T(128)S(1)}, s32[64]{0:T(128)}, u32[]{:S(2)}) copy-start(s32[64]{0:T(128)} %param.5) | copy-start | bytes 772

commit v9 on v8

--- a/solution.py
+++ b/solution.py
@@ -98,7 +98,7 @@
 
     right = (c + 1) % count
     left = (c + count - 1) % count
-    near = min(2, nz)
+    near = min(3, nz)
     right_later = (z < nz - 1) & (c < count - 1)
     right_earlier = (z == nz - 1) & (c < count - 1)
     left_later = (z == 0) & (c > 0)
@@ -136,13 +136,14 @@
 
         lax.fori_loop(1, count, one, 0)
 
-    hands_on = (z == 0) & (c > 0)
-    handed = (z >= near) & (c >= nz)
+    hands_on = z == near - 1
+    handed = z >= near
+    hand = c - z + near - 1
 
     @pl.when(hands_on)
     def _():
         for i in range(near, nz):
-            greet({"dates": d, "cols": c - z + i})
+            greet({"dates": d, "cols": hand - (near - 1) + i})
 
     tables = [
         pltpu.make_async_copy(pairs_hbm, pairs_s, table_sem.at[0]),
@@ -187,35 +188,6 @@
     folded = folded + pltpu.roll(folded, 32, 1)
     own_lane = (iota((8, ROWS), 1) >> 5) == iota((8, ROWS), 0)
     power_row[...] = jnp.sum(jnp.where(own_lane, folded, 0.0), axis=0, keepdims=True)
-    cut(0, matrix)
-
-    first = (d == 0).astype(jnp.int32)
-    last = (d == GROUP - 1).astype(jnp.int32)
-    pl.semaphore_wait(
-        barrier,
-        (GROUP - 1)
-        + (c > 0).astype(jnp.int32)
-        + handed.astype(jnp.int32)
-        + right_earlier.astype(jnp.int32) * (1 + GROUP * last)
-        + left_earlier.astype(jnp.int32) * (1 + GROUP * first),
-    )
-
-    def tell_ready(side, condition, other):
-        @pl.when(condition)
-        def _():
-            for e in range(GROUP):
-                pl.semaphore_signal(
-                    ready.at[side], inc=1, device_id={"dates": e, "cols": other}, device_id_type=MESH
-                )
-
-    @pl.when(handed)
-    def _():
-        pl.semaphore_signal(
-            here, inc=1, device_id={"dates": d, "cols": c - z}, device_id_type=MESH
-        )
-
-    tell_ready(0, left_earlier & (d == 0), left)
-    tell_ready(1, right_earlier & (d == GROUP - 1), right)
 
     def stage(src, dst, send, recv, peer):
         return pltpu.make_async_remote_copy(
@@ -231,9 +203,43 @@
     def down_copy(i):
         return stage(factor_in, factor_in, down_send.at[0], down_recv.at[0], {"dates": d, "cols": i})
 
-    @pl.when(c > 0)
-    def _():
-        up_copy(c).start()
+    first = (d == 0).astype(jnp.int32)
+    last = (d == GROUP - 1).astype(jnp.int32)
+
+    def enter():
+        pl.semaphore_wait(
+            barrier,
+            (GROUP - 1)
+            + (c > 0).astype(jnp.int32)
+            + handed.astype(jnp.int32)
+            + right_earlier.astype(jnp.int32) * (1 + GROUP * last)
+            + left_earlier.astype(jnp.int32) * (1 + GROUP * first),
+        )
+
+        def tell_ready(side, condition, other):
+            @pl.when(condition)
+            def _():
+                for e in range(GROUP):
+                    pl.semaphore_signal(
+                        ready.at[side], inc=1, device_id={"dates": e, "cols": other}, device_id_type=MESH
+                    )
+
+        @pl.when(handed)
+        def _():
+            pl.semaphore_signal(
+                here, inc=1, device_id={"dates": d, "cols": hand}, device_id_type=MESH
+            )
+
+        tell_ready(0, left_earlier & (d == 0), left)
+        tell_ready(1, right_earlier & (d == GROUP - 1), right)
+
+        @pl.when(c > 0)
+        def _():
+            up_copy(c).start()
+
+    pl.when(z >= nz // 2)(enter)
+    cut(0, matrix)
+    pl.when(z < nz // 2)(enter)
 
     targets = ({"dates": 0, "cols": right}, {"dates": GROUP - 1, "cols": left})
 
@@ -368,7 +374,7 @@
         for date in range(DATES):
             roots[date, HALF:] = smooth[HALF * date : HALF * (date + 1)]
 
-    def pairs_of(half, between=None):
+    def pairs_of(half, then=None):
         window = slice(HALF * half, HALF * half + WINDOW)
 
         def place(field, p):
@@ -410,12 +416,9 @@
                 sums[place(2, p), :] = value[0:8] + value[8:16]
             return carry
 
-        if between is None:
-            lax.fori_loop(0, PAIRS // CHUNK, chunk, 0)
-        else:
-            lax.fori_loop(0, PAIRS // CHUNK // 2, chunk, 0)
-            between()
-            lax.fori_loop(PAIRS // CHUNK // 2, PAIRS // CHUNK, chunk, 0)
+        lax.fori_loop(0, PAIRS // CHUNK, chunk, 0)
+        if then is not None:
+            then()
         rows = sums[pl.ds(3 * half * PAIRS * 8, 3 * PAIRS, stride=8), :]
         for i in range(1, 8):
             rows = rows + sums[pl.ds(3 * half * PAIRS * 8 + i, 3 * PAIRS, stride=8), :]
@@ -501,14 +504,12 @@
         scale = jnp.sqrt(total / (ROWS * WIDTH * count) + 1e-06)
         factor = (1.0 / 64.0) / (scale[:PAIRS] * scale[PAIRS:])
         factor = jnp.broadcast_to(jnp.concatenate([factor, factor], axis=0), (ROWS, ROWS))
-        factor = jnp.transpose(factor)[:8]
+        factor = jnp.transpose(factor)[:1]
         factor_in[...] = factor
         for i in range(near):
             for j in range(count // nz):
                 if i + j > 0:
                     down_copy(j * nz + i).start()
-        for i in range(near, nz):
-            down_copy(i).start()
 
     @pl.when(c > 0)
     def _():
@@ -519,7 +520,7 @@
         if nz > near:
             pl.semaphore_wait(here, nz - near)
         for i in range(near, nz):
-            down_copy(c - z + i).start()
+            down_copy(hand - (near - 1) + i).start()
 
     factor = jnp.transpose(jnp.broadcast_to(factor_in[0:1, :PAIRS], (ROWS, PAIRS)))
     factors = [jnp.sum(own[g] * factor, axis=0, keepdims=True) for g in range(3)]
@@ -539,7 +540,7 @@
 
     def sent_down(number):
         stage(
-            power_in.at[pl.ds(0, 8 * number)], power_in.at[pl.ds(0, 8 * number)], down_send.at[0],
+            power_in.at[pl.ds(0, number)], power_in.at[pl.ds(0, number)], down_send.at[0],
             down_recv.at[0], {"dates": d, "cols": c},
         ).wait_send()
 
@@ -550,7 +551,7 @@
     @pl.when(c == 0)
     def _():
         d_copy(1, GROUP - 1).wait_send()
-        sent_down(near * (count // nz) - 1 + nz - near)
+        sent_down(near * (count // nz) - 1)
 
     if nz > near:
 
@@ -612,9 +613,9 @@
                 pltpu.VMEM((6 * PAIRS * 8, ROWS), F32),
                 pltpu.VMEM((2, 3 * PAIRS, ROWS), F32),
                 pltpu.VMEM((1, ROWS), F32),
-                pltpu.VMEM((8 * columns, ROWS), F32),
+                pltpu.VMEM((columns, ROWS), F32),
                 pltpu.VMEM((GROUP, ROWS), F32),
-                pltpu.VMEM((8, ROWS), F32),
+                pltpu.VMEM((1, ROWS), F32),
                 pltpu.VMEM((GROUP, 24, 128), F32),
                 sem((1,)), sem((4,)), sem((1,)), sem((1,)),
                 sem((2,)), sem((1,)), pltpu.SemaphoreType.REGULAR((2,)), pltpu.SemaphoreType.REGULAR,

time: 28.8 us -> 27.3 us (0.948)
  the two profiles are of different devices: /device:TPU:8 before, /device:TPU:1 now
where the time goes in v9:
time: 27.3 us; the launch traced here: 26.9 us
  Pallas kernels  25.6 us (94%)
  local copies, waits for them, and re-layouts  0.67 us (2%)
  between operations  0.65 us (2%)
    pallas_call x1, Pallas kernels, local(): pl.pallas_call(lambda *refs: kernel(nz, columns, *refs), out_shape=(jax.S...  24.8 us
    pallas_call x1, Pallas kernels, local(): pl.pallas_call(place_kernel, out_shape=(jax.ShapeDtypeStruct((2, CAP, 16,...  0.81 us
    unnamed x4, local copies, waits for them, and re-layouts  0.67 us

profile of v9, /device:TPU:1, one launch (start us, length us, event | category | flops | bytes accessed | tf_op | source)
XLA Modules:
  0.0 26.9 jit_solution(15832098404363679270)
XLA Ops:
  0.6 0.0 copy-start
  0.6 0.0 copy-start.1
  0.6 0.7 %copy-done = s32[64,2]{0,1:T(2,128)S(1)} copy-done((s32[64,2]{0,1:T(2,128)S(1)}, s32[64,2]{0,1:T(2,128)}, u32[]{:S(2)}) %copy-start) | copy-done | bytes 536
  1.3 0.0 copy-done.1
  1.3 24.8 %shard_map.50 = (f32[8,24,128]{2,1,0:T(8,128)S(1)}, f32[8,128]{1,0:T(8,128)S(1)}) custom-call(bf16[2,4,128,256]{3,2,1,0:T(8,128)(2,1)} %refs_0_.1, s32[2,64]{1,0:T(2,128)S(1)} %bitcast.6, s32[1,64]{1,0:T(1,128)S(1)} %bitcast.7), custom_call_target="tpu_custom_call" | custom-call | tf_op jit(solution)/shard_map/pallas_call | solution.py:586
  26.1 0.8 %shard_map.51 = (f32[2,12,16,32]{3,2,1,0:T(8,128)}, f32[12,16,32]{2,1,0:T(8,128)}) custom-call(f32[192,128]{1,0:T(8,128)S(1)} %bitcast.5, f32[8,128]{1,0:T(8,128)S(1)} %get-tuple-element.7.scaling), custom_call_target="tpu_custom_call" | custom-call | tf_op jit(solution)/shard_map/pallas_call | solution.py:630
Async XLA Ops:
  0.6 0.7 %copy-start = (s32[64,2]{0,1:T(2,128)S(1)}, s32[64,2]{0,1:T(2,128)}, u32[]{:S(2)}) copy-start(s32[64,2]{0,1:T(2,128)} %param.4) | copy-start | bytes 1540
  0.6 0.7 %copy-start.1 = (s32[64]{0:T(128)S(1)}, s32[64]{0:T(128)}, u32[]{:S(2)}) copy-start(s32[64]{0:T(128)} %param.5) | copy-start | bytes 772

commit v10 on v9

--- a/solution.py
+++ b/solution.py
@@ -83,12 +83,15 @@
 
 def kernel(
     nz, count, slc_hbm, pairs_hbm, owner_hbm, landed, scaling,
-    slc, pairs_s, pairs_v, owner_v, select, own, look, hot, quarters, smoother, sent_0, sent_1, got_0, got_1,
+    slc, pairs_s, pairs_v, owner_v, select, own, look, hot, source_of, smoother, sent_0, sent_1, got_0, got_1,
     edge_out, edge_left, edge_right, images, roots, fields, lhs, sums, looked,
     power_row, power_in, totals, factor_in, results,
     main_send_0, main_recv_0, main_send_1, main_recv_1, edge_send, edge_recv, ready,
     here, up_send, up_recv, down_send, down_recv, d_send, d_recv, out_send, out_recv, in_sem, table_sem,
 ):
+    load = pltpu.make_async_copy(slc_hbm, slc, in_sem.at[0])
+    load.start()
+
     d = lax.axis_index("dates")
     c = lax.axis_index("cols")
     z = c % nz
@@ -103,9 +106,6 @@
     right_earlier = (z == nz - 1) & (c < count - 1)
     left_later = (z == 0) & (c > 0)
     left_earlier = (z > 0) & (c > 0)
-
-    load = pltpu.make_async_copy(slc_hbm, slc, in_sem.at[0])
-    load.start()
 
     barrier = pltpu.get_barrier_semaphore()
 
@@ -306,20 +306,14 @@
     rank_down = jnp.sum(jnp.where(same & later, 1.0, 0.0), axis=1, keepdims=True)
     quarter = (iota((PAIRS, 128), 1) >> 5).astype(F32)
     mine = jnp.where(owner_down[:, :1] == d.astype(F32), rank_down, -1.0)
-    for g in range(3):
-        own[g] = jnp.where(mine == quarter + 4.0 * g, 1.0, 0.0)
-
-    def date_rows(which):
-        date = pairs_v[which : which + 1, :].astype(F32)
-        return jnp.transpose(jnp.broadcast_to(date, (ROWS, PAIRS)))
-
-    date = jnp.concatenate([date_rows(0), date_rows(1)], axis=0)
-    lane = iota((2 * PAIRS, ROWS), 1)
-    first_date = (EACH * (lane & 7)).astype(F32)
-    one = jnp.where((date >= first_date) & (date < first_date + EACH) & (lane < 24), 1.0, 0.0)
-    hot[...] = one[:, : 3 * GROUP].astype(BF16)
-    phase = date - EACH * jnp.floor(date * (1.0 / EACH))
-    quarters[...] = jnp.where(phase == (lane >> 5).astype(F32), 1.0, 0.0)
+    masks = [jnp.where(mine == quarter + 4.0 * g, 1.0, 0.0) for g in range(3)]
+    masks = jnp.concatenate(masks, axis=1)
+    own[...] = jnp.concatenate([masks, jnp.zeros_like(masks)], axis=0).astype(BF16)
+
+    date = jnp.concatenate([pairs_v[0:1, :], pairs_v[1:2, :]], axis=1)
+    one = jnp.where((iota((ROWS, 2 * PAIRS), 0) >> 5) == (date & (EACH - 1)), 1.0, 0.0)
+    hot[...] = jnp.concatenate([one, one, one], axis=0).astype(BF16)
+    source_of[...] = jnp.where(iota((GROUP, 2 * PAIRS), 0) == (date >> 2), 1.0, 0.0)
     one = jnp.where((iota((ROWS, 128), 0) >> 2) == (iota((ROWS, 128), 1) & 31), 1.0, 0.0)
     look[...] = jnp.concatenate([one, one, one], axis=0).astype(BF16)
 
@@ -499,12 +493,10 @@
     @pl.when(c == 0)
     def _():
         d_copy(1, GROUP - 1).wait_recv()
-        parts = jnp.concatenate(split3(totals[...]), axis=0)
-        total = jnp.sum(dot(hot[...], parts) * quarters[...], axis=1, keepdims=True)
+        parts = jnp.concatenate(split3(totals[...]), axis=1)
+        total = jnp.sum(dot(parts, hot[...]) * source_of[...], axis=0, keepdims=True)
         scale = jnp.sqrt(total / (ROWS * WIDTH * count) + 1e-06)
-        factor = (1.0 / 64.0) / (scale[:PAIRS] * scale[PAIRS:])
-        factor = jnp.broadcast_to(jnp.concatenate([factor, factor], axis=0), (ROWS, ROWS))
-        factor = jnp.transpose(factor)[:1]
+        factor = (1.0 / 64.0) / (scale * pltpu.roll(scale, PAIRS, 1))
         factor_in[...] = factor
         for i in range(near):
             for j in range(count // nz):
@@ -522,10 +514,11 @@
         for i in range(near, nz):
             down_copy(hand - (near - 1) + i).start()
 
-    factor = jnp.transpose(jnp.broadcast_to(factor_in[0:1, :PAIRS], (ROWS, PAIRS)))
-    factors = [jnp.sum(own[g] * factor, axis=0, keepdims=True) for g in range(3)]
+    factors = dot(jnp.concatenate(split3(factor_in[...]), axis=0), own[...])
+    factors = jnp.sum(factors, axis=0, keepdims=True)
+    for g in range(3):
+        scaling[g : g + 1, :] = factors[:, 128 * g : 128 * (g + 1)]
     out_copy(1, GROUP - 1).wait_recv()
-    scaling[...] = jnp.concatenate(factors + [jnp.zeros((5, 128), F32)], axis=0)
     first_copy(1, GROUP - 1).wait_send()
     second_copy(1, GROUP - 1).wait_send()
     out_copy(1, GROUP - 1).wait_send()
@@ -594,10 +587,10 @@
                 pltpu.VMEM((2, PAIRS), jnp.int32),
                 pltpu.VMEM((1, PAIRS), jnp.int32),
                 pltpu.VMEM((128, 3 * PAIRS), BF16),
-                pltpu.VMEM((3, PAIRS, 128), F32),
+                pltpu.VMEM((128, 3 * 128), BF16),
                 pltpu.VMEM((3 * ROWS, 128), BF16),
-                pltpu.VMEM((2 * PAIRS, 3 * GROUP), BF16),
-                pltpu.VMEM((2 * PAIRS, ROWS), F32),
+                pltpu.VMEM((3 * ROWS, 2 * PAIRS), BF16),
+                pltpu.VMEM((GROUP, 2 * PAIRS), F32),
                 pltpu.VMEM((2 * ROWS, 2 * ROWS), BF16),
                 pltpu.VMEM((GROUP, EACH * 2 * PIECES[0], ROWS), BF16),
                 pltpu.VMEM((GROUP, EACH * 2 * PIECES[1], ROWS), BF16),

time: 27.3 us -> 27.2 us (level)
  no operation moved by 1% of the time
where the time goes in v10:
time: 27.2 us; the launch traced here: 26.8 us
  Pallas kernels  25.5 us (94%)
  local copies, waits for them, and re-layouts  0.67 us (2%)
  between operations  0.65 us (2%)
    pallas_call x1, Pallas kernels, local(): pl.pallas_call(lambda *refs: kernel(nz, columns, *refs), out_shape=(jax.S...  24.7 us
    pallas_call x1, Pallas kernels, local(): pl.pallas_call(place_kernel, out_shape=(jax.ShapeDtypeStruct((2, CAP, 16,...  0.81 us
    unnamed x4, local copies, waits for them, and re-layouts  0.67 us

profile of v10, /device:TPU:1, one launch (start us, length us, event | category | flops | bytes accessed | tf_op | source)
XLA Modules:
  0.0 26.8 jit_solution(2994999478387880216)
XLA Ops:
  0.6 0.0 copy-start
  0.6 0.0 copy-start.1
  0.6 0.7 %copy-done = s32[64,2]{0,1:T(2,128)S(1)} copy-done((s32[64,2]{0,1:T(2,128)S(1)}, s32[64,2]{0,1:T(2,128)}, u32[]{:S(2)}) %copy-start) | copy-done | bytes 536
  1.3 0.0 copy-done.1
  1.3 24.7 %shard_map.50 = (f32[8,24,128]{2,1,0:T(8,128)S(1)}, f32[8,128]{1,0:T(8,128)S(1)}) custom-call(bf16[2,4,128,256]{3,2,1,0:T(8,128)(2,1)} %refs_0_.1, s32[2,64]{1,0:T(2,128)S(1)} %bitcast.6, s32[1,64]{1,0:T(1,128)S(1)} %bitcast.7), custom_call_target="tpu_custom_call" | custom-call | tf_op jit(solution)/shard_map/pallas_call | solution.py:579
  26.0 0.8 %shard_map.51 = (f32[2,12,16,32]{3,2,1,0:T(8,128)}, f32[12,16,32]{2,1,0:T(8,128)}) custom-call(f32[192,128]{1,0:T(8,128)S(1)} %bitcast.5, f32[8,128]{1,0:T(8,128)S(1)} %get-tuple-element.7.scaling), custom_call_target="tpu_custom_call" | custom-call | tf_op jit(solution)/shard_map/pallas_call | solution.py:623
Async XLA Ops:
  0.6 0.7 %copy-start = (s32[64,2]{0,1:T(2,128)S(1)}, s32[64,2]{0,1:T(2,128)}, u32[]{:S(2)}) copy-start(s32[64,2]{0,1:T(2,128)} %param.4) | copy-start | bytes 1540
  0.6 0.7 %copy-start.1 = (s32[64]{0:T(128)S(1)}, s32[64]{0:T(128)}, u32[]{:S(2)}) copy-start(s32[64]{0:T(128)} %param.5) | copy-start | bytes 772

commit v11 on v10

--- a/solution.py
+++ b/solution.py
@@ -31,7 +31,7 @@
 HALF = PART // 2
 WINDOW = HALF + 8
 EDGE = EACH * 2 * 8
-CHUNK = 16
+CHUNK = 32
 
 
 def split(x):
@@ -85,7 +85,7 @@
     nz, count, slc_hbm, pairs_hbm, owner_hbm, landed, scaling,
     slc, pairs_s, pairs_v, owner_v, select, own, look, hot, source_of, smoother, sent_0, sent_1, got_0, got_1,
     edge_out, edge_left, edge_right, images, roots, fields, lhs, sums, looked,
-    power_row, power_in, totals, factor_in, results,
+    power_row, power_in, totals, results,
     main_send_0, main_recv_0, main_send_1, main_recv_1, edge_send, edge_recv, ready,
     here, up_send, up_recv, down_send, down_recv, d_send, d_recv, out_send, out_recv, in_sem, table_sem,
 ):
@@ -201,7 +201,7 @@
         )
 
     def down_copy(i):
-        return stage(factor_in, factor_in, down_send.at[0], down_recv.at[0], {"dates": d, "cols": i})
+        return stage(scaling, scaling, down_send.at[0], down_recv.at[0], {"dates": d, "cols": i})
 
     first = (d == 0).astype(jnp.int32)
     last = (d == GROUP - 1).astype(jnp.int32)
@@ -497,7 +497,8 @@
         total = jnp.sum(dot(parts, hot[...]) * source_of[...], axis=0, keepdims=True)
         scale = jnp.sqrt(total / (ROWS * WIDTH * count) + 1e-06)
         factor = (1.0 / 64.0) / (scale * pltpu.roll(scale, PAIRS, 1))
-        factor_in[...] = factor
+        rows = dot(jnp.concatenate(split3(factor), axis=0), own[...])
+        scaling[...] = jnp.sum(rows, axis=0, keepdims=True)
         for i in range(near):
             for j in range(count // nz):
                 if i + j > 0:
@@ -514,10 +515,6 @@
         for i in range(near, nz):
             down_copy(hand - (near - 1) + i).start()
 
-    factors = dot(jnp.concatenate(split3(factor_in[...]), axis=0), own[...])
-    factors = jnp.sum(factors, axis=0, keepdims=True)
-    for g in range(3):
-        scaling[g : g + 1, :] = factors[:, 128 * g : 128 * (g + 1)]
     out_copy(1, GROUP - 1).wait_recv()
     first_copy(1, GROUP - 1).wait_send()
     second_copy(1, GROUP - 1).wait_send()
@@ -533,7 +530,7 @@
 
     def sent_down(number):
         stage(
-            power_in.at[pl.ds(0, number)], power_in.at[pl.ds(0, number)], down_send.at[0],
+            power_in.at[pl.ds(0, 3 * number)], power_in.at[pl.ds(0, 3 * number)], down_send.at[0],
             down_recv.at[0], {"dates": d, "cols": c},
         ).wait_send()
 
@@ -558,7 +555,7 @@
         for g in range(3):
             block = landed[pl.ds(f * 4 + g, 16, stride=12), :]
             if f < 2:
-                block = block * scaling[g : g + 1, :]
+                block = block * scaling[:, 128 * g : 128 * (g + 1)]
             for j in range(4):
                 piece = block[:, 32 * j : 32 * j + 32]
                 if f < 2:
@@ -578,7 +575,7 @@
         owner = owner.reshape(1, PAIRS)
         landed, scaling = pl.pallas_call(
             lambda *refs: kernel(nz, columns, *refs),
-            out_shape=(jax.ShapeDtypeStruct((GROUP, 24, 128), F32), jax.ShapeDtypeStruct((8, 128), F32)),
+            out_shape=(jax.ShapeDtypeStruct((GROUP, 24, 128), F32), jax.ShapeDtypeStruct((1, 384), F32)),
             in_specs=[pl.BlockSpec(memory_space=pl.ANY)] * 3,
             out_specs=(vmem, vmem),
             scratch_shapes=[
@@ -606,9 +603,8 @@
                 pltpu.VMEM((6 * PAIRS * 8, ROWS), F32),
                 pltpu.VMEM((2, 3 * PAIRS, ROWS), F32),
                 pltpu.VMEM((1, ROWS), F32),
-                pltpu.VMEM((columns, ROWS), F32),
+                pltpu.VMEM((2 * columns, ROWS), F32),
                 pltpu.VMEM((GROUP, ROWS), F32),
-                pltpu.VMEM((1, ROWS), F32),
                 pltpu.VMEM((GROUP, 24, 128), F32),
                 sem((1,)), sem((4,)), sem((1,)), sem((1,)),
                 sem((2,)), sem((1,)), pltpu.SemaphoreType.REGULAR((2,)), pltpu.SemaphoreType.REGULAR,

time: 27.2 us -> 27.3 us (level)
  Pallas kernels: 25.5 us -> 25.8 us
    pallas_call x1, Pallas kernels: 24.7 us -> 25 us  [local(): pl.pallas_call(lambda *refs: kernel(nz, columns, *refs), out_shape=(jax.S...]
where the time goes in v11:
time: 27.3 us; the launch traced here: 27.1 us
  Pallas kernels  25.8 us (95%)
  local copies, waits for them, and re-layouts  0.67 us (2%)
  between operations  0.65 us (2%)
    pallas_call x1, Pallas kernels, local(): pl.pallas_call(lambda *refs: kernel(nz, columns, *refs), out_shape=(jax.S...  25 us
    pallas_call x1, Pallas kernels, local(): pl.pallas_call(place_kernel, out_shape=(jax.ShapeDtypeStruct((2, CAP, 16,...  0.81 us
    unnamed x4, local copies, waits for them, and re-layouts  0.67 us

profile of v11, /device:TPU:1, one launch (start us, length us, event | category | flops | bytes accessed | tf_op | source)
XLA Modules:
  0.0 27.1 jit_solution(100268353936274912)
XLA Ops:
  0.6 0.0 copy-start
  0.6 0.0 copy-start.1
  0.6 0.7 %copy-done = s32[64,2]{0,1:T(2,128)S(1)} copy-done((s32[64,2]{0,1:T(2,128)S(1)}, s32[64,2]{0,1:T(2,128)}, u32[]{:S(2)}) %copy-start) | copy-done | bytes 536
  1.3 0.0 copy-done.1
  1.3 25.0 %shard_map.50 = (f32[8,24,128]{2,1,0:T(8,128)S(1)}, f32[1,384]{1,0:T(1,128)S(1)}) custom-call(bf16[2,4,128,256]{3,2,1,0:T(8,128)(2,1)} %refs_0_.1, s32[2,64]{1,0:T(2,128)S(1)} %bitcast.6, s32[1,64]{1,0:T(1,128)S(1)} %bitcast.7), custom_call_target="tpu_custom_call" | custom-call | tf_op jit(solution)/shard_map/pallas_call | solution.py:576
  26.3 0.8 %shard_map.51 = (f32[2,12,16,32]{3,2,1,0:T(8,128)}, f32[12,16,32]{2,1,0:T(8,128)}) custom-call(f32[192,128]{1,0:T(8,128)S(1)} %bitcast.5, f32[1,384]{1,0:T(1,128)S(1)} %get-tuple-element.7.scaling), custom_call_target="tpu_custom_call" | custom-call | tf_op jit(solution)/shard_map/pallas_call | solution.py:619
Async XLA Ops:
  0.6 0.7 %copy-start = (s32[64,2]{0,1:T(2,128)S(1)}, s32[64,2]{0,1:T(2,128)}, u32[]{:S(2)}) copy-start(s32[64,2]{0,1:T(2,128)} %param.4) | copy-start | bytes 1540
  0.6 0.7 %copy-start.1 = (s32[64]{0:T(128)S(1)}, s32[64]{0:T(128)}, u32[]{:S(2)}) copy-start(s32[64]{0:T(128)} %param.5) | copy-start | bytes 772

commit v12 on v11

--- a/solution.py
+++ b/solution.py
@@ -115,18 +115,19 @@
     for k in range(1, GROUP):
         greet(date_peer(k))
 
-    def greet_neighbour(later, receiver, other):
-        @pl.when(later)
-        def _():
-            greet({"dates": receiver, "cols": other})
-
-        @pl.when(later & (d == GROUP - 1 - receiver))
-        def _():
-            for e in range(GROUP):
-                greet({"dates": e, "cols": other})
-
-    greet_neighbour(right_later, 0, right)
-    greet_neighbour(left_later, GROUP - 1, left)
+    @pl.when(right_later & (d == GROUP - 1))
+    def _():
+        for e in range(GROUP):
+            greet({"dates": e, "cols": right})
+
+    @pl.when(left_later)
+    def _():
+        greet({"dates": GROUP - 1, "cols": left})
+
+    @pl.when(left_later & (d == 0))
+    def _():
+        for e in range(GROUP):
+            greet({"dates": e, "cols": left})
 
     @pl.when(c == 0)
     def _():
@@ -203,8 +204,12 @@
     def down_copy(i):
         return stage(scaling, scaling, down_send.at[0], down_recv.at[0], {"dates": d, "cols": i})
 
-    first = (d == 0).astype(jnp.int32)
     last = (d == GROUP - 1).astype(jnp.int32)
+
+    def tell_ready(side, e, other):
+        pl.semaphore_signal(
+            ready.at[side], inc=1, device_id={"dates": e, "cols": other}, device_id_type=MESH
+        )
 
     def enter():
         pl.semaphore_wait(
@@ -213,16 +218,8 @@
             + (c > 0).astype(jnp.int32)
             + handed.astype(jnp.int32)
             + right_earlier.astype(jnp.int32) * (1 + GROUP * last)
-            + left_earlier.astype(jnp.int32) * (1 + GROUP * first),
-        )
-
-        def tell_ready(side, condition, other):
-            @pl.when(condition)
-            def _():
-                for e in range(GROUP):
-                    pl.semaphore_signal(
-                        ready.at[side], inc=1, device_id={"dates": e, "cols": other}, device_id_type=MESH
-                    )
+            + left_earlier.astype(jnp.int32),
+        )
 
         @pl.when(handed)
         def _():
@@ -230,12 +227,18 @@
                 here, inc=1, device_id={"dates": d, "cols": hand}, device_id_type=MESH
             )
 
-        tell_ready(0, left_earlier & (d == 0), left)
-        tell_ready(1, right_earlier & (d == GROUP - 1), right)
-
         @pl.when(c > 0)
         def _():
             up_copy(c).start()
+
+        @pl.when(left_earlier & (d == 0))
+        def _():
+            tell_ready(0, GROUP - 1, left)
+
+        @pl.when(right_earlier & (d == GROUP - 1))
+        def _():
+            for e in range(GROUP):
+                tell_ready(1, e, right)
 
     pl.when(z >= nz // 2)(enter)
     cut(0, matrix)
@@ -368,7 +371,7 @@
         for date in range(DATES):
             roots[date, HALF:] = smooth[HALF * date : HALF * (date + 1)]
 
-    def pairs_of(half, then=None):
+    def pairs_of(half, between=None):
         window = slice(HALF * half, HALF * half + WINDOW)
 
         def place(field, p):
@@ -410,9 +413,12 @@
                 sums[place(2, p), :] = value[0:8] + value[8:16]
             return carry
 
-        lax.fori_loop(0, PAIRS // CHUNK, chunk, 0)
-        if then is not None:
-            then()
+        if between is None:
+            lax.fori_loop(0, PAIRS // CHUNK, chunk, 0)
+        else:
+            lax.fori_loop(0, PAIRS // CHUNK // 2, chunk, 0)
+            between()
+            lax.fori_loop(PAIRS // CHUNK // 2, PAIRS // CHUNK, chunk, 0)
         rows = sums[pl.ds(3 * half * PAIRS * 8, 3 * PAIRS, stride=8), :]
         for i in range(1, 8):
             rows = rows + sums[pl.ds(3 * half * PAIRS * 8 + i, 3 * PAIRS, stride=8), :]
@@ -421,6 +427,12 @@
     @pl.when(right_later)
     def _():
         pl.semaphore_wait(ready.at[0], 1)
+
+        @pl.when(d == GROUP - 1)
+        def _():
+            for e in range(GROUP - 1):
+                tell_ready(0, e, c)
+
         edge_copy(0).start()
 
     @pl.when(left_later)

time: 27.3 us -> 27.5 us (level)
  no operation moved by 1% of the time
where the time goes in v12:
time: 27.5 us; the launch traced here: 27.2 us
  Pallas kernels  25.9 us (94%)
  local copies, waits for them, and re-layouts  0.67 us (2%)
  between operations  0.65 us (2%)
    pallas_call x1, Pallas kernels, local(): pl.pallas_call(lambda *refs: kernel(nz, columns, *refs), out_shape=(jax.S...  25 us
    pallas_call x1, Pallas kernels, local(): pl.pallas_call(place_kernel, out_shape=(jax.ShapeDtypeStruct((2, CAP, 16,...  0.81 us
    unnamed x4, local copies, waits for them, and re-layouts  0.67 us

profile of v12, /device:TPU:1, one launch (start us, length us, event | category | flops | bytes accessed | tf_op | source)
XLA Modules:
  0.0 27.2 jit_solution(18062180473600067791)
XLA Ops:
  0.6 0.0 copy-start
  0.6 0.0 copy-start.1
  0.6 0.7 %copy-done = s32[64,2]{0,1:T(2,128)S(1)} copy-done((s32[64,2]{0,1:T(2,128)S(1)}, s32[64,2]{0,1:T(2,128)}, u32[]{:S(2)}) %copy-start) | copy-done | bytes 536
  1.3 0.0 copy-done.1
  1.3 25.0 %shard_map.50 = (f32[8,24,128]{2,1,0:T(8,128)S(1)}, f32[1,384]{1,0:T(1,128)S(1)}) custom-call(bf16[2,4,128,256]{3,2,1,0:T(8,128)(2,1)} %refs_0_.1, s32[2,64]{1,0:T(2,128)S(1)} %bitcast.6, s32[1,64]{1,0:T(1,128)S(1)} %bitcast.7), custom_call_target="tpu_custom_call" | custom-call | tf_op jit(solution)/shard_map/pallas_call | solution.py:588
  26.4 0.8 %shard_map.51 = (f32[2,12,16,32]{3,2,1,0:T(8,128)}, f32[12,16,32]{2,1,0:T(8,128)}) custom-call(f32[192,128]{1,0:T(8,128)S(1)} %bitcast.5, f32[1,384]{1,0:T(1,128)S(1)} %get-tuple-element.7.scaling), custom_call_target="tpu_custom_call" | custom-call | tf_op jit(solution)/shard_map/pallas_call | solution.py:631
Async XLA Ops:
  0.6 0.7 %copy-start = (s32[64,2]{0,1:T(2,128)S(1)}, s32[64,2]{0,1:T(2,128)}, u32[]{:S(2)}) copy-start(s32[64,2]{0,1:T(2,128)} %param.4) | copy-start | bytes 1540
  0.6 0.7 %copy-start.1 = (s32[64]{0:T(128)S(1)}, s32[64]{0:T(128)}, u32[]{:S(2)}) copy-start(s32[64]{0:T(128)} %param.5) | copy-start | bytes 772

commit v13 on v12

--- a/solution.py
+++ b/solution.py
@@ -85,7 +85,7 @@
     nz, count, slc_hbm, pairs_hbm, owner_hbm, landed, scaling,
     slc, pairs_s, pairs_v, owner_v, select, own, look, hot, source_of, smoother, sent_0, sent_1, got_0, got_1,
     edge_out, edge_left, edge_right, images, roots, fields, lhs, sums, looked,
-    power_row, power_in, totals, results,
+    power_row, power_in, totals, factor_in, results,
     main_send_0, main_recv_0, main_send_1, main_recv_1, edge_send, edge_recv, ready,
     here, up_send, up_recv, down_send, down_recv, d_send, d_recv, out_send, out_recv, in_sem, table_sem,
 ):
@@ -179,16 +179,18 @@
     smoother[:, :ROWS] = jnp.concatenate([high, high], axis=0)
     smoother[:, ROWS:] = jnp.concatenate([low, low], axis=0)
     load.wait()
-    power_rows = []
-    for t in range(EACH):
-        wide = jnp.concatenate([slc[0, t], slc[1, t]], axis=0).astype(F32)
-        square = jnp.sum(wide * wide, axis=0, keepdims=True)
-        power_rows.append(square[:, :ROWS] + square[:, ROWS:])
-    folded = jnp.concatenate(power_rows + [jnp.zeros((8 - EACH, ROWS), F32)], axis=0)
-    folded = folded + pltpu.roll(folded, 64, 1)
-    folded = folded + pltpu.roll(folded, 32, 1)
-    own_lane = (iota((8, ROWS), 1) >> 5) == iota((8, ROWS), 0)
-    power_row[...] = jnp.sum(jnp.where(own_lane, folded, 0.0), axis=0, keepdims=True)
+
+    def powers():
+        power_rows = []
+        for t in range(EACH):
+            wide = jnp.concatenate([slc[0, t], slc[1, t]], axis=0).astype(F32)
+            square = jnp.sum(wide * wide, axis=0, keepdims=True)
+            power_rows.append(square[:, :ROWS] + square[:, ROWS:])
+        folded = jnp.concatenate(power_rows + [jnp.zeros((8 - EACH, ROWS), F32)], axis=0)
+        folded = folded + pltpu.roll(folded, 64, 1)
+        folded = folded + pltpu.roll(folded, 32, 1)
+        own_lane = (iota((8, ROWS), 1) >> 5) == iota((8, ROWS), 0)
+        power_row[...] = jnp.sum(jnp.where(own_lane, folded, 0.0), axis=0, keepdims=True)
 
     def stage(src, dst, send, recv, peer):
         return pltpu.make_async_remote_copy(
@@ -202,7 +204,7 @@
         )
 
     def down_copy(i):
-        return stage(scaling, scaling, down_send.at[0], down_recv.at[0], {"dates": d, "cols": i})
+        return stage(factor_in, factor_in, down_send.at[0], down_recv.at[0], {"dates": d, "cols": i})
 
     last = (d == GROUP - 1).astype(jnp.int32)
 
@@ -227,10 +229,6 @@
                 here, inc=1, device_id={"dates": d, "cols": hand}, device_id_type=MESH
             )
 
-        @pl.when(c > 0)
-        def _():
-            up_copy(c).start()
-
         @pl.when(left_earlier & (d == 0))
         def _():
             tell_ready(0, GROUP - 1, left)
@@ -240,7 +238,19 @@
             for e in range(GROUP):
                 tell_ready(1, e, right)
 
-    pl.when(z >= nz // 2)(enter)
+    def send_up():
+        @pl.when(c > 0)
+        def _():
+            up_copy(c).start()
+
+    late = z >= nz // 2
+
+    @pl.when(late)
+    def _():
+        powers()
+        enter()
+        send_up()
+
     cut(0, matrix)
     pl.when(z < nz // 2)(enter)
 
@@ -271,6 +281,11 @@
 
     for k in order:
         first_copy(k).start()
+
+    @pl.when(z < nz // 2)
+    def _():
+        powers()
+        send_up()
 
     @pl.when(right_earlier)
     def _():
@@ -371,7 +386,7 @@
         for date in range(DATES):
             roots[date, HALF:] = smooth[HALF * date : HALF * (date + 1)]
 
-    def pairs_of(half, between=None):
+    def pairs_of(half, then=None):
         window = slice(HALF * half, HALF * half + WINDOW)
 
         def place(field, p):
@@ -413,12 +428,9 @@
                 sums[place(2, p), :] = value[0:8] + value[8:16]
             return carry
 
-        if between is None:
-            lax.fori_loop(0, PAIRS // CHUNK, chunk, 0)
-        else:
-            lax.fori_loop(0, PAIRS // CHUNK // 2, chunk, 0)
-            between()
-            lax.fori_loop(PAIRS // CHUNK // 2, PAIRS // CHUNK, chunk, 0)
+        lax.fori_loop(0, PAIRS // CHUNK, chunk, 0)
+        if then is not None:
+            then()
         rows = sums[pl.ds(3 * half * PAIRS * 8, 3 * PAIRS, stride=8), :]
         for i in range(1, 8):
             rows = rows + sums[pl.ds(3 * half * PAIRS * 8 + i, 3 * PAIRS, stride=8), :]
@@ -509,8 +521,7 @@
         total = jnp.sum(dot(parts, hot[...]) * source_of[...], axis=0, keepdims=True)
         scale = jnp.sqrt(total / (ROWS * WIDTH * count) + 1e-06)
         factor = (1.0 / 64.0) / (scale * pltpu.roll(scale, PAIRS, 1))
-        rows = dot(jnp.concatenate(split3(factor), axis=0), own[...])
-        scaling[...] = jnp.sum(rows, axis=0, keepdims=True)
+        factor_in[...] = factor
         for i in range(near):
             for j in range(count // nz):
                 if i + j > 0:
@@ -527,6 +538,10 @@
         for i in range(near, nz):
             down_copy(hand - (near - 1) + i).start()
 
+    factors = dot(jnp.concatenate(split3(factor_in[...]), axis=0), own[...])
+    factors = jnp.sum(factors, axis=0, keepdims=True)
+    for g in range(3):
+        scaling[g : g + 1, :] = factors[:, 128 * g : 128 * (g + 1)]
     out_copy(1, GROUP - 1).wait_recv()
     first_copy(1, GROUP - 1).wait_send()
     second_copy(1, GROUP - 1).wait_send()
@@ -542,7 +557,7 @@
 
     def sent_down(number):
         stage(
-            power_in.at[pl.ds(0, 3 * number)], power_in.at[pl.ds(0, 3 * number)], down_send.at[0],
+            power_in.at[pl.ds(0, number)], power_in.at[pl.ds(0, number)], down_send.at[0],
             down_recv.at[0], {"dates": d, "cols": c},
         ).wait_send()
 
@@ -567,7 +582,7 @@
         for g in range(3):
             block = landed[pl.ds(f * 4 + g, 16, stride=12), :]
             if f < 2:
-                block = block * scaling[:, 128 * g : 128 * (g + 1)]
+                block = block * scaling[g : g + 1, :]
             for j in range(4):
                 piece = block[:, 32 * j : 32 * j + 32]
                 if f < 2:
@@ -587,7 +602,7 @@
         owner = owner.reshape(1, PAIRS)
         landed, scaling = pl.pallas_call(
             lambda *refs: kernel(nz, columns, *refs),
-            out_shape=(jax.ShapeDtypeStruct((GROUP, 24, 128), F32), jax.ShapeDtypeStruct((1, 384), F32)),
+            out_shape=(jax.ShapeDtypeStruct((GROUP, 24, 128), F32), jax.ShapeDtypeStruct((8, 128), F32)),
             in_specs=[pl.BlockSpec(memory_space=pl.ANY)] * 3,
             out_specs=(vmem, vmem),
             scratch_shapes=[
@@ -615,8 +630,9 @@
                 pltpu.VMEM((6 * PAIRS * 8, ROWS), F32),
                 pltpu.VMEM((2, 3 * PAIRS, ROWS), F32),
                 pltpu.VMEM((1, ROWS), F32),
-                pltpu.VMEM((2 * columns, ROWS), F32),
+                pltpu.VMEM((columns, ROWS), F32),
                 pltpu.VMEM((GROUP, ROWS), F32),
+                pltpu.VMEM((1, ROWS), F32),
                 pltpu.VMEM((GROUP, 24, 128), F32),
                 sem((1,)), sem((4,)), sem((1,)), sem((1,)),
                 sem((2,)), sem((1,)), pltpu.SemaphoreType.REGULAR((2,)), pltpu.SemaphoreType.REGULAR,

time: 27.5 us -> 27.2 us (0.989)
  Pallas kernels: 25.9 us -> 25.6 us
    pallas_call x1, Pallas kernels: 25 us -> 24.8 us  [local(): pl.pallas_call(lambda *refs: kernel(nz, columns, *refs), out_shape=(jax.S...]
where the time goes in v13:
time: 27.2 us; the launch traced here: 26.9 us
  Pallas kernels  25.6 us (94%)
  local copies, waits for them, and re-layouts  0.67 us (2%)
  between operations  0.65 us (2%)
    pallas_call x1, Pallas kernels, local(): pl.pallas_call(lambda *refs: kernel(nz, columns, *refs), out_shape=(jax.S...  24.8 us
    pallas_call x1, Pallas kernels, local(): pl.pallas_call(place_kernel, out_shape=(jax.ShapeDtypeStruct((2, CAP, 16,...  0.81 us
    unnamed x4, local copies, waits for them, and re-layouts  0.67 us

profile of v13, /device:TPU:1, one launch (start us, length us, event | category | flops | bytes accessed | tf_op | source)
XLA Modules:
  0.0 26.9 jit_solution(4847280545412034764)
XLA Ops:
  0.6 0.0 copy-start
  0.6 0.0 copy-start.1
  0.6 0.7 %copy-done = s32[64,2]{0,1:T(2,128)S(1)} copy-done((s32[64,2]{0,1:T(2,128)S(1)}, s32[64,2]{0,1:T(2,128)}, u32[]{:S(2)}) %copy-start) | copy-done | bytes 536
  1.3 0.0 copy-done.1
  1.3 24.8 %shard_map.50 = (f32[8,24,128]{2,1,0:T(8,128)S(1)}, f32[8,128]{1,0:T(8,128)S(1)}) custom-call(bf16[2,4,128,256]{3,2,1,0:T(8,128)(2,1)} %refs_0_.1, s32[2,64]{1,0:T(2,128)S(1)} %bitcast.6, s32[1,64]{1,0:T(1,128)S(1)} %bitcast.7), custom_call_target="tpu_custom_call" | custom-call | tf_op jit(solution)/shard_map/pallas_call | solution.py:603
  26.1 0.8 %shard_map.51 = (f32[2,12,16,32]{3,2,1,0:T(8,128)}, f32[12,16,32]{2,1,0:T(8,128)}) custom-call(f32[192,128]{1,0:T(8,128)S(1)} %bitcast.5, f32[8,128]{1,0:T(8,128)S(1)} %get-tuple-element.7.scaling), custom_call_target="tpu_custom_call" | custom-call | tf_op jit(solution)/shard_map/pallas_call | solution.py:647
Async XLA Ops:
  0.6 0.7 %copy-start = (s32[64,2]{0,1:T(2,128)S(1)}, s32[64,2]{0,1:T(2,128)}, u32[]{:S(2)}) copy-start(s32[64,2]{0,1:T(2,128)} %param.4) | copy-start | bytes 1540
  0.6 0.7 %copy-start.1 = (s32[64]{0:T(128)S(1)}, s32[64]{0:T(128)}, u32[]{:S(2)}) copy-start(s32[64]{0:T(128)} %param.5) | copy-start | bytes 772

commit v14 on v13

--- a/solution.py
+++ b/solution.py
@@ -86,7 +86,7 @@
     slc, pairs_s, pairs_v, owner_v, select, own, look, hot, source_of, smoother, sent_0, sent_1, got_0, got_1,
     edge_out, edge_left, edge_right, images, roots, fields, lhs, sums, looked,
     power_row, power_in, totals, factor_in, results,
-    main_send_0, main_recv_0, main_send_1, main_recv_1, edge_send, edge_recv, ready,
+    main_send_0, main_recv_0, main_send_1, main_recv_1, edge_send, edge_recv, ready, joined,
     here, up_send, up_recv, down_send, down_recv, d_send, d_recv, out_send, out_recv, in_sem, table_sem,
 ):
     load = pltpu.make_async_copy(slc_hbm, slc, in_sem.at[0])
@@ -112,8 +112,15 @@
     def greet(device):
         pl.semaphore_signal(barrier, inc=1, device_id=device, device_id_type=MESH)
 
+    def turn(e):
+        return jnp.where(c == 0, (e + GROUP - 1) % GROUP, e)
+
+    mine_turn = turn(d)
     for k in range(1, GROUP):
-        greet(date_peer(k))
+
+        @pl.when(turn((d + k) % GROUP) > mine_turn)
+        def _():
+            greet(date_peer(k))
 
     @pl.when(right_later & (d == GROUP - 1))
     def _():
@@ -178,7 +185,6 @@
     low = band(LOW)
     smoother[:, :ROWS] = jnp.concatenate([high, high], axis=0)
     smoother[:, ROWS:] = jnp.concatenate([low, low], axis=0)
-    load.wait()
 
     def powers():
         power_rows = []
@@ -214,14 +220,23 @@
         )
 
     def enter():
-        pl.semaphore_wait(
-            barrier,
-            (GROUP - 1)
+        awaited = (
+            mine_turn
             + (c > 0).astype(jnp.int32)
             + handed.astype(jnp.int32)
             + right_earlier.astype(jnp.int32) * (1 + GROUP * last)
-            + left_earlier.astype(jnp.int32),
-        )
+            + left_earlier.astype(jnp.int32)
+        )
+
+        @pl.when(awaited > 0)
+        def _():
+            pl.semaphore_wait(barrier, awaited)
+
+        for k in range(1, GROUP):
+
+            @pl.when(turn((d + k) % GROUP) < mine_turn)
+            def _():
+                pl.semaphore_signal(joined, inc=1, device_id=date_peer(k), device_id_type=MESH)
 
         @pl.when(handed)
         def _():
@@ -245,14 +260,19 @@
 
     late = z >= nz // 2
 
+    enter()
+    load.wait()
+
     @pl.when(late)
     def _():
         powers()
-        enter()
         send_up()
 
     cut(0, matrix)
-    pl.when(z < nz // 2)(enter)
+
+    @pl.when(mine_turn < GROUP - 1)
+    def _():
+        pl.semaphore_wait(joined, GROUP - 1 - mine_turn)
 
     targets = ({"dates": 0, "cols": right}, {"dates": GROUP - 1, "cols": left})
 
@@ -635,7 +655,7 @@
                 pltpu.VMEM((1, ROWS), F32),
                 pltpu.VMEM((GROUP, 24, 128), F32),
                 sem((1,)), sem((4,)), sem((1,)), sem((1,)),
-                sem((2,)), sem((1,)), pltpu.SemaphoreType.REGULAR((2,)), pltpu.SemaphoreType.REGULAR,
+                sem((2,)), sem((1,)), pltpu.SemaphoreType.REGULAR((2,)), pltpu.SemaphoreType.REGULAR, pltpu.SemaphoreType.REGULAR,
                 sem((1,)), sem((1,)), sem((1,)), sem((1,)),
                 sem((1,)), sem((1,)), sem((1,)), sem((1,)),
                 sem((1,)), sem((3,)),

time: 27.2 us -> 27.7 us (1.018)
  Pallas kernels: 25.6 us -> 25.9 us
    pallas_call x1, Pallas kernels: 24.8 us -> 25.1 us  [local(): pl.pallas_call(lambda *refs: kernel(nz, columns, *refs), out_shape=(jax.S...]
where the time goes in v14:
time: 27.7 us; the launch traced here: 27.2 us
  Pallas kernels  25.9 us (94%)
  local copies, waits for them, and re-layouts  0.67 us (2%)
  between operations  0.65 us (2%)
    pallas_call x1, Pallas kernels, local(): pl.pallas_call(lambda *refs: kernel(nz, columns, *refs), out_shape=(jax.S...  25.1 us
    pallas_call x1, Pallas kernels, local(): pl.pallas_call(place_kernel, out_shape=(jax.ShapeDtypeStruct((2, CAP, 16,...  0.81 us
    unnamed x4, local copies, waits for them, and re-layouts  0.67 us

profile of v14, /device:TPU:1, one launch (start us, length us, event | category | flops | bytes accessed | tf_op | source)
XLA Modules:
  0.0 27.2 jit_solution(8214996167414428020)
XLA Ops:
  0.6 0.0 copy-start
  0.6 0.0 copy-start.1
  0.6 0.7 %copy-done = s32[64,2]{0,1:T(2,128)S(1)} copy-done((s32[64,2]{0,1:T(2,128)S(1)}, s32[64,2]{0,1:T(2,128)}, u32[]{:S(2)}) %copy-start) | copy-done | bytes 536
  1.3 0.0 copy-done.1
  1.3 25.1 %shard_map.50 = (f32[8,24,128]{2,1,0:T(8,128)S(1)}, f32[8,128]{1,0:T(8,128)S(1)}) custom-call(bf16[2,4,128,256]{3,2,1,0:T(8,128)(2,1)} %refs_0_.1, s32[2,64]{1,0:T(2,128)S(1)} %bitcast.6, s32[1,64]{1,0:T(1,128)S(1)} %bitcast.7), custom_call_target="tpu_custom_call" | custom-call | tf_op jit(solution)/shard_map/pallas_call | solution.py:623
  26.4 0.8 %shard_map.51 = (f32[2,12,16,32]{3,2,1,0:T(8,128)}, f32[12,16,32]{2,1,0:T(8,128)}) custom-call(f32[192,128]{1,0:T(8,128)S(1)} %bitcast.5, f32[8,128]{1,0:T(8,128)S(1)} %get-tuple-element.7.scaling), custom_call_target="tpu_custom_call" | custom-call | tf_op jit(solution)/shard_map/pallas_call | solution.py:667
Async XLA Ops:
  0.6 0.7 %copy-start = (s32[64,2]{0,1:T(2,128)S(1)}, s32[64,2]{0,1:T(2,128)}, u32[]{:S(2)}) copy-start(s32[64,2]{0,1:T(2,128)} %param.4) | copy-start | bytes 1540
  0.6 0.7 %copy-start.1 = (s32[64]{0:T(128)S(1)}, s32[64]{0:T(128)}, u32[]{:S(2)}) copy-start(s32[64]{0:T(128)} %param.5) | copy-start | bytes 772

commit v15 on v14

--- a/solution.py
+++ b/solution.py
@@ -136,6 +136,58 @@
         for e in range(GROUP):
             greet({"dates": e, "cols": left})
 
+    hands_on = z == near - 1
+    handed = z >= near
+    hand = c - z + near - 1
+
+    @pl.when(hands_on)
+    def _():
+        for i in range(near, nz):
+            greet({"dates": d, "cols": hand - (near - 1) + i})
+
+    last = (d == GROUP - 1).astype(jnp.int32)
+
+    def tell_ready(side, e, other):
+        pl.semaphore_signal(
+            ready.at[side], inc=1, device_id={"dates": e, "cols": other}, device_id_type=MESH
+        )
+
+    def enter():
+        awaited = (
+            mine_turn
+            + (c > 0).astype(jnp.int32)
+            + handed.astype(jnp.int32)
+            + right_earlier.astype(jnp.int32) * (1 + GROUP * last)
+            + left_earlier.astype(jnp.int32)
+        )
+
+        @pl.when(awaited > 0)
+        def _():
+            pl.semaphore_wait(barrier, awaited)
+
+        for k in range(1, GROUP):
+
+            @pl.when(turn((d + k) % GROUP) < mine_turn)
+            def _():
+                pl.semaphore_signal(joined, inc=1, device_id=date_peer(k), device_id_type=MESH)
+
+        @pl.when(handed)
+        def _():
+            pl.semaphore_signal(
+                here, inc=1, device_id={"dates": d, "cols": hand}, device_id_type=MESH
+            )
+
+        @pl.when(left_earlier & (d == 0))
+        def _():
+            tell_ready(0, GROUP - 1, left)
+
+        @pl.when(right_earlier & (d == GROUP - 1))
+        def _():
+            for e in range(GROUP):
+                tell_ready(1, e, right)
+
+    enter()
+
     @pl.when(c == 0)
     def _():
         def one(i, carry):
@@ -143,15 +195,6 @@
             return carry
 
         lax.fori_loop(1, count, one, 0)
-
-    hands_on = z == near - 1
-    handed = z >= near
-    hand = c - z + near - 1
-
-    @pl.when(hands_on)
-    def _():
-        for i in range(near, nz):
-            greet({"dates": d, "cols": hand - (near - 1) + i})
 
     tables = [
         pltpu.make_async_copy(pairs_hbm, pairs_s, table_sem.at[0]),
@@ -212,47 +255,6 @@
     def down_copy(i):
         return stage(factor_in, factor_in, down_send.at[0], down_recv.at[0], {"dates": d, "cols": i})
 
-    last = (d == GROUP - 1).astype(jnp.int32)
-
-    def tell_ready(side, e, other):
-        pl.semaphore_signal(
-            ready.at[side], inc=1, device_id={"dates": e, "cols": other}, device_id_type=MESH
-        )
-
-    def enter():
-        awaited = (
-            mine_turn
-            + (c > 0).astype(jnp.int32)
-            + handed.astype(jnp.int32)
-            + right_earlier.astype(jnp.int32) * (1 + GROUP * last)
-            + left_earlier.astype(jnp.int32)
-        )
-
-        @pl.when(awaited > 0)
-        def _():
-            pl.semaphore_wait(barrier, awaited)
-
-        for k in range(1, GROUP):
-
-            @pl.when(turn((d + k) % GROUP) < mine_turn)
-            def _():
-                pl.semaphore_signal(joined, inc=1, device_id=date_peer(k), device_id_type=MESH)
-
-        @pl.when(handed)
-        def _():
-            pl.semaphore_signal(
-                here, inc=1, device_id={"dates": d, "cols": hand}, device_id_type=MESH
-            )
-
-        @pl.when(left_earlier & (d == 0))
-        def _():
-            tell_ready(0, GROUP - 1, left)
-
-        @pl.when(right_earlier & (d == GROUP - 1))
-        def _():
-            for e in range(GROUP):
-                tell_ready(1, e, right)
-
     def send_up():
         @pl.when(c > 0)
         def _():
@@ -260,7 +262,6 @@
 
     late = z >= nz // 2
 
-    enter()
     load.wait()
 
     @pl.when(late)

time: 27.7 us -> 27.5 us (level)
  no operation moved by 1% of the time
where the time goes in v15:
time: 27.5 us; the launch traced here: 27.2 us
  Pallas kernels  25.8 us (94%)
  local copies, waits for them, and re-layouts  0.67 us (2%)
  between operations  0.65 us (2%)
    pallas_call x1, Pallas kernels, local(): pl.pallas_call(lambda *refs: kernel(nz, columns, *refs), out_shape=(jax.S...  25 us
    pallas_call x1, Pallas kernels, local(): pl.pallas_call(place_kernel, out_shape=(jax.ShapeDtypeStruct((2, CAP, 16,...  0.81 us
    unnamed x4, local copies, waits for them, and re-layouts  0.67 us

profile of v15, /device:TPU:1, one launch (start us, length us, event | category | flops | bytes accessed | tf_op | source)
XLA Modules:
  0.0 27.2 jit_solution(1455144900503440526)
XLA Ops:
  0.6 0.0 copy-start
  0.6 0.0 copy-start.1
  0.6 0.7 %copy-done = s32[64,2]{0,1:T(2,128)S(1)} copy-done((s32[64,2]{0,1:T(2,128)S(1)}, s32[64,2]{0,1:T(2,128)}, u32[]{:S(2)}) %copy-start) | copy-done | bytes 536
  1.3 0.0 copy-done.1
  1.3 25.0 %shard_map.50 = (f32[8,24,128]{2,1,0:T(8,128)S(1)}, f32[8,128]{1,0:T(8,128)S(1)}) custom-call(bf16[2,4,128,256]{3,2,1,0:T(8,128)(2,1)} %refs_0_.1, s32[2,64]{1,0:T(2,128)S(1)} %bitcast.6, s32[1,64]{1,0:T(1,128)S(1)} %bitcast.7), custom_call_target="tpu_custom_call" | custom-call | tf_op jit(solution)/shard_map/pallas_call | solution.py:624
  26.3 0.8 %shard_map.51 = (f32[2,12,16,32]{3,2,1,0:T(8,128)}, f32[12,16,32]{2,1,0:T(8,128)}) custom-call(f32[192,128]{1,0:T(8,128)S(1)} %bitcast.5, f32[8,128]{1,0:T(8,128)S(1)} %get-tuple-element.7.scaling), custom_call_target="tpu_custom_call" | custom-call | tf_op jit(solution)/shard_map/pallas_call | solution.py:668
Async XLA Ops:
  0.6 0.7 %copy-start = (s32[64,2]{0,1:T(2,128)S(1)}, s32[64,2]{0,1:T(2,128)}, u32[]{:S(2)}) copy-start(s32[64,2]{0,1:T(2,128)} %param.4) | copy-start | bytes 1540
  0.6 0.7 %copy-start.1 = (s32[64]{0:T(128)S(1)}, s32[64]{0:T(128)}, u32[]{:S(2)}) copy-start(s32[64]{0:T(128)} %param.5) | copy-start | bytes 772

commit v16 on v13

--- a/solution.py
+++ b/solution.py
@@ -522,10 +522,8 @@
         scale = jnp.sqrt(total / (ROWS * WIDTH * count) + 1e-06)
         factor = (1.0 / 64.0) / (scale * pltpu.roll(scale, PAIRS, 1))
         factor_in[...] = factor
-        for i in range(near):
-            for j in range(count // nz):
-                if i + j > 0:
-                    down_copy(j * nz + i).start()
+        for j in range(1, count // nz):
+            down_copy(j * nz).start()
 
     @pl.when(c > 0)
     def _():
@@ -542,6 +540,13 @@
     factors = jnp.sum(factors, axis=0, keepdims=True)
     for g in range(3):
         scaling[g : g + 1, :] = factors[:, 128 * g : 128 * (g + 1)]
+
+    @pl.when(c == 0)
+    def _():
+        for i in range(1, near):
+            for j in range(count // nz):
+                down_copy(j * nz + i).start()
+
     out_copy(1, GROUP - 1).wait_recv()
     first_copy(1, GROUP - 1).wait_send()
     second_copy(1, GROUP - 1).wait_send()

time: 27.2 us -> 27.2 us (level)
  no operation moved by 1% of the time
where the time goes in v16:
time: 27.2 us; the launch traced here: 27.1 us
  Pallas kernels  25.7 us (94%)
  local copies, waits for them, and re-layouts  0.67 us (2%)
  between operations  0.65 us (2%)
    pallas_call x1, Pallas kernels, local(): pl.pallas_call(lambda *refs: kernel(nz, columns, *refs), out_shape=(jax.S...  24.9 us
    pallas_call x1, Pallas kernels, local(): pl.pallas_call(place_kernel, out_shape=(jax.ShapeDtypeStruct((2, CAP, 16,...  0.81 us
    unnamed x4, local copies, waits for them, and re-layouts  0.67 us

profile of v16, /device:TPU:1, one launch (start us, length us, event | category | flops | bytes accessed | tf_op | source)
XLA Modules:
  0.0 27.1 jit_solution(11526723843408056538)
XLA Ops:
  0.6 0.0 copy-start
  0.6 0.0 copy-start.1
  0.6 0.7 %copy-done = s32[64,2]{0,1:T(2,128)S(1)} copy-done((s32[64,2]{0,1:T(2,128)S(1)}, s32[64,2]{0,1:T(2,128)}, u32[]{:S(2)}) %copy-start) | copy-done | bytes 536
  1.3 0.0 copy-done.1
  1.3 24.9 %shard_map.50 = (f32[8,24,128]{2,1,0:T(8,128)S(1)}, f32[8,128]{1,0:T(8,128)S(1)}) custom-call(bf16[2,4,128,256]{3,2,1,0:T(8,128)(2,1)} %refs_0_.1, s32[2,64]{1,0:T(2,128)S(1)} %bitcast.6, s32[1,64]{1,0:T(1,128)S(1)} %bitcast.7), custom_call_target="tpu_custom_call" | custom-call | tf_op jit(solution)/shard_map/pallas_call | solution.py:608
  26.2 0.8 %shard_map.51 = (f32[2,12,16,32]{3,2,1,0:T(8,128)}, f32[12,16,32]{2,1,0:T(8,128)}) custom-call(f32[192,128]{1,0:T(8,128)S(1)} %bitcast.5, f32[8,128]{1,0:T(8,128)S(1)} %get-tuple-element.7.scaling), custom_call_target="tpu_custom_call" | custom-call | tf_op jit(solution)/shard_map/pallas_call | solution.py:652
Async XLA Ops:
  0.6 0.7 %copy-start = (s32[64,2]{0,1:T(2,128)S(1)}, s32[64,2]{0,1:T(2,128)}, u32[]{:S(2)}) copy-start(s32[64,2]{0,1:T(2,128)} %param.4) | copy-start | bytes 1540
  0.6 0.7 %copy-start.1 = (s32[64]{0:T(128)S(1)}, s32[64]{0:T(128)}, u32[]{:S(2)}) copy-start(s32[64]{0:T(128)} %param.5) | copy-start | bytes 772
